TPU v7x, 32 devices: a whole 2x2x4 slice. The times are simulated.
32 devices in a mesh: circ: 16 (over z, y, core), mode: 2 (over x).
Axes of the slice: x: 2, y: 2, z: 4, core: 2. Of those that a mesh axis runs over, the one named last changes fastest.
Arguments:
- right_side: float32 [20, 3, 32, 1024], P('mode', None, 'circ'), may hold values from -5 to 5
- stiffness: float32 [4, 32, 1024], P(None, 'circ'), may hold values from -0.15 to 2, as said below
- pairing: int32 [3, 20], replicated, may hold values from 0 to 19, each once within a row
- coupling: float32 [3, 20], replicated, may hold values from -1 to 1
Outputs:
- solution_field: float32 [20, 3, 32, 1024], P('mode', None, 'circ')
- residual: float32 [20, 3, 32, 1024], P('mode', None, 'circ')
Inputs may be any that keep to these rules, and one draw needn't show every extreme that they name: `pairing`: each row is a permutation of the 20 chaos modes. The mean stiffness lies in [1, 2], the three random modes in [-0.15, 0.15].
All inputs are finite; a program needn't handle non-finite values.
Results may differ from a plain program's by a relative error of at most 0.001.
Values sent between devices are 32-bit elements; how exact they have to be, the bound alone decides.
No kernel may reach another device: no remote copies, remote signals or barrier semaphores. Data moves between devices by JAX's collectives and lax.ppermute only.
A program may use at most 64 MiB of HBM per device.

v0:
```python
import math

import jax
import jax.numpy as jnp
from jax import lax
from jax.sharding import PartitionSpec as P

KM = 4
NL = 16
NT = 64
ITERS = 2


LAME_RATIO = 1.0


def padded_2(cells, sides, width):
    for axis, dim in sides:
        count = lax.axis_size(axis)
        head = lax.slice_in_dim(cells, 0, width, axis=dim)
        tail = lax.slice_in_dim(cells, cells.shape[dim] - width, cells.shape[dim], axis=dim)
        cells = jnp.concatenate(
            [
                lax.ppermute(tail, axis, [(i, (i + 1) % count) for i in range(count)]),
                cells,
                lax.ppermute(head, axis, [((i + 1) % count, i) for i in range(count)]),
            ],
            axis=dim,
        )
    return cells


def dir_weight(component, direction):
    return 1.0 + LAME_RATIO if component == direction else 1.0


def weight_column(direction, trailing):
    values = jnp.array([dir_weight(comp_no, direction) for comp_no in range(3)], jnp.float32)
    return values.reshape((3,) + (1,) * trailing)


def stencil(padded, coeff_pad, n_long, n_trans):
    num_modes, num_comps, span_pad, num_cells = padded.shape
    span = span_pad - 2
    center = padded[:, :, 1:-1]
    coeff_mid = coeff_pad[1:-1]
    right_face = 0.5 * (coeff_mid + coeff_pad[2:])
    left_face = 0.5 * (coeff_mid + coeff_pad[:-2])
    circ_part = right_face * (center - padded[:, :, 2:]) + left_face * (center - padded[:, :, :-2])
    field = center.reshape(num_modes, num_comps, span, n_long, n_trans)
    coeff_cube = coeff_mid.reshape(span, n_long, n_trans)
    long_face = 0.5 * (coeff_cube[:, :-1] + coeff_cube[:, 1:])
    long_flux = long_face * (field[:, :, :, 1:] - field[:, :, :, :-1])
    zero_row = jnp.zeros((num_modes, num_comps, span, 1, n_trans), jnp.float32)
    long_part = jnp.concatenate([zero_row, long_flux], 3) - jnp.concatenate(
        [long_flux, zero_row], 3
    )
    edge_pad = jnp.pad(coeff_cube, ((0, 0), (0, 0), (1, 1)), mode="edge")
    trans_face = 0.5 * (edge_pad[:, :, :-1] + edge_pad[:, :, 1:])
    zero_pad = jnp.pad(field, ((0, 0), (0, 0), (0, 0), (0, 0), (1, 1)))
    trans_flux = trans_face * (zero_pad[..., 1:] - zero_pad[..., :-1])
    trans_part = trans_flux[..., :-1] - trans_flux[..., 1:]
    inner = weight_column(1, 3) * long_part + weight_column(2, 3) * trans_part
    return weight_column(0, 2) * circ_part + inner.reshape(num_modes, num_comps, span, num_cells)


def build_coupling(pairing, coupling):
    modes = pairing.shape[1]
    onehot = (pairing[:, :, None] == jnp.arange(modes, dtype=jnp.int32)[None, None, :]).astype(
        jnp.float32
    )
    halfway = coupling[:, :, None] * onehot
    return 0.5 * (halfway + jnp.swapaxes(halfway, 1, 2))


def hartley_table(size):
    indices = jnp.arange(size, dtype=jnp.int32)
    product = indices[:, None] * indices[None, :] % size
    angle = 2.0 * math.pi / size * product.astype(jnp.float32)
    return jnp.cos(angle) + jnp.sin(angle)


def cosine_table(size):
    indices = jnp.arange(size, dtype=jnp.int32)
    product = (2 * indices[:, None] + 1) * indices[None, :] % (4 * size)
    return jnp.cos(math.pi / (2 * size) * product.astype(jnp.float32))


def sine_table(size):
    indices = jnp.arange(size, dtype=jnp.int32) + 1
    product = indices[:, None] * indices[None, :] % (2 * (size + 1))
    return jnp.sin(math.pi / (size + 1) * product.astype(jnp.float32))


def eigen_denominator(freq_circ, freq_long, freq_trans, n_circ, n_long, n_trans):
    lam_circ = 2.0 - 2.0 * jnp.cos(2.0 * math.pi / n_circ * freq_circ.astype(jnp.float32))
    lam_long = 2.0 - 2.0 * jnp.cos(math.pi / n_long * freq_long.astype(jnp.float32))
    lam_trans = 2.0 - 2.0 * jnp.cos(math.pi / (n_trans + 1) * (freq_trans + 1).astype(jnp.float32))
    norm_long = jnp.where(freq_long == 0, 1.0 * n_long, 0.5 * n_long).astype(jnp.float32)
    scale = n_circ * norm_long * (0.5 * (n_trans + 1))
    rows = []
    for comp_no in range(3):
        lam = (
            dir_weight(comp_no, 0) * lam_circ
            + dir_weight(comp_no, 1) * lam_long
            + dir_weight(comp_no, 2) * lam_trans
        )
        rows.append(lam * scale)
    return jnp.stack(rows, 0)


def on_device(right_side, stiffness, pairing, coupling):
    highest = lax.Precision.HIGHEST
    local_modes, num_comps, local_circ, num_cells = right_side.shape
    circ_devices = lax.axis_size("circ")
    full_circ = local_circ * circ_devices
    local_cols = num_cells // circ_devices
    gmat = build_coupling(pairing, coupling)
    coeff_pad = padded_2(stiffness, (("circ", 1),), 1)
    row_start = lax.axis_index("mode") * local_modes
    htab = hartley_table(full_circ)
    ctab = cosine_table(NL)
    stab = sine_table(NT)
    column_ids = lax.axis_index("circ") * local_cols + jnp.arange(local_cols, dtype=jnp.int32)
    denom = eigen_denominator(
        jnp.arange(full_circ, dtype=jnp.int32)[None, :],
        (column_ids // NT)[:, None],
        (column_ids % NT)[:, None],
        full_circ,
        NL,
        NT,
    )

    def spectral(piece):
        lanes = jnp.swapaxes(piece, 2, 3)
        scaled = jnp.einsum("pcqn,nk->pcqk", lanes, htab, precision=highest) / denom[None]
        restored = jnp.einsum("pcqk,kn->pcqn", scaled, htab, precision=highest)
        return lax.all_to_all(
            jnp.swapaxes(restored, 2, 3), "circ", split_axis=2, concat_axis=3, tiled=True
        )

    def precondition(values):
        field = values.reshape(local_modes, num_comps, local_circ, NL, NT)
        spec = jnp.einsum("pcnlt,lm->pcnmt", field, ctab, precision=highest)
        spec = jnp.einsum("pcnmt,ts->pcnms", spec, stab, precision=highest)
        spec = spec.reshape(local_modes, num_comps, local_circ, num_cells)
        spec = spectral(lax.all_to_all(spec, "circ", split_axis=3, concat_axis=2, tiled=True))
        spec = spec.reshape(local_modes, num_comps, local_circ, NL, NT)
        spec = jnp.einsum("pcnms,lm->pcnls", spec, ctab, precision=highest)
        spec = jnp.einsum("pcnls,ts->pcnlt", spec, stab, precision=highest)
        return spec.reshape(local_modes, num_comps, local_circ, num_cells)

    def precond_sum(residual, smoothed):
        return lax.psum(jnp.sum(residual * smoothed), ("circ", "mode"))

    solution_field = jnp.zeros_like(right_side)
    residual = right_side
    smoothed = precondition(residual)
    direction = smoothed
    inner_now = precond_sum(residual, smoothed)
    for iteration in range(ITERS):
        padded = padded_2(direction, (("circ", 2),), 1)
        result = stencil(padded, coeff_pad[0], NL, NT)
        empty = jnp.zeros((local_modes, num_comps, local_circ, num_cells), jnp.float32)
        total = empty
        fold_piece = lax.all_gather(padded, "mode", axis=0, tiled=True)
        piece_modes = fold_piece.shape[0]
        for order in range(1, KM):
            term = stencil(fold_piece, coeff_pad[order], NL, NT)
            block = lax.dynamic_slice(gmat[order - 1], (row_start, 0), (local_modes, piece_modes))
            total = total + jnp.einsum("ij,jcnq->icnq", block, term, precision=highest)
        image = result + total
        alpha = inner_now / lax.psum(jnp.sum(direction * image), ("circ", "mode"))
        solution_field = solution_field + alpha * direction
        residual = residual - alpha * image
        if iteration + 1 < ITERS:
            smoothed = precondition(residual)
            inner_next = precond_sum(residual, smoothed)
            direction = smoothed + inner_next / inner_now * direction
            inner_now = inner_next
    return (solution_field, residual)


def solution(mesh):
    placed = (P("mode", None, "circ", None), P(None, "circ", None), P(), P())
    return jax.shard_map(
        on_device,
        mesh=mesh,
        in_specs=placed,
        out_specs=(P("mode", None, "circ", None), P("mode", None, "circ", None)),
        check_vma=False,
    )
```

profile of v0, /device:TPU:0, one launch (start us, length us, event | category | flops | bytes accessed | tf_op | source)
XLA Modules:
  0.0 329.7 jit_solution(13580110705302427264)
XLA Ops:
  4.2 4.2 %copy.229 = f32[10,3,2,16,64]{0,2,1,4,3:T(2,128)S(1)} copy(f32[10,3,2,16,64]{4,3,2,1,0:T(8,128)} %fusion.59) | data formatting | bytes 491520 | tf_op jit(solution)/shard_map/reshape | solution.py:146
  8.4 5.7 %reshape.625 = f32[16,1,3840]{2,1,0:T(1,128)} reshape(f32[1024,3,2,10]{3,2,1,0:T(2,128)S(1)} %bitcast.150) | data formatting | bytes 491520
  14.1 7.4 %all-to-all-start = ((f32[16,1,3840]{2,1,0:T(1,128)}), f32[16,1,3840]{2,1,0:T(1,128)S(1)}, u32[]{:S(2)}, u32[]{:S(2)}) async-start(f32[16,1,3840]{2,1,0:T(1,128)} %reshape.625), calls=%async_computation | async-start | bytes 491520 | tf_op jit(solution)/shard_map/all_to_all | solution.py:147
  22.1 4.4 %collective-permute-start = (f32[4,1,1024]{2,1,0:T(1,128)S(1)}, f32[4,1,1024]{2,1,0:T(1,128)S(1)}, u32[]{:S(2)}, u32[]{:S(2)}) collective-permute-start(f32[4,1,1024]{2,1,0:T(1,128)S(1)} %get-tuple-element.53), channel_id=1, source_target_pairs={{2,0},{4,2},{6,4},{8,6},{10,8},{12,10},{14,12},{16,14},{18,16},{20... | collective-permute-start | bytes 49160 | tf_op jit(solution)/shard_map/ppermute | solution.py:26
  32.2 1.9 reduce
  34.1 5.9 %reshape.626 = f32[1024,3,2,10]{3,2,1,0:T(2,128)S(1)} reshape(f32[16,3840]{1,0:T(8,128)} %reduce) | data formatting | bytes 491520
  40.0 3.5 %copy.230 = f32[10,3,2,16,64]{4,3,2,1,0:T(8,128)} copy(f32[10,3,2,16,64]{0,2,1,4,3:T(2,128)S(1)} %bitcast.151) | data formatting | bytes 491520 | tf_op jit(solution)/shard_map/all_to_all | solution.py:147
  47.7 5.8 %all-to-all-start.1 = ((f32[16,1,3840]{2,1,0:T(1,128)}), f32[16,1,3840]{2,1,0:T(1,128)S(1)}, u32[]{:S(2)}, u32[]{:S(2)}) async-start(f32[16,1,3840]{2,1,0:T(1,128)} %reshape.627), calls=%async_computation.1 | async-start | bytes 491520 | tf_op jit(solution)/shard_map/all_to_all | solution.py:138
  55.6 7.7 %all-to-all-done.1 = f32[16,1,3840]{2,1,0:T(1,128)S(1)} async-done(((f32[16,1,3840]{2,1,0:T(1,128)}), f32[16,1,3840]{2,1,0:T(1,128)S(1)}, u32[]{:S(2)}, u32[]{:S(2)}) %all-to-all-start.1) | async-done | bytes 245792 | tf_op jit(solution)/shard_map/all_to_all | solution.py:138
  66.9 4.4 %collective-permute-start.1 = (f32[10,3,1,1024]{3,0,2,1:T(8,128)S(1)}, f32[10,3,1,1024]{3,0,2,1:T(8,128)S(1)}, u32[]{:S(2)}, u32[]{:S(2)}) collective-permute-start(f32[10,3,1,1024]{3,0,2,1:T(8,128)S(1)} %get-tuple-element.37), channel_id=1, source_target_pairs={{2,0},{4,2},{6,4},{8,6},{10,8},{12,10},{14,12},{16,14},{18,16},{20... | collective-permute-start | bytes 368648 | tf_op jit(solution)/shard_map/ppermute | solution.py:26
  75.9 11.3 %all_gather.6 = f32[20,3,4,1024]{3,2,1,0:T(4,128)S(1)} all-gather(f32[10,3,4,1024]{3,2,1,0:T(4,128)S(1)} %pad_maximum_fusion.1), channel_id=1, replica_groups=mesh['circ'=16,'mode'=2] {'mode'}, dimensions={0}, use_global_device_ids=true | all-gather | bytes 1474560 | tf_op jit(solution)/shard_map/all_gather | solution.py:166
  91.9 2.5 fusion.9
  94.5 2.5 reshape.604
  96.9 2.5 reshape.606
  100.7 2.8 multiply_add_fusion.4
  106.3 40.1 %all-reduce.20 = (f32[]{:T(128)}, f32[]{:T(128)}) all-reduce(f32[]{:T(128)} %multiply_reduce_fusion.2, f32[]{:T(128)} %get-tuple-element.72), channel_id=1, replica_groups=mesh['circ'=16,'mode'=2] {'circ','mode'}, use_global_device_ids=true, to_apply=%region_1.2 | all-reduce | flops 2 | bytes 16 | tf_op jit(solution)/shard_map/psum | solution.py:154
  149.9 3.6 %copy.234 = f32[10,3,2,16,64]{0,2,1,4,3:T(2,128)} copy(f32[10,3,2,16,64]{4,3,2,1,0:T(8,128)S(1)} %fusion.55) | data formatting | bytes 491520 | tf_op jit(solution)/shard_map/reshape | solution.py:146
  153.5 5.4 %reshape.629 = f32[16,1,3840]{2,1,0:T(1,128)S(1)} reshape(f32[1024,3,2,10]{3,2,1,0:T(2,128)} %bitcast.152) | data formatting | bytes 491520
  158.9 15.3 %all_to_all.66 = f32[16,1,3840]{2,1,0:T(1,128)S(1)} all-to-all(f32[16,1,3840]{2,1,0:T(1,128)S(1)} %reshape.629), channel_id=1, replica_groups=mesh['circ'=16,'mode'=2] {'circ'}, dimensions={0} | all-to-all | bytes 491520 | tf_op jit(solution)/shard_map/all_to_all | solution.py:147
  175.4 6.6 %reshape.630 = f32[1024,3,2,10]{3,2,1,0:T(2,128)} reshape(f32[16,3840]{1,0:T(8,128)S(1)} %reduce.2) | data formatting | bytes 491520
  182.0 4.1 %copy.235 = f32[10,3,2,16,64]{4,3,2,1,0:T(8,128)S(1)} copy(f32[10,3,2,16,64]{0,2,1,4,3:T(2,128)} %bitcast.153) | data formatting | bytes 491520 | tf_op jit(solution)/shard_map/all_to_all | solution.py:147
  188.5 12.5 %all_to_all.67 = f32[16,1,3840]{2,1,0:T(1,128)S(1)} all-to-all(f32[16,1,3840]{2,1,0:T(1,128)S(1)} %reshape.631), channel_id=1, replica_groups=mesh['circ'=16,'mode'=2] {'circ'}, dimensions={0} | all-to-all | bytes 491520 | tf_op jit(solution)/shard_map/all_to_all | solution.py:138
  205.1 38.5 %psum.30 = f32[]{:T(128)} all-reduce(f32[]{:T(128)} %fusion.32), channel_id=1, replica_groups=mesh['circ'=16,'mode'=2] {'circ','mode'}, use_global_device_ids=true, to_apply=%region_5.6 | all-reduce | flops 1 | bytes 8 | tf_op jit(solution)/shard_map/psum | solution.py:154
  245.4 2.6 collective-permute-start.4
  249.2 2.0 collective-permute-done.4
  251.2 4.6 %collective-permute-done.5 = f32[10,3,1,1024]{3,0,2,1:T(8,128)S(1)} collective-permute-done((f32[10,3,1,1024]{3,0,2,1:T(8,128)S(1)}, f32[10,3,1,1024]{3,0,2,1:T(8,128)S(1)}, u32[]{:S(2)}, u32[]{:S(2)}) %collective-permute-start.5) | collective-permute-done | bytes 122912 | tf_op jit(solution)/shard_map/ppermute | solution.py:24
  256.8 10.8 %all_gather.7 = f32[20,3,4,1024]{3,2,1,0:T(4,128)S(1)} all-gather(f32[10,3,4,1024]{3,2,1,0:T(4,128)S(1)} %copy.214), channel_id=1, replica_groups=mesh['circ'=16,'mode'=2] {'mode'}, dimensions={0}, use_global_device_ids=true | all-gather | bytes 1474560 | tf_op jit(solution)/shard_map/all_gather | solution.py:166
  271.6 2.5 fusion.3
  274.2 2.5 reshape.614
  276.7 2.5 reshape.615
  280.6 2.8 multiply_add_fusion
  286.2 39.9 %psum.31 = f32[]{:T(128)} all-reduce(f32[]{:T(128)} %get-tuple-element.74), channel_id=1, replica_groups=mesh['circ'=16,'mode'=2] {'circ','mode'}, use_global_device_ids=true, to_apply=%region_7.8 | all-reduce | flops 1 | bytes 8 | tf_op jit(solution)/shard_map/psum | solution.py:173
  (217 shorter events, 54.9 us)
Async XLA Ops:
  0.6 7.7 %copy-start.41 = (s32[16]{0:T(128)}, s32[16]{0:T(128)S(1)}, u32[]{:S(2)}) copy-start(s32[16]{0:T(128)S(1)} %multiply_add_fusion.8) | copy-start | bytes 196
  0.7 7.7 %copy-start.38 = (s32[64]{0:T(128)}, s32[64]{0:T(128)S(1)}, u32[]{:S(2)}) copy-start(s32[64]{0:T(128)S(1)} %iota_add_fusion.1) | copy-start | bytes 772
  4.2 17.3 %copy-start.3 = (f32[4,2,1024]{2,1,0:T(2,128)S(1)}, f32[4,2,1024]{2,1,0:T(2,128)}, u32[]{:S(2)}) copy-start(f32[4,2,1024]{2,1,0:T(2,128)} %param.29) | copy-start | bytes 98308
  4.2 22.7 %copy-start.54 = (f32[3,20]{1,0:T(4,128)S(1)}, f32[3,20]{1,0:T(4,128)}, u32[]{:S(2)}) copy-start(f32[3,20]{1,0:T(4,128)} %param.31) | copy-start | bytes 724
  4.2 22.7 %copy-start.55 = (s32[3,20]{1,0:T(4,128)S(1)}, s32[3,20]{1,0:T(4,128)}, u32[]{:S(2)}) copy-start(s32[3,20]{1,0:T(4,128)} %param.30) | copy-start | bytes 724
  14.1 17.5 %all-to-all-start = ((f32[16,1,3840]{2,1,0:T(1,128)}), f32[16,1,3840]{2,1,0:T(1,128)S(1)}, u32[]{:S(2)}, u32[]{:S(2)}) async-start(f32[16,1,3840]{2,1,0:T(1,128)} %reshape.625), calls=%async_computation | async-start | bytes 491520 | tf_op jit(solution)/shard_map/all_to_all | solution.py:147
  22.1 6.2 %collective-permute-start = (f32[4,1,1024]{2,1,0:T(1,128)S(1)}, f32[4,1,1024]{2,1,0:T(1,128)S(1)}, u32[]{:S(2)}, u32[]{:S(2)}) collective-permute-start(f32[4,1,1024]{2,1,0:T(1,128)S(1)} %get-tuple-element.53), channel_id=1, source_target_pairs={{2,0},{4,2},{6,4},{8,6},{10,8},{12,10},{14,12},{16,14},{18,16},{20... | collective-permute-start | bytes 49160 | tf_op jit(solution)/shard_map/ppermute | solution.py:26
  26.5 27.1 %collective-permute-start.2 = (f32[4,1,1024]{2,1,0:T(1,128)}, f32[4,1,1024]{2,1,0:T(1,128)}, u32[]{:S(2)}, u32[]{:S(2)}) collective-permute-start(f32[4,1,1024]{2,1,0:T(1,128)} %get-tuple-element.54), channel_id=1, source_target_pairs={{0,2},{2,4},{4,6},{6,8},{8,10},{10,12},{12,14},{14,16},{16,18},{18... | collective-permute-start | bytes 49160 | tf_op jit(solution)/shard_map/ppermute | solution.py:24
  44.9 20.0 %copy-start.42 = (s32[16]{0:T(128)S(1)}, s32[16]{0:T(128)}, u32[]{:S(2)}) copy-start(s32[16]{0:T(128)} %copy-done.41) | copy-start | bytes 196
  45.5 20.1 %copy-start.39 = (s32[64]{0:T(128)S(1)}, s32[64]{0:T(128)}, u32[]{:S(2)}) copy-start(s32[64]{0:T(128)} %copy-done.38) | copy-start | bytes 772
  47.7 15.6 %all-to-all-start.1 = ((f32[16,1,3840]{2,1,0:T(1,128)}), f32[16,1,3840]{2,1,0:T(1,128)S(1)}, u32[]{:S(2)}, u32[]{:S(2)}) async-start(f32[16,1,3840]{2,1,0:T(1,128)} %reshape.627), calls=%async_computation.1 | async-start | bytes 491520 | tf_op jit(solution)/shard_map/all_to_all | solution.py:138
  53.6 17.9 %copy-start.14 = (f32[2,16,65]{2,1,0:T(8,128)}, f32[2,16,65]{2,1,0:T(8,128)S(1)}, u32[]{:S(2)}) copy-start(f32[2,16,65]{2,1,0:T(8,128)S(1)} %fusion.69) | copy-start | bytes 24964
  55.6 15.9 %copy-start.8 = (f32[2,15,64]{2,1,0:T(8,128)S(1)}, f32[2,15,64]{2,1,0:T(8,128)}, u32[]{:S(2)}) copy-start(f32[2,15,64]{2,1,0:T(8,128)} %fusion.68) | copy-start | bytes 23044
  64.9 6.7 %copy-start.46 = (f32[3]{0:T(128)S(1)}, f32[3]{0:T(128)}, u32[]{:S(2)}) copy-start(f32[3]{0:T(128)} %constant.120.clone) | copy-start | bytes 40
  64.9 6.7 %copy-start.50 = (f32[3]{0:T(128)S(1)}, f32[3]{0:T(128)}, u32[]{:S(2)}) copy-start(f32[3]{0:T(128)} %constant.121.clone) | copy-start | bytes 40
  66.8 7.8 %collective-permute-start.3 = (f32[10,3,1,1024]{3,0,2,1:T(8,128)S(1)}, f32[10,3,1,1024]{3,0,2,1:T(8,128)S(1)}, u32[]{:S(2)}, u32[]{:S(2)}) collective-permute-start(f32[10,3,1,1024]{3,0,2,1:T(8,128)S(1)} %get-tuple-element.36), channel_id=1, source_target_pairs={{0,2},{2,4},{4,6},{6,8},{8,10},{10,12},{12,14},{14,16},{16,18},{18... | collective-permute-start | bytes 368648 | tf_op jit(solution)/shard_map/ppermute | solution.py:24
  66.9 7.9 %collective-permute-start.1 = (f32[10,3,1,1024]{3,0,2,1:T(8,128)S(1)}, f32[10,3,1,1024]{3,0,2,1:T(8,128)S(1)}, u32[]{:S(2)}, u32[]{:S(2)}) collective-permute-start(f32[10,3,1,1024]{3,0,2,1:T(8,128)S(1)} %get-tuple-element.37), channel_id=1, source_target_pairs={{2,0},{4,2},{6,4},{8,6},{10,8},{12,10},{14,12},{16,14},{18,16},{20... | collective-permute-start | bytes 368648 | tf_op jit(solution)/shard_map/ppermute | solution.py:26
  104.2 44.2 %copy-start.43 = (s32[16]{0:T(128)S(1)}, s32[16]{0:T(128)}, u32[]{:S(2)}) copy-start(s32[16]{0:T(128)} %copy-done.41) | copy-start | bytes 196
  104.9 44.3 %copy-start.40 = (s32[64]{0:T(128)S(1)}, s32[64]{0:T(128)}, u32[]{:S(2)}) copy-start(s32[64]{0:T(128)} %copy-done.38) | copy-start | bytes 772
  201.0 44.0 %copy-start.9 = (f32[2,15,64]{2,1,0:T(8,128)S(1)}, f32[2,15,64]{2,1,0:T(8,128)}, u32[]{:S(2)}) copy-start(f32[2,15,64]{2,1,0:T(8,128)} %fusion.68) | copy-start | bytes 23044
  202.6 42.5 %copy-start.15 = (f32[2,16,65]{2,1,0:T(8,128)S(1)}, f32[2,16,65]{2,1,0:T(8,128)}, u32[]{:S(2)}) copy-start(f32[2,16,65]{2,1,0:T(8,128)} %copy-done.14) | copy-start | bytes 24964
  204.3 43.7 %copy-start.48 = (f32[3]{0:T(128)S(1)}, f32[3]{0:T(128)}, u32[]{:S(2)}) copy-start(f32[3]{0:T(128)} %constant.120.clone) | copy-start | bytes 40
  204.3 43.7 %copy-start.52 = (f32[3]{0:T(128)S(1)}, f32[3]{0:T(128)}, u32[]{:S(2)}) copy-start(f32[3]{0:T(128)} %constant.121.clone) | copy-start | bytes 40
  245.4 5.8 %collective-permute-start.4 = (f32[10,3,1,1024]{3,0,2,1:T(8,128)S(1)}, f32[10,3,1,1024]{3,0,2,1:T(8,128)S(1)}, u32[]{:S(2)}, u32[]{:S(2)}) collective-permute-start(f32[10,3,1,1024]{3,0,2,1:T(8,128)S(1)} %get-tuple-element.35), channel_id=1, source_target_pairs={{2,0},{4,2},{6,4},{8,6},{10,8},{12,10},{14,12},{16,14},{18,16},{20... | collective-permute-start | bytes 368648 | tf_op jit(solution)/shard_map/ppermute | solution.py:26
  248.0 7.8 %collective-permute-start.5 = (f32[10,3,1,1024]{3,0,2,1:T(8,128)S(1)}, f32[10,3,1,1024]{3,0,2,1:T(8,128)S(1)}, u32[]{:S(2)}, u32[]{:S(2)}) collective-permute-start(f32[10,3,1,1024]{3,0,2,1:T(8,128)S(1)} %get-tuple-element.34), channel_id=1, source_target_pairs={{0,2},{2,4},{4,6},{6,8},{8,10},{10,12},{12,14},{14,16},{16,18},{18... | collective-permute-start | bytes 368648 | tf_op jit(solution)/shard_map/ppermute | solution.py:24
  249.2 21.1 %copy-start.12 = (f32[2,15,64]{2,1,0:T(8,128)S(1)}, f32[2,15,64]{2,1,0:T(8,128)}, u32[]{:S(2)}) copy-start(f32[2,15,64]{2,1,0:T(8,128)} %get-tuple-element.84) | copy-start | bytes 23044
  249.2 21.1 %copy-start.13 = (f32[2,15,64]{2,1,0:T(8,128)S(1)}, f32[2,15,64]{2,1,0:T(8,128)}, u32[]{:S(2)}) copy-start(f32[2,15,64]{2,1,0:T(8,128)} %get-tuple-element.85) | copy-start | bytes 23044
  274.2 6.4 %copy-start.24 = (f32[2,1024]{1,0:T(2,128)S(1)}, f32[2,1024]{1,0:T(2,128)}, u32[]{:S(2)}) copy-start(f32[2,1024]{1,0:T(2,128)} %get-tuple-element.45) | copy-start | bytes 24580
  274.2 6.4 %copy-start.27 = (f32[2,1024]{1,0:T(2,128)S(1)}, f32[2,1024]{1,0:T(2,128)}, u32[]{:S(2)}) copy-start(f32[2,1024]{1,0:T(2,128)} %get-tuple-element.39) | copy-start | bytes 24580
  274.2 6.4 %copy-start.28 = (f32[2,1024]{1,0:T(2,128)S(1)}, f32[2,1024]{1,0:T(2,128)}, u32[]{:S(2)}) copy-start(f32[2,1024]{1,0:T(2,128)} %get-tuple-element.40) | copy-start | bytes 24580
  274.2 6.4 %copy-start.29 = (f32[2,1024]{1,0:T(2,128)S(1)}, f32[2,1024]{1,0:T(2,128)}, u32[]{:S(2)}) copy-start(f32[2,1024]{1,0:T(2,128)} %get-tuple-element.41) | copy-start | bytes 24580
  274.2 6.4 %copy-start.45 = (f32[3]{0:T(128)S(1)}, f32[3]{0:T(128)}, u32[]{:S(2)}) copy-start(f32[3]{0:T(128)} %constant.122.clone) | copy-start | bytes 40
  (32 other events, 103.2 us)
where the time goes:
time: 336 us; the launch traced here: 330 us
  blocking collectives  168 us (50%)
  local copies, waits for them, and re-layouts  72.1 us (21%)
  other arithmetic  28.6 us (9%)
  starting transfers between devices  24.8 us (7%)
  waiting for transfers between devices  15.2 us (5%)
  matrix products  14.5 us (4%)
  between operations  6 us (2%)
    psum x2, blocking collectives, precond_sum(): return lax.psum(jnp.sum(residual * smoothed), ('circ', 'mode'))  78.6 us
    psum x1, blocking collectives, on_device(): alpha = inner_now / lax.psum(jnp.sum(direction * image), ('circ', 'mode'))  39.9 us
    unnamed x122, local copies, waits for them, and re-layouts  29.3 us
    all_gather x2, blocking collectives, on_device(): fold_piece = lax.all_gather(padded, 'mode', axis=0, tiled=True)  22.1 us
    all_to_all x1, blocking collectives, precondition(): lax.all_to_all(spec, 'circ', split_axis=3, concat_axis=2, tiled=True)  15.3 us
    reshape x8, local copies, waits for them, and re-layouts, stencil(): inner.reshape(num_modes, num_comps, span, num_cells)  14.4 us
    all_to_all x1, blocking collectives, spectral(): lax.all_to_all(jnp.swapaxes(restored, 2, 3), 'circ', split_axis=2, concat...  12.5 us
    ppermute x3, starting transfers between devices, padded_2(): lax.ppermute(head, axis, [((i + 1) % count, i) for i in range(count)])  11.4 us
  transfers between devices with their start and end apart: 8, of which 4 were waited for; matrix products, arithmetic and copies ran while one was open for 8% of the time, Pallas kernels for 0%

commit v1 on v0

v1 whole, which is shorter than its diff:
```python
import math

import jax
import jax.numpy as jnp
import numpy as np
from jax import lax
from jax.experimental import pallas as pl
from jax.experimental.pallas import tpu as pltpu
from jax.sharding import PartitionSpec as P

KM = 4
NL = 16
NT = 64
COMPS = 3
LANES = 2 * NT
HIGHEST = lax.Precision.HIGHEST

SHIFT = 2.0 / 3.0


def weight(comp, direction):
    return 2.0 if comp == direction else 1.0


def cosine_np():
    l = np.arange(NL)
    return np.cos(math.pi * l[None, :] * (2 * l[:, None] + 1) / (2 * NL))


def sine_np():
    t = np.arange(NT) + 1
    return np.sin(math.pi * t[:, None] * t[None, :] / (NT + 1))


def hartley_np(size):
    n = np.arange(size)
    angle = 2.0 * math.pi / size * (n[:, None] * n[None, :] % size)
    return np.cos(angle) + np.sin(angle)


def denominator_np(n_circ):
    lam_c = 2.0 - 2.0 * np.cos(2.0 * math.pi / n_circ * np.arange(n_circ))[:, None, None]
    lam_l = 2.0 - 2.0 * np.cos(math.pi / NL * np.arange(NL))[None, :, None]
    lam_t = 2.0 - 2.0 * np.cos(math.pi / (NT + 1) * (np.arange(NT) + 1))[None, None, :]
    norm = np.where(np.arange(NL) == 0, 1.0 * NL, 0.5 * NL)[None, :, None]
    rows = [weight(c, 0) * lam_c + weight(c, 1) * lam_l + weight(c, 2) * lam_t for c in range(COMPS)]
    return np.stack(rows) * (n_circ * norm * (0.5 * (NT + 1)))


COS = cosine_np()


def sine_pair():
    both = np.zeros((LANES, LANES))
    both[:NT, :NT] = sine_np()
    both[NT:, NT:] = sine_np()
    return both.astype(np.float32)


def circulant_table(n_circ):
    half = n_circ // 2
    quarter = half // 2
    freq = np.arange(n_circ)
    inverse = 1.0 / denominator_np(n_circ)
    turn = np.cos(2.0 * math.pi / n_circ * (freq[:, None] * freq[None, :] % n_circ))
    g = np.einsum("dk,ckms->dcms", turn, inverse)
    same = np.stack([np.concatenate([g[2 * d], g[2 * d]], -1) for d in range(half)])
    cross = np.stack(
        [np.concatenate([g[(2 * d - 1) % n_circ], g[(2 * d + 1) % n_circ]], -1) for d in range(half)]
    )
    parts = []
    for full in (same, cross):
        parts.append(0.5 * (full[:quarter] + full[quarter:]))
        parts.append(0.5 * (full[:quarter] - full[quarter:]))
    table = np.stack(parts)
    return np.transpose(table, (3, 0, 1, 2, 4)).astype(np.float32)


def whole():
    return pl.BlockSpec(memory_space=pltpu.VMEM)


def smem():
    return pl.BlockSpec(memory_space=pltpu.SMEM)


def params():
    return pltpu.CompilerParams(vmem_limit_bytes=32 * 1024 * 1024)


def forward_rows(load, sine_ref, out_ref, fields):
    for base in range(0, fields, 8):
        plus, minus = [], []
        for l in range(NL // 2):
            a, b = load(l, base), load(NL - 1 - l, base)
            plus.append(a + b)
            minus.append(a - b)
        for m in range(NL):
            src = plus if m % 2 == 0 else minus
            acc = src[0] * float(COS[0, m])
            for l in range(1, NL // 2):
                acc = acc + src[l] * float(COS[l, m])
            out_ref[m, base : base + 8, :] = acc
    flat = out_ref[...].reshape(NL * fields, LANES)
    done = jnp.dot(flat, sine_ref[...], precision=HIGHEST, preferred_element_type=jnp.float32)
    out_ref[...] = done.reshape(NL, fields, LANES)


def first_kernel(fields, b_ref, sine_ref, out_ref):
    forward_rows(lambda l, base: b_ref[pl.ds(base * NL + l, 8, stride=NL), :], sine_ref, out_ref, fields)


def next_kernel(fields, b_ref, own_ref, recv_ref, sine_ref, out_ref, image_ref, work_ref):
    image = own_ref[...] + recv_ref[...]
    image_ref[...] = image
    work_ref[...] = b_ref[...] - SHIFT * image
    forward_rows(lambda l, base: work_ref[pl.ds(base * NL + l, 8, stride=NL), :], sine_ref, out_ref, fields)


def circ_kernel(fields, half, x_ref, table_ref, out_ref):
    quarter = half // 2
    comp_row = lax.broadcasted_iota(jnp.int32, (8, LANES), 0)
    low = lax.broadcasted_iota(jnp.int32, (8, LANES), 1) < NT
    for base in range(0, fields, 8):
        comp = (comp_row + base) % COMPS

        def spread(part, d):
            rows = table_ref[part, d]
            return jnp.where(comp == 0, rows[0:1], jnp.where(comp == 1, rows[1:2], rows[2:3]))

        coef = [[spread(part, d) for d in range(quarter)] for part in range(4)]
        plus, minus, plus_x, minus_x = [], [], [], []
        for c in range(quarter):
            a = x_ref[c, base : base + 8, :]
            b = x_ref[c + quarter, base : base + 8, :]
            plus.append(a + b)
            minus.append(a - b)
            plus_x.append(pltpu.roll(a + b, NT, 1))
            minus_x.append(pltpu.roll(a - b, NT, 1))
        outs = [None] * half
        for c in range(quarter):
            even = odd = None
            for e in range(quarter):
                d = (c - e) % quarter
                term = coef[0][d] * plus[e] + coef[2][d] * plus_x[e]
                even = term if even is None else even + term
                term = coef[1][d] * minus[e] + coef[3][d] * minus_x[e]
                if c < e:
                    term = -term
                odd = term if odd is None else odd + term
            outs[c] = even + odd
            outs[c + quarter] = even - odd
        for c in range(half):
            out_ref[c, 0, base : base + 8, :] = outs[c]
            out_ref[c, 1, base : base + 8, :] = jnp.where(low, outs[(c + 1) % half], outs[c - 1])


def lane_masks(rows):
    lane = lax.broadcasted_iota(jnp.int32, (rows, LANES), 1)
    return lane < NT, lane % NT == 0, lane % NT == NT - 1


def neighbours(mid, ends, low):
    right = pltpu.roll(jnp.where(low, ends, mid), NT, 1)
    left = pltpu.roll(jnp.where(low, mid, ends), NT, 1)
    return right, left


def operator_kernel(
    modes, fields, row_ref, pair_ref, coup_ref, spec_ref, sine_ref, stiff_ref, stiff_l_ref, stiff_r_ref,
    field_ref, own_ref, cross_ref, work_ref, ends_ref, face_ref, term_ref, inv_ref
):
    total_modes = pair_ref.shape[1]
    low, first, last = lane_masks(NL)
    row = lax.broadcasted_iota(jnp.int32, (NL, LANES), 0)
    for k in range(KM):
        a = stiff_ref[k]
        ends = jnp.where(low, stiff_r_ref[k], stiff_l_ref[k])
        right, left = neighbours(a, ends, low)
        above = jnp.where(last, a, pltpu.roll(a, LANES - 1, 1))
        below = jnp.where(first, a, pltpu.roll(a, 1, 1))
        ahead = pltpu.roll(a, NL - 1, 0)
        behind = pltpu.roll(a, 1, 0)
        faces = [
            0.5 * (a + right),
            0.5 * (a + left),
            jnp.where(row == NL - 1, 0.0, 0.5 * (a + ahead)),
            jnp.where(row == 0, 0.0, 0.5 * (a + behind)),
            0.5 * (a + above),
            0.5 * (a + below),
        ]
        for nb in range(6):
            for c in range(COMPS):
                w = weight(c, nb // 2)
                face_ref[k, nb, c * NL : (c + 1) * NL, :] = faces[nb] * w if w != 1.0 else faces[nb]
    def invert(j, carry):
        for k in range(KM - 1):
            inv_ref[k, pair_ref[k, j]] = j
        return carry

    lax.fori_loop(0, total_modes, invert, 0)
    flat = spec_ref[...].reshape(NL * 2 * fields, LANES)
    term = jnp.dot(flat, sine_ref[...], precision=HIGHEST, preferred_element_type=jnp.float32)
    term = term.reshape(NL, 2, fields, LANES)
    for part in range(2):
        dst = field_ref if part == 0 else ends_ref
        for base in range(0, fields, 8):
            y = [term[m, part, base : base + 8, :] for m in range(NL)]
            for l in range(NL // 2):
                even = y[0] * float(COS[l, 0])
                odd = y[1] * float(COS[l, 1])
                for m in range(2, NL, 2):
                    even = even + y[m] * float(COS[l, m])
                    odd = odd + y[m + 1] * float(COS[l, m + 1])
                dst[pl.ds(base * NL + l, 8, stride=NL), :] = even + odd
                dst[pl.ds(base * NL + NL - 1 - l, 8, stride=NL), :] = even - odd
    span = COMPS * NL
    low, first, last = lane_masks(span)

    def stencils(j, carry):
        at = pl.ds(pl.multiple_of(j * span, 8), span)
        mid = field_ref[at, :]
        right, left = neighbours(mid, ends_ref[at, :], low)
        diffs = [
            mid - right,
            mid - left,
            mid - pltpu.roll(mid, span - 1, 0),
            mid - pltpu.roll(mid, 1, 0),
            mid - jnp.where(last, 0.0, pltpu.roll(mid, LANES - 1, 1)),
            mid - jnp.where(first, 0.0, pltpu.roll(mid, 1, 1)),
        ]
        for k in range(KM):
            acc = face_ref[k, 0] * diffs[0]
            for nb in range(1, 6):
                acc = acc + face_ref[k, nb] * diffs[nb]
            term_ref[k, j] = acc
        return carry

    lax.fori_loop(0, modes, stencils, 0)
    row_start = row_ref[0]

    def mixed(i, acc):
        for k in range(KM - 1):
            for way in range(2):
                partner = pair_ref[k, i] if way == 0 else inv_ref[k, i]
                coef = 0.5 * (coup_ref[k, i] if way == 0 else coup_ref[k, partner])
                local = partner - row_start
                inside = jnp.logical_and(local >= 0, local < modes)
                coef = jnp.where(inside, coef, 0.0)
                local = jnp.clip(local, 0, modes - 1)
                part = coef * term_ref[k + 1, local]
                acc = part if acc is None else acc + part
        return acc

    other_start = total_modes - modes - row_start

    def mix(i, carry):
        at = pl.ds(pl.multiple_of(i * span, 8), span)
        cross_ref[at, :] = mixed(other_start + i, None)
        own_ref[at, :] = mixed(row_start + i, term_ref[0, i])
        return carry

    lax.fori_loop(0, modes, mix, 0)
    pad = fields * NL - modes * span
    if pad:
        zero = jnp.zeros((pad, LANES), jnp.float32)
        cross_ref[modes * span :, :] = zero
        own_ref[modes * span :, :] = zero
        field_ref[modes * span :, :] = zero


def sums_kernel(rows, b_ref, u_ref, v_ref, z_ref, own_ref, recv_ref, image_ref, part_ref):
    q = own_ref[...] + recv_ref[...]
    image_ref[...] = q
    b, u, v, z = b_ref[...], u_ref[...], v_ref[...], z_ref[...]

    def fold(x):
        x = jnp.sum(x.reshape(rows // 8, 8, LANES), axis=0)
        return jnp.sum(x, axis=0, keepdims=True)

    sums = [fold(b * u), fold(u * v), fold(v * z), fold(b * z), fold(z * q)]
    sums += [jnp.zeros((3, LANES), jnp.float32)]
    part = jnp.concatenate(sums, axis=0)
    for i in range(part_ref.shape[0]):
        part_ref[i] = part


def final_kernel(parts_ref, b_ref, u_ref, v_ref, z_ref, q_ref, x_ref, r_ref):
    total = jnp.sum(jnp.sum(parts_ref[...], axis=0), axis=1, keepdims=True)
    bu, uv, vz, bz, zq = (total[i : i + 1, :] for i in range(5))
    a0 = bu / uv
    t = vz / uv
    c1 = (bz - a0 * vz) / (zq - t * vz)
    c0 = a0 - c1 * t
    x_ref[...] = c0 * u_ref[...] + c1 * z_ref[...]
    r_ref[...] = b_ref[...] - c0 * v_ref[...] - c1 * q_ref[...]


def on_device(right_side, stiffness, pairing, coupling):
    modes, comps, local_circ, num_cells = right_side.shape
    circ = lax.axis_size("circ")
    mode_blocks = lax.axis_size("mode")
    n_circ = local_circ * circ
    fields = -(-(modes * comps) // 8) * 8
    rows = fields * NL
    pad_fields = fields - modes * comps
    f32 = jnp.float32

    def struct(*shape):
        return jax.ShapeDtypeStruct(shape, f32)

    sine = jnp.asarray(sine_pair())
    b = right_side.reshape(modes * comps, local_circ, NL, NT)
    b = jnp.swapaxes(b, 1, 2).reshape(modes * comps * NL, LANES)
    b = jnp.pad(b, ((0, pad_fields * NL), (0, 0)))
    stiff = jnp.swapaxes(stiffness.reshape(KM, local_circ, NL, NT), 1, 2).reshape(KM, NL, LANES)
    ahead = [(i, (i + 1) % circ) for i in range(circ)]
    back = [((i + 1) % circ, i) for i in range(circ)]
    stiff_l = lax.ppermute(stiff, "circ", ahead)
    stiff_r = lax.ppermute(stiff, "circ", back)
    row_start = (lax.axis_index("mode") * modes).astype(jnp.int32).reshape(1)
    me = lax.axis_index("circ").astype(jnp.int32)

    split = circ // NL
    if split == 1:
        table = lax.dynamic_index_in_dim(jnp.asarray(circulant_table(n_circ)), me, 0, keepdims=False)

        def round_trip(spec):
            spec = lax.all_to_all(spec, "circ", split_axis=0, concat_axis=0)
            spec = pl.pallas_call(
                lambda *refs: circ_kernel(fields, circ, *refs),
                out_shape=struct(circ, 2, fields, LANES),
                in_specs=[whole()] * 2,
                out_specs=whole(),
                compiler_params=params(),
            )(spec, table)
            return lax.all_to_all(spec, "circ", split_axis=0, concat_axis=0)

    else:
        span = NT // split
        htab = jnp.asarray(hartley_np(n_circ), f32)
        denom = jnp.asarray(denominator_np(n_circ), f32).reshape(comps, n_circ, NL, split, span)
        denom = denom.transpose(2, 3, 0, 1, 4).reshape(circ, comps, n_circ, span)
        denom = lax.dynamic_index_in_dim(denom, me, 0, keepdims=False)

        def round_trip(spec):
            spec = spec.reshape(NL, fields, local_circ, split, span).transpose(0, 3, 1, 2, 4)
            spec = spec.reshape(circ, fields, local_circ, span)
            spec = lax.all_to_all(spec, "circ", split_axis=0, concat_axis=0)
            spec = spec[:, : modes * comps]
            spec = jnp.einsum("cfes,cek->fks", spec, htab.reshape(circ, local_circ, n_circ), precision=HIGHEST)
            spec = spec.reshape(modes, comps, n_circ, span) / denom[None]
            spec = jnp.einsum("pcks,kn->npcs", spec, htab, precision=HIGHEST)
            spec = spec.reshape(n_circ, modes * comps, span)
            spec = jnp.pad(spec, ((0, 0), (0, pad_fields), (0, 0)))
            own = spec.reshape(circ, local_circ, fields, span)
            after = jnp.roll(own[:, 0], -1, axis=0)
            before = jnp.roll(own[:, -1], 1, axis=0)
            spec = jnp.stack([own[:, 0], own[:, 1], after, before], axis=1)
            spec = lax.all_to_all(spec, "circ", split_axis=0, concat_axis=0)
            spec = spec.reshape(NL, split, 2, 2, fields, span).transpose(0, 2, 4, 3, 1, 5)
            return spec.reshape(NL, 2, fields, LANES)

    def operate(spec):
        return pl.pallas_call(
            lambda *refs: operator_kernel(modes, fields, *refs),
            out_shape=[struct(rows, LANES)] * 3,
            in_specs=[smem()] * 3 + [whole()] * 5,
            out_specs=[whole()] * 3,
            scratch_shapes=[
                pltpu.VMEM((8, LANES), f32),
                pltpu.VMEM((rows, LANES), f32),
                pltpu.VMEM((KM, 6, COMPS * NL, LANES), f32),
                pltpu.VMEM((KM, modes, COMPS * NL, LANES), f32),
                pltpu.SMEM((KM - 1, modes * mode_blocks), jnp.int32),
            ],
            compiler_params=params(),
        )(row_start, pairing, coupling, spec, sine, stiff, stiff_l, stiff_r)

    swap = [(0, 1), (1, 0)]

    spec = pl.pallas_call(
        lambda *refs: first_kernel(fields, *refs),
        out_shape=struct(NL, fields, LANES),
        in_specs=[whole()] * 2,
        out_specs=whole(),
        compiler_params=params(),
    )(b, sine)
    u, own, cross = operate(round_trip(spec))
    recv = lax.ppermute(cross, "mode", swap)
    spec, v = pl.pallas_call(
        lambda *refs: next_kernel(fields, *refs),
        out_shape=[struct(NL, fields, LANES), struct(rows, LANES)],
        in_specs=[whole()] * 4,
        out_specs=[whole()] * 2,
        scratch_shapes=[pltpu.VMEM((rows, LANES), f32)],
        compiler_params=params(),
    )(b, own, recv, sine)
    z, own, cross = operate(round_trip(spec))
    recv = lax.ppermute(cross, "mode", swap)
    devices = circ * mode_blocks
    q, part = pl.pallas_call(
        lambda *refs: sums_kernel(rows, *refs),
        out_shape=[struct(rows, LANES), struct(devices, 8, LANES)],
        in_specs=[whole()] * 6,
        out_specs=[whole()] * 2,
        compiler_params=params(),
    )(b, u, v, z, own, recv)
    parts = lax.all_to_all(part, ("circ", "mode"), split_axis=0, concat_axis=0)
    x, r = pl.pallas_call(
        final_kernel,
        out_shape=[struct(rows, LANES)] * 2,
        in_specs=[whole()] * 6,
        out_specs=[whole()] * 2,
        compiler_params=params(),
    )(parts, b, u, v, z, q)

    def give(values):
        values = values[: modes * comps * NL].reshape(modes * comps, NL, local_circ, NT)
        return jnp.swapaxes(values, 1, 2).reshape(right_side.shape)

    return give(x), give(r)


def solution(mesh):
    placed = (P("mode", None, "circ", None), P(None, "circ", None), P(), P())
    return jax.shard_map(
        on_device,
        mesh=mesh,
        in_specs=placed,
        out_specs=(P("mode", None, "circ", None), P("mode", None, "circ", None)),
        check_vma=False,
    )
```

time: 336 us -> 114 us (0.34); the launches traced: 330 us -> 114 us
  blocking collectives: 168 us -> 44.1 us
  local copies, waits for them, and re-layouts: 72.1 us -> 6.33 us
  other arithmetic: 28.6 us -> 0 us
  waiting for transfers between devices: 15.2 us -> 32.8 us
  matrix products: 14.5 us -> 0 us
  Pallas kernels: 0 us -> 11.1 us
  starting transfers between devices: 24.8 us -> 18.6 us
  between operations: 6 us -> 0.79 us
    psum x3 -> x0, blocking collectives: 118 us -> none  [the longest x2 78.6 us: precond_sum(): return lax.psum(jnp.sum(residual * smoothed), ('circ', 'mode'))]
    unnamed x122 -> x8, local copies, waits for them, and re-layouts: 29.3 us -> 0.82 us
    reshape x21 -> x10, local copies, waits for them, and re-layouts: 27.9 us -> 4.53 us  [the longest x2 1.91 us: give(): return jnp.swapaxes(values, 1, 2).reshape(right_side.shape)]
    all_gather x2 -> x0, blocking collectives: 22.1 us -> none  [on_device(): fold_piece = lax.all_gather(padded, 'mode', axis=0, tiled=True)]
    all_to_all x2 -> x3, blocking collectives: 27.8 us -> 44.1 us  [the longest x1 17.2 us: round_trip(): return lax.all_to_all(spec, 'circ', split_axis=0, concat_axis=0)]
    ppermute x6 -> x4, waiting for transfers between devices: 7.52 us -> 23.5 us  [the longest x2 13.5 us: on_device(): recv = lax.ppermute(cross, 'mode', swap)]
    dot_general x18 -> x0, matrix products: 14.5 us -> none  [the longest x6 5.38 us: on_device(): total = total + jnp.einsum('ij,jcnq->icnq', block, term, precision=highest)]
    add x11 -> x0, other arithmetic: 11.5 us -> none  [the longest x2 5.62 us: stencil(): weight_column(0, 2) * circ_part]
  transfers between devices with their start and end apart: 8 -> 6, of which waited for: 4 -> 6; matrix products, arithmetic and copies ran while one was open for 8% -> 1% of each run, Pallas kernels for 0% -> 0%
where the time goes in v1:
time: 114 us
  blocking collectives  44.1 us (39%)
  waiting for transfers between devices  32.8 us (29%)
  starting transfers between devices  18.6 us (16%)
  Pallas kernels  11.1 us (10%)
  local copies, waits for them, and re-layouts  6.33 us (6%)
    all_to_all x1, blocking collectives, round_trip(): return lax.all_to_all(spec, 'circ', split_axis=0, concat_axis=0)  17.2 us
    all_to_all x1, blocking collectives, round_trip(): spec = lax.all_to_all(spec, 'circ', split_axis=0, concat_axis=0)  14.2 us
    ppermute x2, waiting for transfers between devices, on_device(): recv = lax.ppermute(cross, 'mode', swap)  13.5 us
    all_to_all x1, blocking collectives, on_device(): parts = lax.all_to_all(part, ('circ', 'mode'), split_axis=0, concat_axis=0)  12.7 us
    all_to_all x1, waiting for transfers between devices, round_trip(): spec = lax.all_to_all(spec, 'circ', split_axis=0, concat_axis=0)  9.18 us
    all_to_all x1, starting transfers between devices, round_trip(): spec = lax.all_to_all(spec, 'circ', split_axis=0, concat_axis=0)  7.38 us
    pallas_call x2, Pallas kernels, operate(): pl.pallas_call(lambda *refs: operator_kernel(modes, fields, *refs), out_s...  7.23 us
    ppermute x1, waiting for transfers between devices, on_device(): stiff_r = lax.ppermute(stiff, 'circ', back)  5.13 us
  transfers between devices with their start and end apart: 6, of which 6 were waited for; matrix products, arithmetic and copies ran while one was open for 1% of the time, Pallas kernels for 0%

profile of v1, /device:TPU:0, one launch (start us, length us, event | category | flops | bytes accessed | tf_op | source)
XLA Modules:
  0.0 113.7 jit_solution(2834470441121975383)
XLA Ops:
  0.6 1.3 %reshape.31 = f32[30,2,16,64]{3,2,1,0:T(8,128)S(1)} reshape(f32[10,3,2,1024]{3,2,1,0:T(2,128)} %param.6) | data formatting | bytes 491520 | tf_op jit(solution)/shard_map/reshape | solution.py:313
  1.9 0.3 copy.14
  2.1 0.3 reshape.32
  2.5 0.8 copy-done
  3.3 1.2 %shard_map.77 = f32[16,32,128]{2,1,0:T(8,128)} custom-call(f32[512,128]{1,0:T(8,128)S(1)} %pad.4.refs_0_.b_ref, f32[128,128]{1,0:T(8,128)S(1)} %copy-done), custom_call_target="tpu_custom_call" | custom-call | tf_op jit(solution)/shard_map/pallas_call | solution.py:382
  4.5 7.4 %all-to-all-start = ((f32[16,32,128]{2,1,0:T(8,128)}), f32[16,32,128]{2,1,0:T(8,128)S(1)}, u32[]{:S(2)}, u32[]{:S(2)}) async-start(f32[16,32,128]{2,1,0:T(8,128)} %shard_map.77), calls=%async_computation | async-start | bytes 524288 | tf_op jit(solution)/shard_map/all_to_all | solution.py:329
  11.9 0.9 dynamic-slice_bitcast_fusion.refs_1_
  12.7 9.2 %all-to-all-done.refs_0_ = f32[16,32,128]{2,1,0:T(8,128)S(1)} async-done(((f32[16,32,128]{2,1,0:T(8,128)}), f32[16,32,128]{2,1,0:T(8,128)S(1)}, u32[]{:S(2)}, u32[]{:S(2)}) %all-to-all-start) | async-done | bytes 262176 | tf_op jit(solution)/shard_map/all_to_all | solution.py:329
  21.9 1.2 %shard_map.78 = f32[16,2,32,128]{3,2,1,0:T(8,128)} custom-call(f32[16,32,128]{2,1,0:T(8,128)S(1)} %all-to-all-done.refs_0_, f32[4,8,3,128]{3,2,1,0:T(4,128)S(1)} %dynamic-slice_bitcast_fusion.refs_1_), custom_call_target="tpu_custom_call" | custom-call | tf_op jit(solution)/shard_map/pallas_call | solution.py:330
  23.2 3.7 %all-to-all-start.1 = ((f32[16,2,32,128]{3,2,1,0:T(8,128)}), f32[16,2,32,128]{3,2,1,0:T(8,128)S(1)}, u32[]{:S(2)}, u32[]{:S(2)}) async-start(f32[16,2,32,128]{3,2,1,0:T(8,128)} %shard_map.78), calls=%async_computation.1 | async-start | bytes 1048576 | tf_op jit(solution)/shard_map/all_to_all | solution.py:337
  27.0 0.1 reshape.35.refs_5_
  27.1 4.4 %collective-permute-start.1 = (f32[4,16,128]{2,1,0:T(8,128)S(1)}, f32[4,16,128]{2,1,0:T(8,128)S(1)}, u32[]{:S(2)}, u32[]{:S(2)}) collective-permute-start(f32[4,16,128]{2,1,0:T(8,128)S(1)} %reshape.35.refs_5_), channel_id=1, source_target_pairs={{2,0},{4,2},{6,4},{8,6},{10,8},{12,10},{14,12},{16,14},{18,16},{20... | collective-permute-start | bytes 98312 | tf_op jit(solution)/shard_map/ppermute | solution.py:320
  31.5 5.1 %collective-permute-done.1.refs_7_ = f32[4,16,128]{2,1,0:T(8,128)S(1)} collective-permute-done((f32[4,16,128]{2,1,0:T(8,128)S(1)}, f32[4,16,128]{2,1,0:T(8,128)S(1)}, u32[]{:S(2)}, u32[]{:S(2)}) %collective-permute-start.1) | collective-permute-done | bytes 32800 | tf_op jit(solution)/shard_map/ppermute | solution.py:320
  36.6 4.9 %collective-permute-done.refs_6_ = f32[4,16,128]{2,1,0:T(8,128)S(1)} collective-permute-done((f32[4,16,128]{2,1,0:T(8,128)S(1)}, f32[4,16,128]{2,1,0:T(8,128)S(1)}, u32[]{:S(2)}, u32[]{:S(2)}) %collective-permute-start) | collective-permute-done | bytes 32800 | tf_op jit(solution)/shard_map/ppermute | solution.py:319
  41.5 0.1 all-to-all-done.1.refs_3_
  41.6 3.6 %shard_map.79 = (f32[512,128]{1,0:T(8,128)S(1)}, f32[512,128]{1,0:T(8,128)S(1)}, f32[512,128]{1,0:T(8,128)S(1)}) custom-call(s32[1]{0:T(128)} %bitcast.1.refs_0_, s32[3,20]{1,0:T(4,128)S(1)} %copy-done.1, f32[3,20]{1,0:T(4,128)S(1)} %copy-done.2, f32[16,2,32,128]{3,2,1,0:T(8,128)S(1)} %all-to-all-done.1.refs_3_, f32[128,128]{1,0:T(8,128)S(1)} %copy-done, ...), custom_call_target="tpu_custom_call" | custom-call | tf_op jit(solution)/shard_map/pallas_call | solution.py:365
  45.3 1.6 %collective-permute-start.2 = (f32[512,128]{1,0:T(8,128)S(1)}, f32[512,128]{1,0:T(8,128)S(1)}, u32[]{:S(2)}, u32[]{:S(2)}) collective-permute-start(f32[512,128]{1,0:T(8,128)S(1)} %get-tuple-element.16), channel_id=1, source_target_pairs={{0,1},{1,0},{2,3},{3,2},{4,5},{5,4},{6,7},{7,6},{8,9},{9,8},{10,11... | collective-permute-start | bytes 786440 | tf_op jit(solution)/shard_map/ppermute | solution.py:390
  46.8 6.7 %collective-permute-done.2.refs_2_ = f32[512,128]{1,0:T(8,128)S(1)} collective-permute-done((f32[512,128]{1,0:T(8,128)S(1)}, f32[512,128]{1,0:T(8,128)S(1)}, u32[]{:S(2)}, u32[]{:S(2)}) %collective-permute-start.2) | collective-permute-done | bytes 262176 | tf_op jit(solution)/shard_map/ppermute | solution.py:390
  53.6 0.6 shard_map.80
  54.1 14.2 %all_to_all.25.refs_0_ = f32[16,32,128]{2,1,0:T(8,128)S(1)} all-to-all(f32[16,32,128]{2,1,0:T(8,128)S(1)} %get-tuple-element.18), channel_id=1, replica_groups=mesh['circ'=16,'mode'=2] {'circ'}, dimensions={0} | all-to-all | bytes 524288 | tf_op jit(solution)/shard_map/all_to_all | solution.py:329
  68.3 0.4 shard_map.81
  68.7 17.2 %all_to_all.26.refs_3_ = f32[16,2,32,128]{3,2,1,0:T(8,128)S(1)} all-to-all(f32[16,2,32,128]{3,2,1,0:T(8,128)S(1)} %shard_map.81), channel_id=1, replica_groups=mesh['circ'=16,'mode'=2] {'circ'}, dimensions={0} | all-to-all | bytes 1048576 | tf_op jit(solution)/shard_map/all_to_all | solution.py:337
  86.0 3.6 %shard_map.82 = (f32[512,128]{1,0:T(8,128)S(1)}, f32[512,128]{1,0:T(8,128)S(1)}, f32[512,128]{1,0:T(8,128)S(1)}) custom-call(s32[1]{0:T(128)} %bitcast.1.refs_0_, s32[3,20]{1,0:T(4,128)S(1)} %copy-done.1, f32[3,20]{1,0:T(4,128)S(1)} %copy-done.2, f32[16,2,32,128]{3,2,1,0:T(8,128)S(1)} %all_to_all.26.refs_3_, f32[128,128]{1,0:T(8,128)S(1)} %copy-done, ...), custom_call_target="tpu_custom_call" | custom-call | tf_op jit(solution)/shard_map/pallas_call | solution.py:365
  89.6 1.6 %collective-permute-start.3 = (f32[512,128]{1,0:T(8,128)S(1)}, f32[512,128]{1,0:T(8,128)S(1)}, u32[]{:S(2)}, u32[]{:S(2)}) collective-permute-start(f32[512,128]{1,0:T(8,128)S(1)} %get-tuple-element.21), channel_id=1, source_target_pairs={{0,1},{1,0},{2,3},{3,2},{4,5},{5,4},{6,7},{7,6},{8,9},{9,8},{10,11... | collective-permute-start | bytes 786440 | tf_op jit(solution)/shard_map/ppermute | solution.py:400
  91.2 6.7 %collective-permute-done.3.refs_5_ = f32[512,128]{1,0:T(8,128)S(1)} collective-permute-done((f32[512,128]{1,0:T(8,128)S(1)}, f32[512,128]{1,0:T(8,128)S(1)}, u32[]{:S(2)}, u32[]{:S(2)}) %collective-permute-start.3) | collective-permute-done | bytes 262176 | tf_op jit(solution)/shard_map/ppermute | solution.py:400
  97.9 0.1 shard_map.83
  98.1 12.7 %all_to_all.27.parts_ref = f32[32,8,128]{2,1,0:T(8,128)S(1)} all-to-all(f32[32,8,128]{2,1,0:T(8,128)S(1)} %get-tuple-element.22), channel_id=1, replica_groups=mesh['circ'=16,'mode'=2] {'circ','mode'}, dimensions={0} | all-to-all | bytes 262144 | tf_op jit(solution)/shard_map/all_to_all | solution.py:409
  110.8 0.3 shard_map.84
  111.1 0.3 reshape.36
  111.4 1.0 reshape.37
  112.4 0.3 reshape.38
  112.8 1.0 reshape.39
  (15 shorter events, 0.3 us)
Async XLA Ops:
  2.4 0.8 copy-start
  4.5 17.4 %all-to-all-start = ((f32[16,32,128]{2,1,0:T(8,128)}), f32[16,32,128]{2,1,0:T(8,128)S(1)}, u32[]{:S(2)}, u32[]{:S(2)}) async-start(f32[16,32,128]{2,1,0:T(8,128)} %shard_map.77), calls=%async_computation | async-start | bytes 524288 | tf_op jit(solution)/shard_map/all_to_all | solution.py:329
  23.2 3.7 %copy-start.3 = (f32[4,2,1024]{2,1,0:T(2,128)S(1)}, f32[4,2,1024]{2,1,0:T(2,128)}, u32[]{:S(2)}) copy-start(f32[4,2,1024]{2,1,0:T(2,128)} %param.7) | copy-start | bytes 98308
  23.2 18.5 %all-to-all-start.1 = ((f32[16,2,32,128]{3,2,1,0:T(8,128)}), f32[16,2,32,128]{3,2,1,0:T(8,128)S(1)}, u32[]{:S(2)}, u32[]{:S(2)}) async-start(f32[16,2,32,128]{3,2,1,0:T(8,128)} %shard_map.78), calls=%async_computation.1 | async-start | bytes 1048576 | tf_op jit(solution)/shard_map/all_to_all | solution.py:337
  27.1 9.5 %collective-permute-start.1 = (f32[4,16,128]{2,1,0:T(8,128)S(1)}, f32[4,16,128]{2,1,0:T(8,128)S(1)}, u32[]{:S(2)}, u32[]{:S(2)}) collective-permute-start(f32[4,16,128]{2,1,0:T(8,128)S(1)} %reshape.35.refs_5_), channel_id=1, source_target_pairs={{2,0},{4,2},{6,4},{8,6},{10,8},{12,10},{14,12},{16,14},{18,16},{20... | collective-permute-start | bytes 98312 | tf_op jit(solution)/shard_map/ppermute | solution.py:320
  31.5 10.0 %collective-permute-start = (f32[4,16,128]{2,1,0:T(8,128)S(1)}, f32[4,16,128]{2,1,0:T(8,128)S(1)}, u32[]{:S(2)}, u32[]{:S(2)}) collective-permute-start(f32[4,16,128]{2,1,0:T(8,128)S(1)} %reshape.35.refs_5_), channel_id=1, source_target_pairs={{0,2},{2,4},{4,6},{6,8},{8,10},{10,12},{12,14},{14,16},{16,18},{18... | collective-permute-start | bytes 98312 | tf_op jit(solution)/shard_map/ppermute | solution.py:319
  31.5 10.2 %copy-start.2 = (f32[3,20]{1,0:T(4,128)S(1)}, f32[3,20]{1,0:T(4,128)}, u32[]{:S(2)}) copy-start(f32[3,20]{1,0:T(4,128)} %refs_2_.3) | copy-start | bytes 724
  31.5 10.2 %copy-start.1 = (s32[3,20]{1,0:T(4,128)S(1)}, s32[3,20]{1,0:T(4,128)}, u32[]{:S(2)}) copy-start(s32[3,20]{1,0:T(4,128)} %refs_1_.4) | copy-start | bytes 724
  45.3 8.3 %collective-permute-start.2 = (f32[512,128]{1,0:T(8,128)S(1)}, f32[512,128]{1,0:T(8,128)S(1)}, u32[]{:S(2)}, u32[]{:S(2)}) collective-permute-start(f32[512,128]{1,0:T(8,128)S(1)} %get-tuple-element.16), channel_id=1, source_target_pairs={{0,1},{1,0},{2,3},{3,2},{4,5},{5,4},{6,7},{7,6},{8,9},{9,8},{10,11... | collective-permute-start | bytes 786440 | tf_op jit(solution)/shard_map/ppermute | solution.py:390
  89.6 8.3 %collective-permute-start.3 = (f32[512,128]{1,0:T(8,128)S(1)}, f32[512,128]{1,0:T(8,128)S(1)}, u32[]{:S(2)}, u32[]{:S(2)}) collective-permute-start(f32[512,128]{1,0:T(8,128)S(1)} %get-tuple-element.21), channel_id=1, source_target_pairs={{0,1},{1,0},{2,3},{3,2},{4,5},{5,4},{6,7},{7,6},{8,9},{9,8},{10,11... | collective-permute-start | bytes 786440 | tf_op jit(solution)/shard_map/ppermute | solution.py:400

commit v2 on v1

--- a/solution.py
+++ b/solution.py
@@ -106,18 +106,41 @@
     out_ref[...] = done.reshape(NL, fields, LANES)
 
 
-def first_kernel(fields, b_ref, sine_ref, out_ref):
-    forward_rows(lambda l, base: b_ref[pl.ds(base * NL + l, 8, stride=NL), :], sine_ref, out_ref, fields)
-
-
-def next_kernel(fields, b_ref, own_ref, recv_ref, sine_ref, out_ref, image_ref, work_ref):
+def deal(me_ref, all_ref, out_refs):
+    if len(out_refs) == 1:
+        out_refs[0][...] = all_ref[...]
+    else:
+        for d, ref in enumerate(out_refs):
+            ref[...] = all_ref[me_ref[0] ^ d]
+
+
+def collect(me_ref, in_refs, all_ref):
+    if len(in_refs) == 1:
+        all_ref[...] = in_refs[0][...]
+    else:
+        for d, ref in enumerate(in_refs):
+            all_ref[me_ref[0] ^ d] = ref[...]
+
+
+def first_kernel(fields, me_ref, b_ref, sine_ref, *refs):
+    *out_refs, all_ref = refs
+    forward_rows(lambda l, base: b_ref[pl.ds(base * NL + l, 8, stride=NL), :], sine_ref, all_ref, fields)
+    deal(me_ref, all_ref, out_refs)
+
+
+def next_kernel(fields, me_ref, b_ref, own_ref, recv_ref, sine_ref, *refs):
+    *out_refs, image_ref, work_ref, all_ref = refs
     image = own_ref[...] + recv_ref[...]
     image_ref[...] = image
     work_ref[...] = b_ref[...] - SHIFT * image
-    forward_rows(lambda l, base: work_ref[pl.ds(base * NL + l, 8, stride=NL), :], sine_ref, out_ref, fields)
-
-
-def circ_kernel(fields, half, x_ref, table_ref, out_ref):
+    forward_rows(lambda l, base: work_ref[pl.ds(base * NL + l, 8, stride=NL), :], sine_ref, all_ref, fields)
+    deal(me_ref, all_ref, out_refs)
+
+
+def circ_kernel(fields, half, me_ref, table_ref, *refs):
+    in_refs, out_refs = refs[:half], refs[half : 2 * half]
+    x_ref, out_ref = refs[2 * half :]
+    collect(me_ref, in_refs, x_ref)
     quarter = half // 2
     comp_row = lax.broadcasted_iota(jnp.int32, (8, LANES), 0)
     low = lax.broadcasted_iota(jnp.int32, (8, LANES), 1) < NT
@@ -153,6 +176,7 @@
         for c in range(half):
             out_ref[c, 0, base : base + 8, :] = outs[c]
             out_ref[c, 1, base : base + 8, :] = jnp.where(low, outs[(c + 1) % half], outs[c - 1])
+    deal(me_ref, out_ref, out_refs)
 
 
 def lane_masks(rows):
@@ -167,9 +191,10 @@
 
 
 def operator_kernel(
-    modes, fields, row_ref, pair_ref, coup_ref, spec_ref, sine_ref, stiff_ref, stiff_l_ref, stiff_r_ref,
-    field_ref, own_ref, cross_ref, work_ref, ends_ref, face_ref, term_ref, inv_ref
+    modes, fields, me_ref, row_ref, pair_ref, coup_ref, sine_ref, stiff_ref, stiff_l_ref, stiff_r_ref, *refs
 ):
+    *spec_refs, field_ref, own_ref, cross_ref, spec_ref, ends_ref, face_ref, term_ref, inv_ref = refs
+    collect(me_ref, spec_refs, spec_ref)
     total_modes = pair_ref.shape[1]
     low, first, last = lane_masks(NL)
     row = lax.broadcasted_iota(jnp.int32, (NL, LANES), 0)
@@ -319,32 +344,42 @@
     stiff_l = lax.ppermute(stiff, "circ", ahead)
     stiff_r = lax.ppermute(stiff, "circ", back)
     row_start = (lax.axis_index("mode") * modes).astype(jnp.int32).reshape(1)
-    me = lax.axis_index("circ").astype(jnp.int32)
+    me = lax.axis_index("circ").astype(jnp.int32).reshape(1)
 
     split = circ // NL
+    pieces = circ if split == 1 else 1
+    chunks = [struct(fields, LANES)] * circ if split == 1 else [struct(NL, fields, LANES)]
     if split == 1:
-        table = lax.dynamic_index_in_dim(jnp.asarray(circulant_table(n_circ)), me, 0, keepdims=False)
-
-        def round_trip(spec):
-            spec = lax.all_to_all(spec, "circ", split_axis=0, concat_axis=0)
-            spec = pl.pallas_call(
+        table = lax.dynamic_index_in_dim(jnp.asarray(circulant_table(n_circ)), me[0], 0, keepdims=False)
+
+        def exchange(parts):
+            return [parts[0]] + [
+                lax.ppermute(parts[d], "circ", [(i, i ^ d) for i in range(circ)]) for d in range(1, circ)
+            ]
+
+        def round_trip(parts):
+            parts = pl.pallas_call(
                 lambda *refs: circ_kernel(fields, circ, *refs),
-                out_shape=struct(circ, 2, fields, LANES),
-                in_specs=[whole()] * 2,
-                out_specs=whole(),
+                out_shape=[struct(2, fields, LANES)] * circ,
+                in_specs=[smem()] + [whole()] * (1 + circ),
+                out_specs=[whole()] * circ,
+                scratch_shapes=[
+                    pltpu.VMEM((circ, fields, LANES), f32),
+                    pltpu.VMEM((circ, 2, fields, LANES), f32),
+                ],
                 compiler_params=params(),
-            )(spec, table)
-            return lax.all_to_all(spec, "circ", split_axis=0, concat_axis=0)
+            )(me, table, *exchange(parts))
+            return exchange(parts)
 
     else:
         span = NT // split
         htab = jnp.asarray(hartley_np(n_circ), f32)
         denom = jnp.asarray(denominator_np(n_circ), f32).reshape(comps, n_circ, NL, split, span)
         denom = denom.transpose(2, 3, 0, 1, 4).reshape(circ, comps, n_circ, span)
-        denom = lax.dynamic_index_in_dim(denom, me, 0, keepdims=False)
-
-        def round_trip(spec):
-            spec = spec.reshape(NL, fields, local_circ, split, span).transpose(0, 3, 1, 2, 4)
+        denom = lax.dynamic_index_in_dim(denom, me[0], 0, keepdims=False)
+
+        def round_trip(parts):
+            spec = parts[0].reshape(NL, fields, local_circ, split, span).transpose(0, 3, 1, 2, 4)
             spec = spec.reshape(circ, fields, local_circ, span)
             spec = lax.all_to_all(spec, "circ", split_axis=0, concat_axis=0)
             spec = spec[:, : modes * comps]
@@ -359,44 +394,45 @@
             spec = jnp.stack([own[:, 0], own[:, 1], after, before], axis=1)
             spec = lax.all_to_all(spec, "circ", split_axis=0, concat_axis=0)
             spec = spec.reshape(NL, split, 2, 2, fields, span).transpose(0, 2, 4, 3, 1, 5)
-            return spec.reshape(NL, 2, fields, LANES)
-
-    def operate(spec):
+            return [spec.reshape(NL, 2, fields, LANES)]
+
+    def operate(parts):
         return pl.pallas_call(
             lambda *refs: operator_kernel(modes, fields, *refs),
             out_shape=[struct(rows, LANES)] * 3,
-            in_specs=[smem()] * 3 + [whole()] * 5,
+            in_specs=[smem()] * 4 + [whole()] * (4 + pieces),
             out_specs=[whole()] * 3,
             scratch_shapes=[
-                pltpu.VMEM((8, LANES), f32),
+                pltpu.VMEM((NL, 2, fields, LANES), f32),
                 pltpu.VMEM((rows, LANES), f32),
                 pltpu.VMEM((KM, 6, COMPS * NL, LANES), f32),
                 pltpu.VMEM((KM, modes, COMPS * NL, LANES), f32),
                 pltpu.SMEM((KM - 1, modes * mode_blocks), jnp.int32),
             ],
             compiler_params=params(),
-        )(row_start, pairing, coupling, spec, sine, stiff, stiff_l, stiff_r)
+        )(me, row_start, pairing, coupling, sine, stiff, stiff_l, stiff_r, *parts)
 
     swap = [(0, 1), (1, 0)]
 
-    spec = pl.pallas_call(
+    parts = pl.pallas_call(
         lambda *refs: first_kernel(fields, *refs),
-        out_shape=struct(NL, fields, LANES),
-        in_specs=[whole()] * 2,
-        out_specs=whole(),
+        out_shape=chunks,
+        in_specs=[smem()] + [whole()] * 2,
+        out_specs=[whole()] * pieces,
+        scratch_shapes=[pltpu.VMEM((NL, fields, LANES), f32)],
         compiler_params=params(),
-    )(b, sine)
-    u, own, cross = operate(round_trip(spec))
+    )(me, b, sine)
+    u, own, cross = operate(round_trip(parts))
     recv = lax.ppermute(cross, "mode", swap)
-    spec, v = pl.pallas_call(
+    *parts, v = pl.pallas_call(
         lambda *refs: next_kernel(fields, *refs),
-        out_shape=[struct(NL, fields, LANES), struct(rows, LANES)],
-        in_specs=[whole()] * 4,
-        out_specs=[whole()] * 2,
-        scratch_shapes=[pltpu.VMEM((rows, LANES), f32)],
+        out_shape=chunks + [struct(rows, LANES)],
+        in_specs=[smem()] + [whole()] * 4,
+        out_specs=[whole()] * (pieces + 1),
+        scratch_shapes=[pltpu.VMEM((rows, LANES), f32), pltpu.VMEM((NL, fields, LANES), f32)],
         compiler_params=params(),
-    )(b, own, recv, sine)
-    z, own, cross = operate(round_trip(spec))
+    )(me, b, own, recv, sine)
+    z, own, cross = operate(round_trip(parts))
     recv = lax.ppermute(cross, "mode", swap)
     devices = circ * mode_blocks
     q, part = pl.pallas_call(

time: 114 us -> 149 us (1.31)
  starting transfers between devices: 18.6 us -> 88.5 us
  blocking collectives: 44.1 us -> 12.6 us
  waiting for transfers between devices: 32.8 us -> 30.9 us
    ppermute x0 -> x60, starting transfers between devices: none -> 84.4 us  [exchange(): lax.ppermute(parts[d], 'circ', [(i, i ^ d) for i in range(circ)])]
    all_to_all x2 -> x0, blocking collectives: 31.4 us -> none  [the longest x1 17.2 us: round_trip(): return lax.all_to_all(spec, 'circ', split_axis=0, concat_axis=0)]
    ppermute x0 -> x60, waiting for transfers between devices: none -> 17 us  [exchange(): lax.ppermute(parts[d], 'circ', [(i, i ^ d) for i in range(circ)])]
    all_to_all x2 -> x0, starting transfers between devices: 11.1 us -> none  [the longest x1 7.38 us: round_trip(): spec = lax.all_to_all(spec, 'circ', split_axis=0, concat_axis=0)]
    all_to_all x2 -> x0, waiting for transfers between devices: 9.3 us -> none  [the longest x1 9.18 us: round_trip(): spec = lax.all_to_all(spec, 'circ', split_axis=0, concat_axis=0)]
    ppermute x1, waiting for transfers between devices: 5.13 us -> 0.01 us  [on_device(): stiff_r = lax.ppermute(stiff, 'circ', back)]
    ppermute x1, waiting for transfers between devices: 4.89 us -> 0.01 us  [on_device(): stiff_l = lax.ppermute(stiff, 'circ', ahead)]
    ppermute x1, starting transfers between devices: 4.36 us -> 0.99 us  [on_device(): stiff_r = lax.ppermute(stiff, 'circ', back)]
  transfers between devices with their start and end apart: 6 -> 64, of which waited for: 6 -> 12; matrix products, arithmetic and copies ran while one was open for 1% -> 1% of each run, Pallas kernels for 0% -> 0%
where the time goes in v2:
time: 149 us
  starting transfers between devices  88.5 us (59%)
  waiting for transfers between devices  30.9 us (21%)
  blocking collectives  12.6 us (8%)
  Pallas kernels  9.79 us (7%)
  local copies, waits for them, and re-layouts  6.33 us (4%)
    ppermute x60, starting transfers between devices, exchange(): lax.ppermute(parts[d], 'circ', [(i, i ^ d) for i in range(circ)])  84.4 us
    ppermute x60, waiting for transfers between devices, exchange(): lax.ppermute(parts[d], 'circ', [(i, i ^ d) for i in range(circ)])  17 us
    ppermute x2, waiting for transfers between devices, on_device(): recv = lax.ppermute(cross, 'mode', swap)  13.9 us
    all_to_all x1, blocking collectives, on_device(): parts = lax.all_to_all(part, ('circ', 'mode'), split_axis=0, concat_axis=0)  12.6 us
    pallas_call x2, Pallas kernels, operate(): pl.pallas_call(lambda *refs: operator_kernel(modes, fields, *refs), out_s...  7.25 us
    ppermute x2, starting transfers between devices, on_device(): recv = lax.ppermute(cross, 'mode', swap)  3.11 us
  transfers between devices with their start and end apart: 64, of which 12 were waited for; matrix products, arithmetic and copies ran while one was open for 1% of the time, Pallas kernels for 0%

profile of v2, /device:TPU:0, one launch (start us, length us, event | category | flops | bytes accessed | tf_op | source)
XLA Modules:
  0.0 149.0 jit_solution(12051529208928640337)
XLA Ops:
  4.3 2.6 %collective-permute-start.3 = (f32[32,128]{1,0:T(8,128)S(1)}, f32[32,128]{1,0:T(8,128)S(1)}, u32[]{:S(2)}, u32[]{:S(2)}) collective-permute-start(f32[32,128]{1,0:T(8,128)S(1)} %get-tuple-element.79), channel_id=1, source_target_pairs={{0,4},{2,6},{4,0},{6,2},{8,12},{10,14},{12,8},{14,10},{16,20},{18,... | collective-permute-start | bytes 49160 | tf_op jit(solution)/shard_map/ppermute | solution.py:357
  7.0 1.8 %collective-permute-start.5 = (f32[32,128]{1,0:T(8,128)S(1)}, f32[32,128]{1,0:T(8,128)S(1)}, u32[]{:S(2)}, u32[]{:S(2)}) collective-permute-start(f32[32,128]{1,0:T(8,128)S(1)} %get-tuple-element.81), channel_id=1, source_target_pairs={{0,8},{2,10},{4,12},{6,14},{8,0},{10,2},{12,4},{14,6},{16,24},{18,... | collective-permute-start | bytes 49160 | tf_op jit(solution)/shard_map/ppermute | solution.py:357
  8.8 2.6 %collective-permute-start.7 = (f32[32,128]{1,0:T(8,128)S(1)}, f32[32,128]{1,0:T(8,128)S(1)}, u32[]{:S(2)}, u32[]{:S(2)}) collective-permute-start(f32[32,128]{1,0:T(8,128)S(1)} %get-tuple-element.83), channel_id=1, source_target_pairs={{0,12},{2,14},{4,8},{6,10},{8,4},{10,6},{12,0},{14,2},{16,28},{18,... | collective-permute-start | bytes 49160 | tf_op jit(solution)/shard_map/ppermute | solution.py:357
  11.6 2.6 %collective-permute-start.9 = (f32[32,128]{1,0:T(8,128)S(1)}, f32[32,128]{1,0:T(8,128)S(1)}, u32[]{:S(2)}, u32[]{:S(2)}) collective-permute-start(f32[32,128]{1,0:T(8,128)S(1)} %get-tuple-element.85), channel_id=1, source_target_pairs={{0,16},{2,18},{4,20},{6,22},{8,24},{10,26},{12,28},{14,30},{16,0},... | collective-permute-start | bytes 49160 | tf_op jit(solution)/shard_map/ppermute | solution.py:357
  14.2 3.5 %collective-permute-start.11 = (f32[32,128]{1,0:T(8,128)S(1)}, f32[32,128]{1,0:T(8,128)S(1)}, u32[]{:S(2)}, u32[]{:S(2)}) collective-permute-start(f32[32,128]{1,0:T(8,128)S(1)} %get-tuple-element.87), channel_id=1, source_target_pairs={{0,20},{2,22},{4,16},{6,18},{8,28},{10,30},{12,24},{14,26},{16,4},... | collective-permute-start | bytes 49160 | tf_op jit(solution)/shard_map/ppermute | solution.py:357
  17.9 3.5 %collective-permute-start.13 = (f32[32,128]{1,0:T(8,128)S(1)}, f32[32,128]{1,0:T(8,128)S(1)}, u32[]{:S(2)}, u32[]{:S(2)}) collective-permute-start(f32[32,128]{1,0:T(8,128)S(1)} %get-tuple-element.89), channel_id=1, source_target_pairs={{0,24},{2,26},{4,28},{6,30},{8,16},{10,18},{12,20},{14,22},{16,8},... | collective-permute-start | bytes 49160 | tf_op jit(solution)/shard_map/ppermute | solution.py:357
  23.5 5.4 %collective-permute-start.15 = (f32[32,128]{1,0:T(8,128)S(1)}, f32[32,128]{1,0:T(8,128)S(1)}, u32[]{:S(2)}, u32[]{:S(2)}) collective-permute-start(f32[32,128]{1,0:T(8,128)S(1)} %get-tuple-element.91), channel_id=1, source_target_pairs={{0,28},{2,30},{4,24},{6,26},{8,20},{10,22},{12,16},{14,18},{16,12}... | collective-permute-start | bytes 49160 | tf_op jit(solution)/shard_map/ppermute | solution.py:357
  30.7 4.0 %collective-permute-done.16.refs_17_ = f32[32,128]{1,0:T(8,128)S(1)} collective-permute-done((f32[32,128]{1,0:T(8,128)S(1)}, f32[32,128]{1,0:T(8,128)S(1)}, u32[]{:S(2)}, u32[]{:S(2)}) %collective-permute-start.16) | collective-permute-done | bytes 16416 | tf_op jit(solution)/shard_map/ppermute | solution.py:357
  39.4 2.1 %collective-permute-start.23 = (f32[2,32,128]{2,1,0:T(8,128)S(1)}, f32[2,32,128]{2,1,0:T(8,128)S(1)}, u32[]{:S(2)}, u32[]{:S(2)}) collective-permute-start(f32[2,32,128]{2,1,0:T(8,128)S(1)} %get-tuple-element.100), channel_id=1, source_target_pairs={{0,14},{2,12},{4,10},{6,8},{8,6},{10,4},{12,2},{14,0},{16,30},{18,... | collective-permute-start | bytes 98312 | tf_op jit(solution)/shard_map/ppermute | solution.py:357
  42.3 1.9 %collective-permute-start.25 = (f32[2,32,128]{2,1,0:T(8,128)S(1)}, f32[2,32,128]{2,1,0:T(8,128)S(1)}, u32[]{:S(2)}, u32[]{:S(2)}) collective-permute-start(f32[2,32,128]{2,1,0:T(8,128)S(1)} %get-tuple-element.102), channel_id=1, source_target_pairs={{0,18},{2,16},{4,22},{6,20},{8,26},{10,24},{12,30},{14,28},{16,2},... | collective-permute-start | bytes 98312 | tf_op jit(solution)/shard_map/ppermute | solution.py:357
  45.4 2.4 %collective-permute-start.27 = (f32[2,32,128]{2,1,0:T(8,128)S(1)}, f32[2,32,128]{2,1,0:T(8,128)S(1)}, u32[]{:S(2)}, u32[]{:S(2)}) collective-permute-start(f32[2,32,128]{2,1,0:T(8,128)S(1)} %get-tuple-element.104), channel_id=1, source_target_pairs={{0,22},{2,20},{4,18},{6,16},{8,30},{10,28},{12,26},{14,24},{16,6},... | collective-permute-start | bytes 98312 | tf_op jit(solution)/shard_map/ppermute | solution.py:357
  47.8 2.1 %collective-permute-start.28 = (f32[2,32,128]{2,1,0:T(8,128)S(1)}, f32[2,32,128]{2,1,0:T(8,128)S(1)}, u32[]{:S(2)}, u32[]{:S(2)}) collective-permute-start(f32[2,32,128]{2,1,0:T(8,128)S(1)} %get-tuple-element.105), channel_id=1, source_target_pairs={{0,24},{2,26},{4,28},{6,30},{8,16},{10,18},{12,20},{14,22},{16,8},... | collective-permute-start | bytes 98312 | tf_op jit(solution)/shard_map/ppermute | solution.py:357
  52.9 2.8 %collective-permute-start.31 = (f32[2,32,128]{2,1,0:T(8,128)S(1)}, f32[2,32,128]{2,1,0:T(8,128)S(1)}, u32[]{:S(2)}, u32[]{:S(2)}) collective-permute-start(f32[2,32,128]{2,1,0:T(8,128)S(1)} %get-tuple-element.108), channel_id=1, source_target_pairs={{0,30},{2,28},{4,26},{6,24},{8,22},{10,20},{12,18},{14,16},{16,14}... | collective-permute-start | bytes 98312 | tf_op jit(solution)/shard_map/ppermute | solution.py:357
  55.8 2.1 %collective-permute-done.30.refs_22_ = f32[2,32,128]{2,1,0:T(8,128)S(1)} collective-permute-done((f32[2,32,128]{2,1,0:T(8,128)S(1)}, f32[2,32,128]{2,1,0:T(8,128)S(1)}, u32[]{:S(2)}, u32[]{:S(2)}) %collective-permute-start.30) | collective-permute-done | bytes 32800 | tf_op jit(solution)/shard_map/ppermute | solution.py:357
  59.0 3.6 %shard_map.79 = (f32[512,128]{1,0:T(8,128)S(1)}, f32[512,128]{1,0:T(8,128)S(1)}, f32[512,128]{1,0:T(8,128)S(1)}) custom-call(s32[1]{0:T(128)} %bitcast.1.refs_0_, s32[1]{0:T(128)} %bitcast.2.refs_1_, s32[3,20]{1,0:T(4,128)S(1)} %copy-done.1, f32[3,20]{1,0:T(4,128)S(1)} %copy-done.2, f32[128,128]{1,0:T(8,128)S(1)} %copy-done, ...), custom_call_target="tpu_custom_call" | custom-call | tf_op jit(solution)/shard_map/pallas_call | solution.py:400
  64.2 7.1 %collective-permute-done.32.refs_3_ = f32[512,128]{1,0:T(8,128)S(1)} collective-permute-done((f32[512,128]{1,0:T(8,128)S(1)}, f32[512,128]{1,0:T(8,128)S(1)}, u32[]{:S(2)}, u32[]{:S(2)}) %collective-permute-start.32) | collective-permute-done | bytes 262176 | tf_op jit(solution)/shard_map/ppermute | solution.py:426
  71.9 1.8 %collective-permute-start.34 = (f32[32,128]{1,0:T(8,128)S(1)}, f32[32,128]{1,0:T(8,128)S(1)}, u32[]{:S(2)}, u32[]{:S(2)}) collective-permute-start(f32[32,128]{1,0:T(8,128)S(1)} %get-tuple-element.115), channel_id=1, source_target_pairs={{0,4},{2,6},{4,0},{6,2},{8,12},{10,14},{12,8},{14,10},{16,20},{18,... | collective-permute-start | bytes 49160 | tf_op jit(solution)/shard_map/ppermute | solution.py:357
  82.6 1.8 %collective-permute-start.43 = (f32[32,128]{1,0:T(8,128)S(1)}, f32[32,128]{1,0:T(8,128)S(1)}, u32[]{:S(2)}, u32[]{:S(2)}) collective-permute-start(f32[32,128]{1,0:T(8,128)S(1)} %get-tuple-element.124), channel_id=1, source_target_pairs={{0,22},{2,20},{4,18},{6,16},{8,30},{10,28},{12,26},{14,24},{16,6},... | collective-permute-start | bytes 49160 | tf_op jit(solution)/shard_map/ppermute | solution.py:357
  87.9 2.9 %collective-permute-start.46 = (f32[32,128]{1,0:T(8,128)S(1)}, f32[32,128]{1,0:T(8,128)S(1)}, u32[]{:S(2)}, u32[]{:S(2)}) collective-permute-start(f32[32,128]{1,0:T(8,128)S(1)} %get-tuple-element.127), channel_id=1, source_target_pairs={{0,28},{2,30},{4,24},{6,26},{8,20},{10,22},{12,16},{14,18},{16,12}... | collective-permute-start | bytes 49160 | tf_op jit(solution)/shard_map/ppermute | solution.py:357
  92.4 1.9 %collective-permute-done.46.refs_16_ = f32[32,128]{1,0:T(8,128)S(1)} collective-permute-done((f32[32,128]{1,0:T(8,128)S(1)}, f32[32,128]{1,0:T(8,128)S(1)}, u32[]{:S(2)}, u32[]{:S(2)}) %collective-permute-start.46) | collective-permute-done | bytes 16416 | tf_op jit(solution)/shard_map/ppermute | solution.py:357
  94.3 2.3 %collective-permute-done.47.refs_17_ = f32[32,128]{1,0:T(8,128)S(1)} collective-permute-done((f32[32,128]{1,0:T(8,128)S(1)}, f32[32,128]{1,0:T(8,128)S(1)}, u32[]{:S(2)}, u32[]{:S(2)}) %collective-permute-start.47) | collective-permute-done | bytes 16416 | tf_op jit(solution)/shard_map/ppermute | solution.py:357
  99.1 1.8 %collective-permute-start.52 = (f32[2,32,128]{2,1,0:T(8,128)S(1)}, f32[2,32,128]{2,1,0:T(8,128)S(1)}, u32[]{:S(2)}, u32[]{:S(2)}) collective-permute-start(f32[2,32,128]{2,1,0:T(8,128)S(1)} %get-tuple-element.134), channel_id=1, source_target_pairs={{0,10},{2,8},{4,14},{6,12},{8,2},{10,0},{12,6},{14,4},{16,26},{18,... | collective-permute-start | bytes 98312 | tf_op jit(solution)/shard_map/ppermute | solution.py:357
  101.4 2.1 %collective-permute-start.54 = (f32[2,32,128]{2,1,0:T(8,128)S(1)}, f32[2,32,128]{2,1,0:T(8,128)S(1)}, u32[]{:S(2)}, u32[]{:S(2)}) collective-permute-start(f32[2,32,128]{2,1,0:T(8,128)S(1)} %get-tuple-element.136), channel_id=1, source_target_pairs={{0,14},{2,12},{4,10},{6,8},{8,6},{10,4},{12,2},{14,0},{16,30},{18,... | collective-permute-start | bytes 98312 | tf_op jit(solution)/shard_map/ppermute | solution.py:357
  104.2 2.0 %collective-permute-start.56 = (f32[2,32,128]{2,1,0:T(8,128)S(1)}, f32[2,32,128]{2,1,0:T(8,128)S(1)}, u32[]{:S(2)}, u32[]{:S(2)}) collective-permute-start(f32[2,32,128]{2,1,0:T(8,128)S(1)} %get-tuple-element.138), channel_id=1, source_target_pairs={{0,18},{2,16},{4,22},{6,20},{8,26},{10,24},{12,30},{14,28},{16,2},... | collective-permute-start | bytes 98312 | tf_op jit(solution)/shard_map/ppermute | solution.py:357
  107.3 2.3 %collective-permute-start.58 = (f32[2,32,128]{2,1,0:T(8,128)S(1)}, f32[2,32,128]{2,1,0:T(8,128)S(1)}, u32[]{:S(2)}, u32[]{:S(2)}) collective-permute-start(f32[2,32,128]{2,1,0:T(8,128)S(1)} %get-tuple-element.140), channel_id=1, source_target_pairs={{0,22},{2,20},{4,18},{6,16},{8,30},{10,28},{12,26},{14,24},{16,6},... | collective-permute-start | bytes 98312 | tf_op jit(solution)/shard_map/ppermute | solution.py:357
  109.7 2.1 %collective-permute-start.59 = (f32[2,32,128]{2,1,0:T(8,128)S(1)}, f32[2,32,128]{2,1,0:T(8,128)S(1)}, u32[]{:S(2)}, u32[]{:S(2)}) collective-permute-start(f32[2,32,128]{2,1,0:T(8,128)S(1)} %get-tuple-element.141), channel_id=1, source_target_pairs={{0,24},{2,26},{4,28},{6,30},{8,16},{10,18},{12,20},{14,22},{16,8},... | collective-permute-start | bytes 98312 | tf_op jit(solution)/shard_map/ppermute | solution.py:357
  113.3 1.9 %collective-permute-start.61 = (f32[2,32,128]{2,1,0:T(8,128)S(1)}, f32[2,32,128]{2,1,0:T(8,128)S(1)}, u32[]{:S(2)}, u32[]{:S(2)}) collective-permute-start(f32[2,32,128]{2,1,0:T(8,128)S(1)} %get-tuple-element.143), channel_id=1, source_target_pairs={{0,28},{2,30},{4,24},{6,26},{8,20},{10,22},{12,16},{14,18},{16,12}... | collective-permute-start | bytes 98312 | tf_op jit(solution)/shard_map/ppermute | solution.py:357
  115.2 2.5 %collective-permute-start.62 = (f32[2,32,128]{2,1,0:T(8,128)S(1)}, f32[2,32,128]{2,1,0:T(8,128)S(1)}, u32[]{:S(2)}, u32[]{:S(2)}) collective-permute-start(f32[2,32,128]{2,1,0:T(8,128)S(1)} %get-tuple-element.144), channel_id=1, source_target_pairs={{0,30},{2,28},{4,26},{6,24},{8,22},{10,20},{12,18},{14,16},{16,14}... | collective-permute-start | bytes 98312 | tf_op jit(solution)/shard_map/ppermute | solution.py:357
  117.7 2.2 %collective-permute-done.61.refs_22_ = f32[2,32,128]{2,1,0:T(8,128)S(1)} collective-permute-done((f32[2,32,128]{2,1,0:T(8,128)S(1)}, f32[2,32,128]{2,1,0:T(8,128)S(1)}, u32[]{:S(2)}, u32[]{:S(2)}) %collective-permute-start.61) | collective-permute-done | bytes 32800 | tf_op jit(solution)/shard_map/ppermute | solution.py:357
  121.3 3.6 %shard_map.82 = (f32[512,128]{1,0:T(8,128)S(1)}, f32[512,128]{1,0:T(8,128)S(1)}, f32[512,128]{1,0:T(8,128)S(1)}) custom-call(s32[1]{0:T(128)} %bitcast.1.refs_0_, s32[1]{0:T(128)} %bitcast.2.refs_1_, s32[3,20]{1,0:T(4,128)S(1)} %copy-done.1, f32[3,20]{1,0:T(4,128)S(1)} %copy-done.2, f32[128,128]{1,0:T(8,128)S(1)} %copy-done, ...), custom_call_target="tpu_custom_call" | custom-call | tf_op jit(solution)/shard_map/pallas_call | solution.py:400
  126.5 6.8 %collective-permute-done.63.refs_5_ = f32[512,128]{1,0:T(8,128)S(1)} collective-permute-done((f32[512,128]{1,0:T(8,128)S(1)}, f32[512,128]{1,0:T(8,128)S(1)}, u32[]{:S(2)}, u32[]{:S(2)}) %collective-permute-start.63) | collective-permute-done | bytes 262176 | tf_op jit(solution)/shard_map/ppermute | solution.py:436
  133.5 12.6 %all_to_all.5.parts_ref = f32[32,8,128]{2,1,0:T(8,128)S(1)} all-to-all(f32[32,8,128]{2,1,0:T(8,128)S(1)} %get-tuple-element.148), channel_id=1, replica_groups=mesh['circ'=16,'mode'=2] {'circ','mode'}, dimensions={0} | all-to-all | bytes 262144 | tf_op jit(solution)/shard_map/all_to_all | solution.py:445
  (129 shorter events, 47.3 us)
Async XLA Ops:
  4.3 7.1 %collective-permute-start.3 = (f32[32,128]{1,0:T(8,128)S(1)}, f32[32,128]{1,0:T(8,128)S(1)}, u32[]{:S(2)}, u32[]{:S(2)}) collective-permute-start(f32[32,128]{1,0:T(8,128)S(1)} %get-tuple-element.79), channel_id=1, source_target_pairs={{0,4},{2,6},{4,0},{6,2},{8,12},{10,14},{12,8},{14,10},{16,20},{18,... | collective-permute-start | bytes 49160 | tf_op jit(solution)/shard_map/ppermute | solution.py:357
  7.0 7.2 %collective-permute-start.5 = (f32[32,128]{1,0:T(8,128)S(1)}, f32[32,128]{1,0:T(8,128)S(1)}, u32[]{:S(2)}, u32[]{:S(2)}) collective-permute-start(f32[32,128]{1,0:T(8,128)S(1)} %get-tuple-element.81), channel_id=1, source_target_pairs={{0,8},{2,10},{4,12},{6,14},{8,0},{10,2},{12,4},{14,6},{16,24},{18,... | collective-permute-start | bytes 49160 | tf_op jit(solution)/shard_map/ppermute | solution.py:357
  8.8 9.0 %collective-permute-start.7 = (f32[32,128]{1,0:T(8,128)S(1)}, f32[32,128]{1,0:T(8,128)S(1)}, u32[]{:S(2)}, u32[]{:S(2)}) collective-permute-start(f32[32,128]{1,0:T(8,128)S(1)} %get-tuple-element.83), channel_id=1, source_target_pairs={{0,12},{2,14},{4,8},{6,10},{8,4},{10,6},{12,0},{14,2},{16,28},{18,... | collective-permute-start | bytes 49160 | tf_op jit(solution)/shard_map/ppermute | solution.py:357
  11.6 10.1 %collective-permute-start.9 = (f32[32,128]{1,0:T(8,128)S(1)}, f32[32,128]{1,0:T(8,128)S(1)}, u32[]{:S(2)}, u32[]{:S(2)}) collective-permute-start(f32[32,128]{1,0:T(8,128)S(1)} %get-tuple-element.85), channel_id=1, source_target_pairs={{0,16},{2,18},{4,20},{6,22},{8,24},{10,26},{12,28},{14,30},{16,0},... | collective-permute-start | bytes 49160 | tf_op jit(solution)/shard_map/ppermute | solution.py:357
  14.2 8.5 %collective-permute-start.10 = (f32[32,128]{1,0:T(8,128)S(1)}, f32[32,128]{1,0:T(8,128)S(1)}, u32[]{:S(2)}, u32[]{:S(2)}) collective-permute-start(f32[32,128]{1,0:T(8,128)S(1)} %get-tuple-element.86), channel_id=1, source_target_pairs={{0,18},{2,16},{4,22},{6,20},{8,26},{10,24},{12,30},{14,28},{16,2},... | collective-permute-start | bytes 49160 | tf_op jit(solution)/shard_map/ppermute | solution.py:357
  14.2 8.4 %collective-permute-start.11 = (f32[32,128]{1,0:T(8,128)S(1)}, f32[32,128]{1,0:T(8,128)S(1)}, u32[]{:S(2)}, u32[]{:S(2)}) collective-permute-start(f32[32,128]{1,0:T(8,128)S(1)} %get-tuple-element.87), channel_id=1, source_target_pairs={{0,20},{2,22},{4,16},{6,18},{8,28},{10,30},{12,24},{14,26},{16,4},... | collective-permute-start | bytes 49160 | tf_op jit(solution)/shard_map/ppermute | solution.py:357
  17.9 10.9 %collective-permute-start.13 = (f32[32,128]{1,0:T(8,128)S(1)}, f32[32,128]{1,0:T(8,128)S(1)}, u32[]{:S(2)}, u32[]{:S(2)}) collective-permute-start(f32[32,128]{1,0:T(8,128)S(1)} %get-tuple-element.89), channel_id=1, source_target_pairs={{0,24},{2,26},{4,28},{6,30},{8,16},{10,18},{12,20},{14,22},{16,8},... | collective-permute-start | bytes 49160 | tf_op jit(solution)/shard_map/ppermute | solution.py:357
  21.7 15.5 %collective-permute-start.1 = (f32[4,16,128]{2,1,0:T(8,128)S(1)}, f32[4,16,128]{2,1,0:T(8,128)S(1)}, u32[]{:S(2)}, u32[]{:S(2)}) collective-permute-start(f32[4,16,128]{2,1,0:T(8,128)S(1)} %reshape.39.refs_5_), channel_id=1, source_target_pairs={{2,0},{4,2},{6,4},{8,6},{10,8},{12,10},{14,12},{16,14},{18,16},{20... | collective-permute-start | bytes 98312 | tf_op jit(solution)/shard_map/ppermute | solution.py:345
  22.7 14.5 %collective-permute-start = (f32[4,16,128]{2,1,0:T(8,128)S(1)}, f32[4,16,128]{2,1,0:T(8,128)S(1)}, u32[]{:S(2)}, u32[]{:S(2)}) collective-permute-start(f32[4,16,128]{2,1,0:T(8,128)S(1)} %reshape.39.refs_5_), channel_id=1, source_target_pairs={{0,2},{2,4},{4,6},{6,8},{8,10},{10,12},{12,14},{14,16},{16,18},{18... | collective-permute-start | bytes 98312 | tf_op jit(solution)/shard_map/ppermute | solution.py:344
  23.5 7.3 %collective-permute-start.15 = (f32[32,128]{1,0:T(8,128)S(1)}, f32[32,128]{1,0:T(8,128)S(1)}, u32[]{:S(2)}, u32[]{:S(2)}) collective-permute-start(f32[32,128]{1,0:T(8,128)S(1)} %get-tuple-element.91), channel_id=1, source_target_pairs={{0,28},{2,30},{4,24},{6,26},{8,20},{10,22},{12,16},{14,18},{16,12}... | collective-permute-start | bytes 49160 | tf_op jit(solution)/shard_map/ppermute | solution.py:357
  39.4 8.3 %collective-permute-start.23 = (f32[2,32,128]{2,1,0:T(8,128)S(1)}, f32[2,32,128]{2,1,0:T(8,128)S(1)}, u32[]{:S(2)}, u32[]{:S(2)}) collective-permute-start(f32[2,32,128]{2,1,0:T(8,128)S(1)} %get-tuple-element.100), channel_id=1, source_target_pairs={{0,14},{2,12},{4,10},{6,8},{8,6},{10,4},{12,2},{14,0},{16,30},{18,... | collective-permute-start | bytes 98312 | tf_op jit(solution)/shard_map/ppermute | solution.py:357
  41.6 8.3 %collective-permute-start.24 = (f32[2,32,128]{2,1,0:T(8,128)S(1)}, f32[2,32,128]{2,1,0:T(8,128)S(1)}, u32[]{:S(2)}, u32[]{:S(2)}) collective-permute-start(f32[2,32,128]{2,1,0:T(8,128)S(1)} %get-tuple-element.101), channel_id=1, source_target_pairs={{0,16},{2,18},{4,20},{6,22},{8,24},{10,26},{12,28},{14,30},{16,0},... | collective-permute-start | bytes 98312 | tf_op jit(solution)/shard_map/ppermute | solution.py:357
  42.3 9.0 %collective-permute-start.25 = (f32[2,32,128]{2,1,0:T(8,128)S(1)}, f32[2,32,128]{2,1,0:T(8,128)S(1)}, u32[]{:S(2)}, u32[]{:S(2)}) collective-permute-start(f32[2,32,128]{2,1,0:T(8,128)S(1)} %get-tuple-element.102), channel_id=1, source_target_pairs={{0,18},{2,16},{4,22},{6,20},{8,26},{10,24},{12,30},{14,28},{16,2},... | collective-permute-start | bytes 98312 | tf_op jit(solution)/shard_map/ppermute | solution.py:357
  44.2 8.8 %collective-permute-start.26 = (f32[2,32,128]{2,1,0:T(8,128)S(1)}, f32[2,32,128]{2,1,0:T(8,128)S(1)}, u32[]{:S(2)}, u32[]{:S(2)}) collective-permute-start(f32[2,32,128]{2,1,0:T(8,128)S(1)} %get-tuple-element.103), channel_id=1, source_target_pairs={{0,20},{2,22},{4,16},{6,18},{8,28},{10,30},{12,24},{14,26},{16,4},... | collective-permute-start | bytes 98312 | tf_op jit(solution)/shard_map/ppermute | solution.py:357
  45.4 10.4 %collective-permute-start.27 = (f32[2,32,128]{2,1,0:T(8,128)S(1)}, f32[2,32,128]{2,1,0:T(8,128)S(1)}, u32[]{:S(2)}, u32[]{:S(2)}) collective-permute-start(f32[2,32,128]{2,1,0:T(8,128)S(1)} %get-tuple-element.104), channel_id=1, source_target_pairs={{0,22},{2,20},{4,18},{6,16},{8,30},{10,28},{12,26},{14,24},{16,6},... | collective-permute-start | bytes 98312 | tf_op jit(solution)/shard_map/ppermute | solution.py:357
  47.8 8.0 %collective-permute-start.28 = (f32[2,32,128]{2,1,0:T(8,128)S(1)}, f32[2,32,128]{2,1,0:T(8,128)S(1)}, u32[]{:S(2)}, u32[]{:S(2)}) collective-permute-start(f32[2,32,128]{2,1,0:T(8,128)S(1)} %get-tuple-element.105), channel_id=1, source_target_pairs={{0,24},{2,26},{4,28},{6,30},{8,16},{10,18},{12,20},{14,22},{16,8},... | collective-permute-start | bytes 98312 | tf_op jit(solution)/shard_map/ppermute | solution.py:357
  62.6 8.6 %collective-permute-start.32 = (f32[512,128]{1,0:T(8,128)S(1)}, f32[512,128]{1,0:T(8,128)S(1)}, u32[]{:S(2)}, u32[]{:S(2)}) collective-permute-start(f32[512,128]{1,0:T(8,128)S(1)} %get-tuple-element.111), channel_id=1, source_target_pairs={{0,1},{1,0},{2,3},{3,2},{4,5},{5,4},{6,7},{7,6},{8,9},{9,8},{10,11... | collective-permute-start | bytes 786440 | tf_op jit(solution)/shard_map/ppermute | solution.py:426
  75.5 7.1 %collective-permute-start.38 = (f32[32,128]{1,0:T(8,128)S(1)}, f32[32,128]{1,0:T(8,128)S(1)}, u32[]{:S(2)}, u32[]{:S(2)}) collective-permute-start(f32[32,128]{1,0:T(8,128)S(1)} %get-tuple-element.119), channel_id=1, source_target_pairs={{0,12},{2,14},{4,8},{6,10},{8,4},{10,6},{12,0},{14,2},{16,28},{18,... | collective-permute-start | bytes 49160 | tf_op jit(solution)/shard_map/ppermute | solution.py:357
  77.0 7.4 %collective-permute-start.39 = (f32[32,128]{1,0:T(8,128)S(1)}, f32[32,128]{1,0:T(8,128)S(1)}, u32[]{:S(2)}, u32[]{:S(2)}) collective-permute-start(f32[32,128]{1,0:T(8,128)S(1)} %get-tuple-element.120), channel_id=1, source_target_pairs={{0,14},{2,12},{4,10},{6,8},{8,6},{10,4},{12,2},{14,0},{16,30},{18,... | collective-permute-start | bytes 49160 | tf_op jit(solution)/shard_map/ppermute | solution.py:357
  78.2 7.9 %collective-permute-start.40 = (f32[32,128]{1,0:T(8,128)S(1)}, f32[32,128]{1,0:T(8,128)S(1)}, u32[]{:S(2)}, u32[]{:S(2)}) collective-permute-start(f32[32,128]{1,0:T(8,128)S(1)} %get-tuple-element.121), channel_id=1, source_target_pairs={{0,16},{2,18},{4,20},{6,22},{8,24},{10,26},{12,28},{14,30},{16,0},... | collective-permute-start | bytes 49160 | tf_op jit(solution)/shard_map/ppermute | solution.py:357
  79.1 8.8 %collective-permute-start.41 = (f32[32,128]{1,0:T(8,128)S(1)}, f32[32,128]{1,0:T(8,128)S(1)}, u32[]{:S(2)}, u32[]{:S(2)}) collective-permute-start(f32[32,128]{1,0:T(8,128)S(1)} %get-tuple-element.122), channel_id=1, source_target_pairs={{0,18},{2,16},{4,22},{6,20},{8,26},{10,24},{12,30},{14,28},{16,2},... | collective-permute-start | bytes 49160 | tf_op jit(solution)/shard_map/ppermute | solution.py:357
  80.8 10.0 %collective-permute-start.42 = (f32[32,128]{1,0:T(8,128)S(1)}, f32[32,128]{1,0:T(8,128)S(1)}, u32[]{:S(2)}, u32[]{:S(2)}) collective-permute-start(f32[32,128]{1,0:T(8,128)S(1)} %get-tuple-element.123), channel_id=1, source_target_pairs={{0,20},{2,22},{4,16},{6,18},{8,28},{10,30},{12,24},{14,26},{16,4},... | collective-permute-start | bytes 49160 | tf_op jit(solution)/shard_map/ppermute | solution.py:357
  82.6 9.9 %collective-permute-start.43 = (f32[32,128]{1,0:T(8,128)S(1)}, f32[32,128]{1,0:T(8,128)S(1)}, u32[]{:S(2)}, u32[]{:S(2)}) collective-permute-start(f32[32,128]{1,0:T(8,128)S(1)} %get-tuple-element.124), channel_id=1, source_target_pairs={{0,22},{2,20},{4,18},{6,16},{8,30},{10,28},{12,26},{14,24},{16,6},... | collective-permute-start | bytes 49160 | tf_op jit(solution)/shard_map/ppermute | solution.py:357
  84.4 8.0 %collective-permute-start.44 = (f32[32,128]{1,0:T(8,128)S(1)}, f32[32,128]{1,0:T(8,128)S(1)}, u32[]{:S(2)}, u32[]{:S(2)}) collective-permute-start(f32[32,128]{1,0:T(8,128)S(1)} %get-tuple-element.125), channel_id=1, source_target_pairs={{0,24},{2,26},{4,28},{6,30},{8,16},{10,18},{12,20},{14,22},{16,8},... | collective-permute-start | bytes 49160 | tf_op jit(solution)/shard_map/ppermute | solution.py:357
  99.1 7.1 %collective-permute-start.52 = (f32[2,32,128]{2,1,0:T(8,128)S(1)}, f32[2,32,128]{2,1,0:T(8,128)S(1)}, u32[]{:S(2)}, u32[]{:S(2)}) collective-permute-start(f32[2,32,128]{2,1,0:T(8,128)S(1)} %get-tuple-element.134), channel_id=1, source_target_pairs={{0,10},{2,8},{4,14},{6,12},{8,2},{10,0},{12,6},{14,4},{16,26},{18,... | collective-permute-start | bytes 98312 | tf_op jit(solution)/shard_map/ppermute | solution.py:357
  101.4 8.3 %collective-permute-start.54 = (f32[2,32,128]{2,1,0:T(8,128)S(1)}, f32[2,32,128]{2,1,0:T(8,128)S(1)}, u32[]{:S(2)}, u32[]{:S(2)}) collective-permute-start(f32[2,32,128]{2,1,0:T(8,128)S(1)} %get-tuple-element.136), channel_id=1, source_target_pairs={{0,14},{2,12},{4,10},{6,8},{8,6},{10,4},{12,2},{14,0},{16,30},{18,... | collective-permute-start | bytes 98312 | tf_op jit(solution)/shard_map/ppermute | solution.py:357
  103.5 8.3 %collective-permute-start.55 = (f32[2,32,128]{2,1,0:T(8,128)S(1)}, f32[2,32,128]{2,1,0:T(8,128)S(1)}, u32[]{:S(2)}, u32[]{:S(2)}) collective-permute-start(f32[2,32,128]{2,1,0:T(8,128)S(1)} %get-tuple-element.137), channel_id=1, source_target_pairs={{0,16},{2,18},{4,20},{6,22},{8,24},{10,26},{12,28},{14,30},{16,0},... | collective-permute-start | bytes 98312 | tf_op jit(solution)/shard_map/ppermute | solution.py:357
  104.2 9.1 %collective-permute-start.56 = (f32[2,32,128]{2,1,0:T(8,128)S(1)}, f32[2,32,128]{2,1,0:T(8,128)S(1)}, u32[]{:S(2)}, u32[]{:S(2)}) collective-permute-start(f32[2,32,128]{2,1,0:T(8,128)S(1)} %get-tuple-element.138), channel_id=1, source_target_pairs={{0,18},{2,16},{4,22},{6,20},{8,26},{10,24},{12,30},{14,28},{16,2},... | collective-permute-start | bytes 98312 | tf_op jit(solution)/shard_map/ppermute | solution.py:357
  106.2 9.0 %collective-permute-start.57 = (f32[2,32,128]{2,1,0:T(8,128)S(1)}, f32[2,32,128]{2,1,0:T(8,128)S(1)}, u32[]{:S(2)}, u32[]{:S(2)}) collective-permute-start(f32[2,32,128]{2,1,0:T(8,128)S(1)} %get-tuple-element.139), channel_id=1, source_target_pairs={{0,20},{2,22},{4,16},{6,18},{8,28},{10,30},{12,24},{14,26},{16,4},... | collective-permute-start | bytes 98312 | tf_op jit(solution)/shard_map/ppermute | solution.py:357
  107.3 10.3 %collective-permute-start.58 = (f32[2,32,128]{2,1,0:T(8,128)S(1)}, f32[2,32,128]{2,1,0:T(8,128)S(1)}, u32[]{:S(2)}, u32[]{:S(2)}) collective-permute-start(f32[2,32,128]{2,1,0:T(8,128)S(1)} %get-tuple-element.140), channel_id=1, source_target_pairs={{0,22},{2,20},{4,18},{6,16},{8,30},{10,28},{12,26},{14,24},{16,6},... | collective-permute-start | bytes 98312 | tf_op jit(solution)/shard_map/ppermute | solution.py:357
  109.7 8.0 %collective-permute-start.59 = (f32[2,32,128]{2,1,0:T(8,128)S(1)}, f32[2,32,128]{2,1,0:T(8,128)S(1)}, u32[]{:S(2)}, u32[]{:S(2)}) collective-permute-start(f32[2,32,128]{2,1,0:T(8,128)S(1)} %get-tuple-element.141), channel_id=1, source_target_pairs={{0,24},{2,26},{4,28},{6,30},{8,16},{10,18},{12,20},{14,22},{16,8},... | collective-permute-start | bytes 98312 | tf_op jit(solution)/shard_map/ppermute | solution.py:357
  125.0 8.4 %collective-permute-start.63 = (f32[512,128]{1,0:T(8,128)S(1)}, f32[512,128]{1,0:T(8,128)S(1)}, u32[]{:S(2)}, u32[]{:S(2)}) collective-permute-start(f32[512,128]{1,0:T(8,128)S(1)} %get-tuple-element.147), channel_id=1, source_target_pairs={{0,1},{1,0},{2,3},{3,2},{4,5},{5,4},{6,7},{7,6},{8,9},{9,8},{10,11... | collective-permute-start | bytes 786440 | tf_op jit(solution)/shard_map/ppermute | solution.py:436
  (36 other events, 204.5 us)

commit v3 on v1

--- a/solution.py
+++ b/solution.py
@@ -1,3 +1,4 @@
+import functools
 import math
 
 import jax
@@ -32,21 +33,6 @@
     return np.sin(math.pi * t[:, None] * t[None, :] / (NT + 1))
 
 
-def hartley_np(size):
-    n = np.arange(size)
-    angle = 2.0 * math.pi / size * (n[:, None] * n[None, :] % size)
-    return np.cos(angle) + np.sin(angle)
-
-
-def denominator_np(n_circ):
-    lam_c = 2.0 - 2.0 * np.cos(2.0 * math.pi / n_circ * np.arange(n_circ))[:, None, None]
-    lam_l = 2.0 - 2.0 * np.cos(math.pi / NL * np.arange(NL))[None, :, None]
-    lam_t = 2.0 - 2.0 * np.cos(math.pi / (NT + 1) * (np.arange(NT) + 1))[None, None, :]
-    norm = np.where(np.arange(NL) == 0, 1.0 * NL, 0.5 * NL)[None, :, None]
-    rows = [weight(c, 0) * lam_c + weight(c, 1) * lam_l + weight(c, 2) * lam_t for c in range(COMPS)]
-    return np.stack(rows) * (n_circ * norm * (0.5 * (NT + 1)))
-
-
 COS = cosine_np()
 
 
@@ -57,23 +43,47 @@
     return both.astype(np.float32)
 
 
-def circulant_table(n_circ):
-    half = n_circ // 2
-    quarter = half // 2
-    freq = np.arange(n_circ)
-    inverse = 1.0 / denominator_np(n_circ)
-    turn = np.cos(2.0 * math.pi / n_circ * (freq[:, None] * freq[None, :] % n_circ))
-    g = np.einsum("dk,ckms->dcms", turn, inverse)
-    same = np.stack([np.concatenate([g[2 * d], g[2 * d]], -1) for d in range(half)])
-    cross = np.stack(
-        [np.concatenate([g[(2 * d - 1) % n_circ], g[(2 * d + 1) % n_circ]], -1) for d in range(half)]
-    )
-    parts = []
-    for full in (same, cross):
-        parts.append(0.5 * (full[:quarter] + full[quarter:]))
-        parts.append(0.5 * (full[:quarter] - full[quarter:]))
-    table = np.stack(parts)
-    return np.transpose(table, (3, 0, 1, 2, 4)).astype(np.float32)
+def root_np():
+    lam_l = 2.0 - 2.0 * np.cos(math.pi / NL * np.arange(NL))[:, None]
+    lam_t = 2.0 - 2.0 * np.cos(math.pi / (NT + 1) * (np.arange(NT) + 1))[None, :]
+    norm = np.where(np.arange(NL) == 0, 1.0 * NL, 0.5 * NL)[:, None] * (0.5 * (NT + 1))
+    roots, scales = [], []
+    for c in range(COMPS):
+        w = weight(c, 0)
+        half = 1.0 + (weight(c, 1) * lam_l + weight(c, 2) * lam_t) / (2.0 * w)
+        big = half + np.sqrt(half * half - 1.0)
+        roots.append(1.0 / big)
+        scales.append(1.0 / (w * (big - 1.0 / big) * norm))
+    return np.stack(roots), np.stack(scales)
+
+
+def by_core(table):
+    table = np.moveaxis(table, -2, -3)
+    lead = table.shape[:-3]
+    table = table.reshape(lead + (2, NL // 2) + table.shape[-2:])
+    return np.moveaxis(table, len(lead), 0).astype(np.float32)
+
+
+def power_table(n_circ):
+    root, _ = root_np()
+    powers = root[None] ** np.arange(n_circ - 6)[:, None, None, None]
+    return by_core(np.concatenate([powers, powers], -1))
+
+
+def cell_table(n_circ):
+    root, scale = root_np()
+    scale = scale / (1.0 - root**n_circ)
+
+    def kernel(d):
+        return scale * (root ** abs(d) + root ** (n_circ - abs(d)))
+
+    out = []
+    for low, high in ((0, 1), (2, 3), (4, -1)):
+        for first, second in ((0, 1), (1, 0), (2, 3), (3, 2)):
+            out.append(np.concatenate([kernel(low - first), kernel(high - second)], -1))
+        out.append(np.concatenate([scale * root ** (3.0 - low), scale * root ** float(high)], -1))
+        out.append(np.concatenate([scale * root ** float(low), scale * root ** (3.0 - high)], -1))
+    return by_core(np.stack(out))
 
 
 def whole():
@@ -106,53 +116,124 @@
     out_ref[...] = done.reshape(NL, fields, LANES)
 
 
-def first_kernel(fields, b_ref, sine_ref, out_ref):
-    forward_rows(lambda l, base: b_ref[pl.ds(base * NL + l, 8, stride=NL), :], sine_ref, out_ref, fields)
-
-
-def next_kernel(fields, b_ref, own_ref, recv_ref, sine_ref, out_ref, image_ref, work_ref):
+def deal(me_ref, all_ref, keep_ref, send_ref):
+    core = me_ref[0] & 1
+    half = NL // 2
+    keep_ref[...] = all_ref[pl.ds(core * half, half)]
+    send_ref[...] = all_ref[pl.ds((1 - core) * half, half)]
+
+
+def first_kernel(fields, me_ref, b_ref, sine_ref, keep_ref, send_ref, all_ref):
+    forward_rows(lambda l, base: b_ref[pl.ds(base * NL + l, 8, stride=NL), :], sine_ref, all_ref, fields)
+    deal(me_ref, all_ref, keep_ref, send_ref)
+
+
+def next_kernel(fields, me_ref, b_ref, own_ref, recv_ref, sine_ref, keep_ref, send_ref, image_ref, work_ref, all_ref):
     image = own_ref[...] + recv_ref[...]
     image_ref[...] = image
     work_ref[...] = b_ref[...] - SHIFT * image
-    forward_rows(lambda l, base: work_ref[pl.ds(base * NL + l, 8, stride=NL), :], sine_ref, out_ref, fields)
-
-
-def circ_kernel(fields, half, x_ref, table_ref, out_ref):
-    quarter = half // 2
+    forward_rows(lambda l, base: work_ref[pl.ds(base * NL + l, 8, stride=NL), :], sine_ref, all_ref, fields)
+    deal(me_ref, all_ref, keep_ref, send_ref)
+
+
+def swap_halves(x):
+    return pltpu.roll(x, NT, 1)
+
+
+def columns(fields):
     comp_row = lax.broadcasted_iota(jnp.int32, (8, LANES), 0)
-    low = lax.broadcasted_iota(jnp.int32, (8, LANES), 1) < NT
-    for base in range(0, fields, 8):
-        comp = (comp_row + base) % COMPS
-
-        def spread(part, d):
-            rows = table_ref[part, d]
-            return jnp.where(comp == 0, rows[0:1], jnp.where(comp == 1, rows[1:2], rows[2:3]))
-
-        coef = [[spread(part, d) for d in range(quarter)] for part in range(4)]
-        plus, minus, plus_x, minus_x = [], [], [], []
-        for c in range(quarter):
-            a = x_ref[c, base : base + 8, :]
-            b = x_ref[c + quarter, base : base + 8, :]
-            plus.append(a + b)
-            minus.append(a - b)
-            plus_x.append(pltpu.roll(a + b, NT, 1))
-            minus_x.append(pltpu.roll(a - b, NT, 1))
-        outs = [None] * half
-        for c in range(quarter):
-            even = odd = None
-            for e in range(quarter):
-                d = (c - e) % quarter
-                term = coef[0][d] * plus[e] + coef[2][d] * plus_x[e]
-                even = term if even is None else even + term
-                term = coef[1][d] * minus[e] + coef[3][d] * minus_x[e]
-                if c < e:
-                    term = -term
-                odd = term if odd is None else odd + term
-            outs[c] = even + odd
-            outs[c + quarter] = even - odd
-        for c in range(half):
-            out_ref[c, 0, base : base + 8, :] = outs[c]
-            out_ref[c, 1, base : base + 8, :] = jnp.where(low, outs[(c + 1) % half], outs[c - 1])
+
+    def run(body):
+        def step(m, carry):
+            for base in range(0, fields, 8):
+                comp = (comp_row + base) % COMPS
+
+                def spread(rows):
+                    return jnp.where(comp == 0, rows[0:1], jnp.where(comp == 1, rows[1:2], rows[2:3]))
+
+                body(m, slice(base, base + 8), spread)
+            return carry
+
+        lax.fori_loop(0, NL // 2, step, 0)
+
+    return run
+
+
+def four_cells(core, keep, recv):
+    first = jnp.where(core == 0, keep, recv)
+    second = jnp.where(core == 0, recv, keep)
+    return first, swap_halves(first), second, swap_halves(second)
+
+
+def low_lanes(rows):
+    return lax.broadcasted_iota(jnp.int32, (rows, LANES), 1) < NT
+
+
+def ends_kernel(fields, me_ref, keep_ref, recv_ref, power_ref, ends_ref):
+    core = me_ref[0] & 1
+    low = low_lanes(COMPS)
+
+    def body(m, at, spread):
+        cells = four_cells(core, keep_ref[m, at, :], recv_ref[m, at, :])
+        acc = None
+        for cell, (a, b) in zip(cells, ((0, 2), (1, 3), (2, 0), (3, 1))):
+            term = spread(jnp.where(low, power_ref[core, a, m], power_ref[core, b, m])) * cell
+            acc = term if acc is None else acc + term
+        ends_ref[m, at, :] = acc
+
+    columns(fields)(body)
+
+
+def stage_kernel(fields, n_circ, stage, last, me_ref, *refs):
+    own_ref, recv_ref, power_ref = refs[:3]
+    sum_ref = None if stage == 0 else refs[3]
+    outs = refs[3 if stage == 0 else 4 :]
+    me = me_ref[0]
+    core, chip = me & 1, me >> 1
+    block = 4 << stage
+    bit = (chip >> stage) & 1
+    place = 4 * (chip & ((1 << stage) - 1))
+    right = jnp.where(bit == 0, block - 3 - place, n_circ - 3 - place - block)
+    left = jnp.where(bit == 0, n_circ - 2 * block + place + 1, place + 1)
+    low = low_lanes(COMPS)
+
+    def pair(m, a, b):
+        return jnp.where(low, power_ref[core, a, m], power_ref[core, b, m])
+
+    def body(m, at, spread):
+        other = recv_ref[m, at, :]
+        total = spread(pair(m, right, left)) * other
+        outs[0][m, at, :] = total if sum_ref is None else total + sum_ref[m, at, :]
+        if not last:
+            near, far = bit * block, (1 - bit) * block
+            joined = spread(pair(m, near, far)) * own_ref[m, at, :] + spread(pair(m, far, near)) * other
+            outs[1][m, at, :] = joined
+
+    columns(fields)(body)
+
+
+def cells_kernel(fields, me_ref, keep_ref, recv_ref, sum_ref, cell_ref, mine_ref, send_ref):
+    core = me_ref[0] & 1
+    low = low_lanes(8)
+
+    def body(m, at, spread):
+        outside = sum_ref[m, at, :]
+        terms = four_cells(core, keep_ref[m, at, :], recv_ref[m, at, :]) + (outside, swap_halves(outside))
+        cells = []
+        for group in range(3):
+            acc = None
+            for i, term in enumerate(terms):
+                part = spread(cell_ref[core, 6 * group + i, m]) * term
+                acc = part if acc is None else acc + part
+            cells.append(acc)
+        near0 = jnp.where(low, cells[1], cells[2])
+        near1 = jnp.where(low, cells[2], cells[0])
+        mine_ref[m, 0, at, :] = jnp.where(core == 0, cells[0], cells[1])
+        mine_ref[m, 1, at, :] = jnp.where(core == 0, near0, near1)
+        send_ref[m, 0, at, :] = jnp.where(core == 0, cells[1], cells[0])
+        send_ref[m, 1, at, :] = jnp.where(core == 0, near1, near0)
+
+    columns(fields)(body)
 
 
 def lane_masks(rows):
@@ -167,9 +248,12 @@
 
 
 def operator_kernel(
-    modes, fields, row_ref, pair_ref, coup_ref, spec_ref, sine_ref, stiff_ref, stiff_l_ref, stiff_r_ref,
-    field_ref, own_ref, cross_ref, work_ref, ends_ref, face_ref, term_ref, inv_ref
+    modes, fields, me_ref, row_ref, pair_ref, coup_ref, sine_ref, stiff_ref, stiff_l_ref, stiff_r_ref, *refs
 ):
+    keep_ref, recv_ref, field_ref, own_ref, cross_ref, spec_ref, ends_ref, face_ref, term_ref, inv_ref = refs
+    core = me_ref[0] & 1
+    spec_ref[pl.ds(core * (NL // 2), NL // 2)] = keep_ref[...]
+    spec_ref[pl.ds((1 - core) * (NL // 2), NL // 2)] = recv_ref[...]
     total_modes = pair_ref.shape[1]
     low, first, last = lane_masks(NL)
     row = lax.broadcasted_iota(jnp.int32, (NL, LANES), 0)
@@ -319,84 +403,75 @@
     stiff_l = lax.ppermute(stiff, "circ", ahead)
     stiff_r = lax.ppermute(stiff, "circ", back)
     row_start = (lax.axis_index("mode") * modes).astype(jnp.int32).reshape(1)
-    me = lax.axis_index("circ").astype(jnp.int32)
-
-    split = circ // NL
-    if split == 1:
-        table = lax.dynamic_index_in_dim(jnp.asarray(circulant_table(n_circ)), me, 0, keepdims=False)
-
-        def round_trip(spec):
-            spec = lax.all_to_all(spec, "circ", split_axis=0, concat_axis=0)
-            spec = pl.pallas_call(
-                lambda *refs: circ_kernel(fields, circ, *refs),
-                out_shape=struct(circ, 2, fields, LANES),
-                in_specs=[whole()] * 2,
-                out_specs=whole(),
-                compiler_params=params(),
-            )(spec, table)
-            return lax.all_to_all(spec, "circ", split_axis=0, concat_axis=0)
-
-    else:
-        span = NT // split
-        htab = jnp.asarray(hartley_np(n_circ), f32)
-        denom = jnp.asarray(denominator_np(n_circ), f32).reshape(comps, n_circ, NL, split, span)
-        denom = denom.transpose(2, 3, 0, 1, 4).reshape(circ, comps, n_circ, span)
-        denom = lax.dynamic_index_in_dim(denom, me, 0, keepdims=False)
-
-        def round_trip(spec):
-            spec = spec.reshape(NL, fields, local_circ, split, span).transpose(0, 3, 1, 2, 4)
-            spec = spec.reshape(circ, fields, local_circ, span)
-            spec = lax.all_to_all(spec, "circ", split_axis=0, concat_axis=0)
-            spec = spec[:, : modes * comps]
-            spec = jnp.einsum("cfes,cek->fks", spec, htab.reshape(circ, local_circ, n_circ), precision=HIGHEST)
-            spec = spec.reshape(modes, comps, n_circ, span) / denom[None]
-            spec = jnp.einsum("pcks,kn->npcs", spec, htab, precision=HIGHEST)
-            spec = spec.reshape(n_circ, modes * comps, span)
-            spec = jnp.pad(spec, ((0, 0), (0, pad_fields), (0, 0)))
-            own = spec.reshape(circ, local_circ, fields, span)
-            after = jnp.roll(own[:, 0], -1, axis=0)
-            before = jnp.roll(own[:, -1], 1, axis=0)
-            spec = jnp.stack([own[:, 0], own[:, 1], after, before], axis=1)
-            spec = lax.all_to_all(spec, "circ", split_axis=0, concat_axis=0)
-            spec = spec.reshape(NL, split, 2, 2, fields, span).transpose(0, 2, 4, 3, 1, 5)
-            return spec.reshape(NL, 2, fields, LANES)
-
-    def operate(spec):
+    me = lax.axis_index("circ").astype(jnp.int32).reshape(1)
+
+    half = struct(NL // 2, fields, LANES)
+    pairs = struct(NL // 2, 2, fields, LANES)
+    power = jnp.asarray(power_table(n_circ))
+    cell = jnp.asarray(cell_table(n_circ))
+
+    def call(kernel, out_shape, *args, scratch_shapes=()):
+        single = not isinstance(out_shape, list)
+        return pl.pallas_call(
+            kernel,
+            out_shape=out_shape,
+            in_specs=[smem()] + [whole()] * (len(args) - 1),
+            out_specs=whole() if single else [whole()] * len(out_shape),
+            scratch_shapes=scratch_shapes,
+            compiler_params=params(),
+        )(*args)
+
+    def partner(values, d):
+        return lax.ppermute(values, "circ", [(i, i ^ d) for i in range(circ)])
+
+    def round_trip(keep, send):
+        recv = partner(send, 1)
+        ends = call(functools.partial(ends_kernel, fields), half, me, keep, recv, power)
+        stages = (circ // 2).bit_length() - 1
+        total = []
+        for stage in range(stages):
+            last = stage == stages - 1
+            other = partner(ends, 2 << stage)
+            total, *joined = call(
+                functools.partial(stage_kernel, fields, n_circ, stage, last),
+                [half] if last else [half, half],
+                me, ends, other, power, *total,
+            )
+            total = [total]
+            ends = joined[0] if joined else None
+        mine, send = call(functools.partial(cells_kernel, fields), [pairs, pairs], me, keep, recv, *total, cell)
+        return mine, partner(send, 1)
+
+    def operate(parts):
         return pl.pallas_call(
             lambda *refs: operator_kernel(modes, fields, *refs),
             out_shape=[struct(rows, LANES)] * 3,
-            in_specs=[smem()] * 3 + [whole()] * 5,
+            in_specs=[smem()] * 4 + [whole()] * 6,
             out_specs=[whole()] * 3,
             scratch_shapes=[
-                pltpu.VMEM((8, LANES), f32),
+                pltpu.VMEM((NL, 2, fields, LANES), f32),
                 pltpu.VMEM((rows, LANES), f32),
                 pltpu.VMEM((KM, 6, COMPS * NL, LANES), f32),
                 pltpu.VMEM((KM, modes, COMPS * NL, LANES), f32),
                 pltpu.SMEM((KM - 1, modes * mode_blocks), jnp.int32),
             ],
             compiler_params=params(),
-        )(row_start, pairing, coupling, spec, sine, stiff, stiff_l, stiff_r)
+        )(me, row_start, pairing, coupling, sine, stiff, stiff_l, stiff_r, *parts)
 
     swap = [(0, 1), (1, 0)]
 
-    spec = pl.pallas_call(
-        lambda *refs: first_kernel(fields, *refs),
-        out_shape=struct(NL, fields, LANES),
-        in_specs=[whole()] * 2,
-        out_specs=whole(),
-        compiler_params=params(),
-    )(b, sine)
-    u, own, cross = operate(round_trip(spec))
+    keep, send = call(
+        functools.partial(first_kernel, fields), [half, half], me, b, sine, scratch_shapes=[pltpu.VMEM((NL, fields, LANES), f32)]
+    )
+    u, own, cross = operate(round_trip(keep, send))
     recv = lax.ppermute(cross, "mode", swap)
-    spec, v = pl.pallas_call(
-        lambda *refs: next_kernel(fields, *refs),
-        out_shape=[struct(NL, fields, LANES), struct(rows, LANES)],
-        in_specs=[whole()] * 4,
-        out_specs=[whole()] * 2,
-        scratch_shapes=[pltpu.VMEM((rows, LANES), f32)],
-        compiler_params=params(),
-    )(b, own, recv, sine)
-    z, own, cross = operate(round_trip(spec))
+    keep, send, v = call(
+        functools.partial(next_kernel, fields),
+        [half, half, struct(rows, LANES)],
+        me, b, own, recv, sine,
+        scratch_shapes=[pltpu.VMEM((rows, LANES), f32), pltpu.VMEM((NL, fields, LANES), f32)],
+    )
+    z, own, cross = operate(round_trip(keep, send))
     recv = lax.ppermute(cross, "mode", swap)
     devices = circ * mode_blocks
     q, part = pl.pallas_call(

time: 114 us -> 97.9 us (0.86)
  blocking collectives: 44.1 us -> 10.9 us
  waiting for transfers between devices: 32.8 us -> 51.3 us
  starting transfers between devices: 18.6 us -> 15.8 us
  Pallas kernels: 11.1 us -> 12.4 us
    ppermute x0 -> x10, waiting for transfers between devices: none -> 33.5 us  [partner(): return lax.ppermute(values, 'circ', [(i, i ^ d) for i in range(circ)])]
    all_to_all x2 -> x0, blocking collectives: 31.4 us -> none  [the longest x1 17.2 us: round_trip(): return lax.all_to_all(spec, 'circ', split_axis=0, concat_axis=0)]
    all_to_all x2 -> x0, starting transfers between devices: 11.1 us -> none  [the longest x1 7.38 us: round_trip(): spec = lax.all_to_all(spec, 'circ', split_axis=0, concat_axis=0)]
    all_to_all x2 -> x0, waiting for transfers between devices: 9.3 us -> none  [the longest x1 9.18 us: round_trip(): spec = lax.all_to_all(spec, 'circ', split_axis=0, concat_axis=0)]
    ppermute x0 -> x10, starting transfers between devices: none -> 8.54 us  [partner(): return lax.ppermute(values, 'circ', [(i, i ^ d) for i in range(circ)])]
    ppermute x1, waiting for transfers between devices: 5.13 us -> 1.59 us  [on_device(): stiff_r = lax.ppermute(stiff, 'circ', back)]
    all_to_all x1, blocking collectives: 12.7 us -> 10.9 us  [on_device(): parts = lax.all_to_all(part, ('circ', 'mode'), split_axis=0, concat_axis=0)]
    ppermute x2, waiting for transfers between devices: 13.5 us -> 11.7 us  [on_device(): recv = lax.ppermute(cross, 'mode', swap)]
  transfers between devices with their start and end apart: 6 -> 14, of which waited for: 6 -> 13; matrix products, arithmetic and copies ran while one was open for 1% -> 0% of each run, Pallas kernels for 0% -> 0%
where the time goes in v3:
time: 97.9 us; the launch traced here: 97.7 us
  waiting for transfers between devices  51.3 us (52%)
  starting transfers between devices  15.8 us (16%)
  Pallas kernels  12.4 us (13%)
  blocking collectives  10.9 us (11%)
  local copies, waits for them, and re-layouts  6.43 us (7%)
    ppermute x10, waiting for transfers between devices, partner(): return lax.ppermute(values, 'circ', [(i, i ^ d) for i in range(circ)])  33.5 us
    ppermute x2, waiting for transfers between devices, on_device(): recv = lax.ppermute(cross, 'mode', swap)  11.7 us
    all_to_all x1, blocking collectives, on_device(): parts = lax.all_to_all(part, ('circ', 'mode'), split_axis=0, concat_axis=0)  10.9 us
    ppermute x10, starting transfers between devices, partner(): return lax.ppermute(values, 'circ', [(i, i ^ d) for i in range(circ)])  8.54 us
    pallas_call x2, Pallas kernels, operate(): pl.pallas_call(lambda *refs: operator_kernel(modes, fields, *refs), out_s...  7.24 us
    pallas_call x12, Pallas kernels, call(): pl.pallas_call(kernel, out_shape=out_shape, in_specs=[smem()] + [whole()]...  4.77 us
    ppermute x1, waiting for transfers between devices, on_device(): stiff_l = lax.ppermute(stiff, 'circ', ahead)  4.44 us
    ppermute x1, starting transfers between devices, on_device(): stiff_r = lax.ppermute(stiff, 'circ', back)  4.13 us
  transfers between devices with their start and end apart: 14, of which 13 were waited for; matrix products, arithmetic and copies ran while one was open for 0% of the time, Pallas kernels for 0%

profile of v3, /device:TPU:0, one launch (start us, length us, event | category | flops | bytes accessed | tf_op | source)
XLA Modules:
  0.0 97.7 jit_solution(4258362060885213159)
XLA Ops:
  0.6 1.3 %reshape.34 = f32[30,2,16,64]{3,2,1,0:T(8,128)S(1)} reshape(f32[10,3,2,1024]{3,2,1,0:T(2,128)} %param.7) | data formatting | bytes 491520 | tf_op jit(solution)/shard_map/reshape | solution.py:397
  2.5 0.8 copy-done.2
  4.4 1.0 %collective-permute-done.2.recv_ref = f32[8,32,128]{2,1,0:T(8,128)S(1)} collective-permute-done((f32[8,32,128]{2,1,0:T(8,128)S(1)}, f32[8,32,128]{2,1,0:T(8,128)S(1)}, u32[]{:S(2)}, u32[]{:S(2)}) %collective-permute-start.2) | collective-permute-done | bytes 131104 | tf_op jit(solution)/shard_map/ppermute | solution.py:425
  5.3 0.7 shard_map.87.refs_0_
  6.0 2.9 %collective-permute-start.3 = (f32[8,32,128]{2,1,0:T(8,128)S(1)}, f32[8,32,128]{2,1,0:T(8,128)S(1)}, u32[]{:S(2)}, u32[]{:S(2)}) collective-permute-start(f32[8,32,128]{2,1,0:T(8,128)S(1)} %shard_map.87.refs_0_), channel_id=1, source_target_pairs={{0,4},{2,6},{4,0},{6,2},{8,12},{10,14},{12,8},{14,10},{16,20},{18,... | collective-permute-start | bytes 393224 | tf_op jit(solution)/shard_map/ppermute | solution.py:425
  8.9 3.8 %collective-permute-done.3.refs_1_ = f32[8,32,128]{2,1,0:T(8,128)S(1)} collective-permute-done((f32[8,32,128]{2,1,0:T(8,128)S(1)}, f32[8,32,128]{2,1,0:T(8,128)S(1)}, u32[]{:S(2)}, u32[]{:S(2)}) %collective-permute-start.3) | collective-permute-done | bytes 131104 | tf_op jit(solution)/shard_map/ppermute | solution.py:425
  12.9 1.9 %collective-permute-start.4 = (f32[8,32,128]{2,1,0:T(8,128)S(1)}, f32[8,32,128]{2,1,0:T(8,128)S(1)}, u32[]{:S(2)}, u32[]{:S(2)}) collective-permute-start(f32[8,32,128]{2,1,0:T(8,128)S(1)} %get-tuple-element.31.refs_0_), channel_id=1, source_target_pairs={{0,8},{2,10},{4,12},{6,14},{8,0},{10,2},{12,4},{14,6},{16,24},{18,... | collective-permute-start | bytes 393224 | tf_op jit(solution)/shard_map/ppermute | solution.py:425
  14.8 3.2 %collective-permute-done.4.refs_1_ = f32[8,32,128]{2,1,0:T(8,128)S(1)} collective-permute-done((f32[8,32,128]{2,1,0:T(8,128)S(1)}, f32[8,32,128]{2,1,0:T(8,128)S(1)}, u32[]{:S(2)}, u32[]{:S(2)}) %collective-permute-start.4) | collective-permute-done | bytes 131104 | tf_op jit(solution)/shard_map/ppermute | solution.py:425
  18.2 2.8 %collective-permute-start.5 = (f32[8,32,128]{2,1,0:T(8,128)S(1)}, f32[8,32,128]{2,1,0:T(8,128)S(1)}, u32[]{:S(2)}, u32[]{:S(2)}) collective-permute-start(f32[8,32,128]{2,1,0:T(8,128)S(1)} %get-tuple-element.33.refs_0_), channel_id=1, source_target_pairs={{0,16},{2,18},{4,20},{6,22},{8,24},{10,26},{12,28},{14,30},{16,0},... | collective-permute-start | bytes 393224 | tf_op jit(solution)/shard_map/ppermute | solution.py:425
  21.0 5.1 %collective-permute-done.5.refs_1_ = f32[8,32,128]{2,1,0:T(8,128)S(1)} collective-permute-done((f32[8,32,128]{2,1,0:T(8,128)S(1)}, f32[8,32,128]{2,1,0:T(8,128)S(1)}, u32[]{:S(2)}, u32[]{:S(2)}) %collective-permute-start.5) | collective-permute-done | bytes 131104 | tf_op jit(solution)/shard_map/ppermute | solution.py:425
  26.2 0.9 copy-done.1
  27.2 0.7 shard_map.91
  28.2 4.1 %collective-permute-start.1 = (f32[4,16,128]{2,1,0:T(8,128)S(1)}, f32[4,16,128]{2,1,0:T(8,128)S(1)}, u32[]{:S(2)}, u32[]{:S(2)}) collective-permute-start(f32[4,16,128]{2,1,0:T(8,128)S(1)} %reshape.39.refs_5_), channel_id=1, source_target_pairs={{2,0},{4,2},{6,4},{8,6},{10,8},{12,10},{14,12},{16,14},{18,16},{20... | collective-permute-start | bytes 98312 | tf_op jit(solution)/shard_map/ppermute | solution.py:404
  32.4 1.6 %collective-permute-done.1.refs_7_ = f32[4,16,128]{2,1,0:T(8,128)S(1)} collective-permute-done((f32[4,16,128]{2,1,0:T(8,128)S(1)}, f32[4,16,128]{2,1,0:T(8,128)S(1)}, u32[]{:S(2)}, u32[]{:S(2)}) %collective-permute-start.1) | collective-permute-done | bytes 32800 | tf_op jit(solution)/shard_map/ppermute | solution.py:404
  34.0 4.4 %collective-permute-done.refs_6_ = f32[4,16,128]{2,1,0:T(8,128)S(1)} collective-permute-done((f32[4,16,128]{2,1,0:T(8,128)S(1)}, f32[4,16,128]{2,1,0:T(8,128)S(1)}, u32[]{:S(2)}, u32[]{:S(2)}) %collective-permute-start) | collective-permute-done | bytes 32800 | tf_op jit(solution)/shard_map/ppermute | solution.py:403
  38.4 3.6 %shard_map.92 = (f32[512,128]{1,0:T(8,128)S(1)}, f32[512,128]{1,0:T(8,128)S(1)}, f32[512,128]{1,0:T(8,128)S(1)}) custom-call(s32[1]{0:T(128)} %bitcast.1.me_ref.refs_0_, s32[1]{0:T(128)} %bitcast.2.refs_1_, s32[3,20]{1,0:T(4,128)S(1)} %copy-done.3, f32[3,20]{1,0:T(4,128)S(1)} %copy-done.4, f32[128,128]{1,0:T(8,128)S(1)} %copy-done.2, ...), custom_call_target="tpu_custom_call" | custom-call | tf_op jit(solution)/shard_map/pallas_call | solution.py:446
  42.0 1.6 %collective-permute-start.7 = (f32[512,128]{1,0:T(8,128)S(1)}, f32[512,128]{1,0:T(8,128)S(1)}, u32[]{:S(2)}, u32[]{:S(2)}) collective-permute-start(f32[512,128]{1,0:T(8,128)S(1)} %get-tuple-element.39), channel_id=1, source_target_pairs={{0,1},{1,0},{2,3},{3,2},{4,5},{5,4},{6,7},{7,6},{8,9},{9,8},{10,11... | collective-permute-start | bytes 786440 | tf_op jit(solution)/shard_map/ppermute | solution.py:467
  43.6 4.9 %collective-permute-done.7.recv_ref = f32[512,128]{1,0:T(8,128)S(1)} collective-permute-done((f32[512,128]{1,0:T(8,128)S(1)}, f32[512,128]{1,0:T(8,128)S(1)}, u32[]{:S(2)}, u32[]{:S(2)}) %collective-permute-start.7) | collective-permute-done | bytes 262176 | tf_op jit(solution)/shard_map/ppermute | solution.py:467
  48.5 0.6 shard_map.93
  49.2 1.3 %collective-permute-done.8.recv_ref = f32[8,32,128]{2,1,0:T(8,128)S(1)} collective-permute-done((f32[8,32,128]{2,1,0:T(8,128)S(1)}, f32[8,32,128]{2,1,0:T(8,128)S(1)}, u32[]{:S(2)}, u32[]{:S(2)}) %collective-permute-start.8) | collective-permute-done | bytes 131104 | tf_op jit(solution)/shard_map/ppermute | solution.py:425
  50.5 0.7 shard_map.94.refs_0_
  51.2 5.5 %collective-permute-done.9.refs_1_ = f32[8,32,128]{2,1,0:T(8,128)S(1)} collective-permute-done((f32[8,32,128]{2,1,0:T(8,128)S(1)}, f32[8,32,128]{2,1,0:T(8,128)S(1)}, u32[]{:S(2)}, u32[]{:S(2)}) %collective-permute-start.9) | collective-permute-done | bytes 131104 | tf_op jit(solution)/shard_map/ppermute | solution.py:425
  57.0 5.0 %collective-permute-done.10.refs_1_ = f32[8,32,128]{2,1,0:T(8,128)S(1)} collective-permute-done((f32[8,32,128]{2,1,0:T(8,128)S(1)}, f32[8,32,128]{2,1,0:T(8,128)S(1)}, u32[]{:S(2)}, u32[]{:S(2)}) %collective-permute-start.10) | collective-permute-done | bytes 131104 | tf_op jit(solution)/shard_map/ppermute | solution.py:425
  62.2 7.0 %collective-permute-done.11.refs_1_ = f32[8,32,128]{2,1,0:T(8,128)S(1)} collective-permute-done((f32[8,32,128]{2,1,0:T(8,128)S(1)}, f32[8,32,128]{2,1,0:T(8,128)S(1)}, u32[]{:S(2)}, u32[]{:S(2)}) %collective-permute-start.11) | collective-permute-done | bytes 131104 | tf_op jit(solution)/shard_map/ppermute | solution.py:425
  69.3 0.7 shard_map.98
  70.1 1.5 %collective-permute-done.12.refs_9_ = f32[8,2,32,128]{3,2,1,0:T(8,128)S(1)} collective-permute-done((f32[8,2,32,128]{3,2,1,0:T(8,128)S(1)}, f32[8,2,32,128]{3,2,1,0:T(8,128)S(1)}, u32[]{:S(2)}, u32[]{:S(2)}) %collective-permute-start.12) | collective-permute-done | bytes 262176 | tf_op jit(solution)/shard_map/ppermute | solution.py:425
  71.6 3.6 %shard_map.99 = (f32[512,128]{1,0:T(8,128)S(1)}, f32[512,128]{1,0:T(8,128)S(1)}, f32[512,128]{1,0:T(8,128)S(1)}) custom-call(s32[1]{0:T(128)} %bitcast.1.me_ref.refs_0_, s32[1]{0:T(128)} %bitcast.2.refs_1_, s32[3,20]{1,0:T(4,128)S(1)} %copy-done.3, f32[3,20]{1,0:T(4,128)S(1)} %copy-done.4, f32[128,128]{1,0:T(8,128)S(1)} %copy-done.2, ...), custom_call_target="tpu_custom_call" | custom-call | tf_op jit(solution)/shard_map/pallas_call | solution.py:446
  75.3 1.6 %collective-permute-start.13 = (f32[512,128]{1,0:T(8,128)S(1)}, f32[512,128]{1,0:T(8,128)S(1)}, u32[]{:S(2)}, u32[]{:S(2)}) collective-permute-start(f32[512,128]{1,0:T(8,128)S(1)} %get-tuple-element.51), channel_id=1, source_target_pairs={{0,1},{1,0},{2,3},{3,2},{4,5},{5,4},{6,7},{7,6},{8,9},{9,8},{10,11... | collective-permute-start | bytes 786440 | tf_op jit(solution)/shard_map/ppermute | solution.py:475
  76.8 6.9 %collective-permute-done.13.refs_5_ = f32[512,128]{1,0:T(8,128)S(1)} collective-permute-done((f32[512,128]{1,0:T(8,128)S(1)}, f32[512,128]{1,0:T(8,128)S(1)}, u32[]{:S(2)}, u32[]{:S(2)}) %collective-permute-start.13) | collective-permute-done | bytes 262176 | tf_op jit(solution)/shard_map/ppermute | solution.py:475
  83.8 10.9 %all_to_all.5.parts_ref = f32[32,8,128]{2,1,0:T(8,128)S(1)} all-to-all(f32[32,8,128]{2,1,0:T(8,128)S(1)} %get-tuple-element.52), channel_id=1, replica_groups=mesh['circ'=16,'mode'=2] {'circ','mode'}, dimensions={0} | all-to-all | bytes 262144 | tf_op jit(solution)/shard_map/all_to_all | solution.py:484
  95.4 1.0 reshape.41
  96.7 1.0 reshape.43
  (40 shorter events, 4.2 us)
Async XLA Ops:
  2.1 3.2 %copy-start = (f32[2,26,8,3,128]{4,3,2,1,0:T(4,128)S(1)}, f32[2,26,8,3,128]{4,3,2,1,0:T(4,128)}, u32[]{:S(2)}) copy-start(f32[2,26,8,3,128]{4,3,2,1,0:T(4,128)} %constant.20.clone.power_ref.refs_2_) | copy-start | bytes 1916932
  2.4 0.8 copy-start.2
  3.8 1.5 %collective-permute-start.2 = (f32[8,32,128]{2,1,0:T(8,128)S(1)}, f32[8,32,128]{2,1,0:T(8,128)S(1)}, u32[]{:S(2)}, u32[]{:S(2)}) collective-permute-start(f32[8,32,128]{2,1,0:T(8,128)S(1)} %get-tuple-element.30), channel_id=1, source_target_pairs={{0,2},{2,0},{4,6},{6,4},{8,10},{10,8},{12,14},{14,12},{16,18},{18,... | collective-permute-start | bytes 393224 | tf_op jit(solution)/shard_map/ppermute | solution.py:425
  6.0 6.7 %collective-permute-start.3 = (f32[8,32,128]{2,1,0:T(8,128)S(1)}, f32[8,32,128]{2,1,0:T(8,128)S(1)}, u32[]{:S(2)}, u32[]{:S(2)}) collective-permute-start(f32[8,32,128]{2,1,0:T(8,128)S(1)} %shard_map.87.refs_0_), channel_id=1, source_target_pairs={{0,4},{2,6},{4,0},{6,2},{8,12},{10,14},{12,8},{14,10},{16,20},{18,... | collective-permute-start | bytes 393224 | tf_op jit(solution)/shard_map/ppermute | solution.py:425
  12.9 5.1 %collective-permute-start.4 = (f32[8,32,128]{2,1,0:T(8,128)S(1)}, f32[8,32,128]{2,1,0:T(8,128)S(1)}, u32[]{:S(2)}, u32[]{:S(2)}) collective-permute-start(f32[8,32,128]{2,1,0:T(8,128)S(1)} %get-tuple-element.31.refs_0_), channel_id=1, source_target_pairs={{0,8},{2,10},{4,12},{6,14},{8,0},{10,2},{12,4},{14,6},{16,24},{18,... | collective-permute-start | bytes 393224 | tf_op jit(solution)/shard_map/ppermute | solution.py:425
  18.2 7.9 %collective-permute-start.5 = (f32[8,32,128]{2,1,0:T(8,128)S(1)}, f32[8,32,128]{2,1,0:T(8,128)S(1)}, u32[]{:S(2)}, u32[]{:S(2)}) collective-permute-start(f32[8,32,128]{2,1,0:T(8,128)S(1)} %get-tuple-element.33.refs_0_), channel_id=1, source_target_pairs={{0,16},{2,18},{4,20},{6,22},{8,24},{10,26},{12,28},{14,30},{16,0},... | collective-permute-start | bytes 393224 | tf_op jit(solution)/shard_map/ppermute | solution.py:425
  26.1 1.1 %copy-start.1 = (f32[2,18,8,3,128]{4,3,2,1,0:T(4,128)S(1)}, f32[2,18,8,3,128]{4,3,2,1,0:T(4,128)}, u32[]{:S(2)}) copy-start(f32[2,18,8,3,128]{4,3,2,1,0:T(4,128)} %constant.21.clone.cell_ref) | copy-start | bytes 1327108
  27.2 0.8 copy-start.5
  27.9 10.5 %collective-permute-start.6 = (f32[8,2,32,128]{3,2,1,0:T(8,128)S(1)}, f32[8,2,32,128]{3,2,1,0:T(8,128)S(1)}, u32[]{:S(2)}, u32[]{:S(2)}) collective-permute-start(f32[8,2,32,128]{3,2,1,0:T(8,128)S(1)} %get-tuple-element.36), channel_id=1, source_target_pairs={{0,2},{2,0},{4,6},{6,4},{8,10},{10,8},{12,14},{14,12},{16,18},{18,... | collective-permute-start | bytes 786440 | tf_op jit(solution)/shard_map/ppermute | solution.py:425
  28.2 5.7 %collective-permute-start.1 = (f32[4,16,128]{2,1,0:T(8,128)S(1)}, f32[4,16,128]{2,1,0:T(8,128)S(1)}, u32[]{:S(2)}, u32[]{:S(2)}) collective-permute-start(f32[4,16,128]{2,1,0:T(8,128)S(1)} %reshape.39.refs_5_), channel_id=1, source_target_pairs={{2,0},{4,2},{6,4},{8,6},{10,8},{12,10},{14,12},{16,14},{18,16},{20... | collective-permute-start | bytes 98312 | tf_op jit(solution)/shard_map/ppermute | solution.py:404
  32.4 6.0 %collective-permute-start = (f32[4,16,128]{2,1,0:T(8,128)S(1)}, f32[4,16,128]{2,1,0:T(8,128)S(1)}, u32[]{:S(2)}, u32[]{:S(2)}) collective-permute-start(f32[4,16,128]{2,1,0:T(8,128)S(1)} %reshape.39.refs_5_), channel_id=1, source_target_pairs={{0,2},{2,4},{4,6},{6,8},{8,10},{10,12},{12,14},{14,16},{16,18},{18... | collective-permute-start | bytes 98312 | tf_op jit(solution)/shard_map/ppermute | solution.py:403
  32.4 6.0 %copy-start.4 = (f32[3,20]{1,0:T(4,128)S(1)}, f32[3,20]{1,0:T(4,128)}, u32[]{:S(2)}) copy-start(f32[3,20]{1,0:T(4,128)} %refs_3_.3) | copy-start | bytes 724
  32.4 6.0 %copy-start.3 = (s32[3,20]{1,0:T(4,128)S(1)}, s32[3,20]{1,0:T(4,128)}, u32[]{:S(2)}) copy-start(s32[3,20]{1,0:T(4,128)} %refs_2_.9) | copy-start | bytes 724
  42.0 6.4 %collective-permute-start.7 = (f32[512,128]{1,0:T(8,128)S(1)}, f32[512,128]{1,0:T(8,128)S(1)}, u32[]{:S(2)}, u32[]{:S(2)}) collective-permute-start(f32[512,128]{1,0:T(8,128)S(1)} %get-tuple-element.39), channel_id=1, source_target_pairs={{0,1},{1,0},{2,3},{3,2},{4,5},{5,4},{6,7},{7,6},{8,9},{9,8},{10,11... | collective-permute-start | bytes 786440 | tf_op jit(solution)/shard_map/ppermute | solution.py:467
  49.1 1.4 %collective-permute-start.8 = (f32[8,32,128]{2,1,0:T(8,128)S(1)}, f32[8,32,128]{2,1,0:T(8,128)S(1)}, u32[]{:S(2)}, u32[]{:S(2)}) collective-permute-start(f32[8,32,128]{2,1,0:T(8,128)S(1)} %get-tuple-element.42), channel_id=1, source_target_pairs={{0,2},{2,0},{4,6},{6,4},{8,10},{10,8},{12,14},{14,12},{16,18},{18,... | collective-permute-start | bytes 393224 | tf_op jit(solution)/shard_map/ppermute | solution.py:425
  51.2 5.6 %collective-permute-start.9 = (f32[8,32,128]{2,1,0:T(8,128)S(1)}, f32[8,32,128]{2,1,0:T(8,128)S(1)}, u32[]{:S(2)}, u32[]{:S(2)}) collective-permute-start(f32[8,32,128]{2,1,0:T(8,128)S(1)} %shard_map.94.refs_0_), channel_id=1, source_target_pairs={{0,4},{2,6},{4,0},{6,2},{8,12},{10,14},{12,8},{14,10},{16,20},{18,... | collective-permute-start | bytes 393224 | tf_op jit(solution)/shard_map/ppermute | solution.py:425
  56.9 5.0 %collective-permute-start.10 = (f32[8,32,128]{2,1,0:T(8,128)S(1)}, f32[8,32,128]{2,1,0:T(8,128)S(1)}, u32[]{:S(2)}, u32[]{:S(2)}) collective-permute-start(f32[8,32,128]{2,1,0:T(8,128)S(1)} %get-tuple-element.43.refs_0_), channel_id=1, source_target_pairs={{0,8},{2,10},{4,12},{6,14},{8,0},{10,2},{12,4},{14,6},{16,24},{18,... | collective-permute-start | bytes 393224 | tf_op jit(solution)/shard_map/ppermute | solution.py:425
  62.1 7.1 %collective-permute-start.11 = (f32[8,32,128]{2,1,0:T(8,128)S(1)}, f32[8,32,128]{2,1,0:T(8,128)S(1)}, u32[]{:S(2)}, u32[]{:S(2)}) collective-permute-start(f32[8,32,128]{2,1,0:T(8,128)S(1)} %get-tuple-element.45.refs_0_), channel_id=1, source_target_pairs={{0,16},{2,18},{4,20},{6,22},{8,24},{10,26},{12,28},{14,30},{16,0},... | collective-permute-start | bytes 393224 | tf_op jit(solution)/shard_map/ppermute | solution.py:425
  70.0 1.6 %collective-permute-start.12 = (f32[8,2,32,128]{3,2,1,0:T(8,128)S(1)}, f32[8,2,32,128]{3,2,1,0:T(8,128)S(1)}, u32[]{:S(2)}, u32[]{:S(2)}) collective-permute-start(f32[8,2,32,128]{3,2,1,0:T(8,128)S(1)} %get-tuple-element.48), channel_id=1, source_target_pairs={{0,2},{2,0},{4,6},{6,4},{8,10},{10,8},{12,14},{14,12},{16,18},{18,... | collective-permute-start | bytes 786440 | tf_op jit(solution)/shard_map/ppermute | solution.py:425
  75.3 8.4 %collective-permute-start.13 = (f32[512,128]{1,0:T(8,128)S(1)}, f32[512,128]{1,0:T(8,128)S(1)}, u32[]{:S(2)}, u32[]{:S(2)}) collective-permute-start(f32[512,128]{1,0:T(8,128)S(1)} %get-tuple-element.51), channel_id=1, source_target_pairs={{0,1},{1,0},{2,3},{3,2},{4,5},{5,4},{6,7},{7,6},{8,9},{9,8},{10,11... | collective-permute-start | bytes 786440 | tf_op jit(solution)/shard_map/ppermute | solution.py:475

commit v4 on v0

v4 whole, which is shorter than its diff:
```python
import functools
import math

import jax
import jax.numpy as jnp
import numpy as np
from jax import lax
from jax.experimental import pallas as pl
from jax.experimental.pallas import tpu as pltpu
from jax.sharding import PartitionSpec as P

KM = 4
NL = 16
NT = 64
COMPS = 3
LANES = 2 * NT
HALF = NL // 2
WAYS = 2 * (KM - 1)
HIGHEST = lax.Precision.HIGHEST
F32 = jnp.float32

SHIFT = 2.0 / 3.0


def weight(comp, direction):
    return 2.0 if comp == direction else 1.0


def cosine_np():
    l = np.arange(NL)
    return np.cos(math.pi * l[None, :] * (2 * l[:, None] + 1) / (2 * NL))


COS = cosine_np()


def sine_pair():
    t = np.arange(NT) + 1
    both = np.zeros((LANES, LANES))
    both[:NT, :NT] = both[NT:, NT:] = np.sin(math.pi * t[:, None] * t[None, :] / (NT + 1))
    return both.astype(np.float32)


def root_np(comp):
    lam_l = 2.0 - 2.0 * np.cos(math.pi / NL * np.arange(NL))[:, None]
    lam_t = 2.0 - 2.0 * np.cos(math.pi / (NT + 1) * (np.arange(NT) + 1))[None, :]
    norm = np.where(np.arange(NL) == 0, 1.0 * NL, 0.5 * NL)[:, None] * (0.5 * (NT + 1))
    w = weight(comp, 0)
    half = 1.0 + (weight(comp, 1) * lam_l + weight(comp, 2) * lam_t) / (2.0 * w)
    big = half + np.sqrt(half * half - 1.0)
    return 1.0 / big, 1.0 / (w * (big - 1.0 / big) * norm)


def by_core(table):
    table = table.reshape(table.shape[0], 2, HALF, LANES)
    return np.moveaxis(table, 1, 0).astype(np.float32)


def power_table(comp, n_circ):
    root, _ = root_np(comp)
    powers = root[None] ** np.arange(n_circ - 6)[:, None, None]
    return by_core(np.concatenate([powers, powers], -1))


def cell_table(comp, n_circ):
    root, scale = root_np(comp)
    scale = scale / (1.0 - root**n_circ)

    def kernel(d):
        return scale * (root ** abs(d) + root ** (n_circ - abs(d)))

    out = []
    for low, high in ((0, 1), (2, 3), (4, -1)):
        for first, second in ((0, 1), (1, 0), (2, 3), (3, 2)):
            out.append(np.concatenate([kernel(low - first), kernel(high - second)], -1))
        out.append(np.concatenate([scale * root ** (3.0 - low), scale * root ** float(high)], -1))
        out.append(np.concatenate([scale * root ** float(low), scale * root ** (3.0 - high)], -1))
    return by_core(np.stack(out))


def low_lanes(rows):
    return lax.broadcasted_iota(jnp.int32, (rows, LANES), 1) < NT


def swap_halves(x):
    return pltpu.roll(x, NT, x.ndim - 1)


def exchange_bits(x):
    rows = x.shape[0]
    even = lax.broadcasted_iota(jnp.int32, x.shape, 0) % 2 == 0
    low = low_lanes(rows)
    other = swap_halves(x)
    moved = jnp.where(even, pltpu.roll(other, rows - 1, 0), pltpu.roll(other, 1, 0))
    return jnp.where(low == even, x, moved)


def forward(modes, core, src_ref, sine_ref, keep_ref, send_ref, rows_ref):
    plus, minus = [], []
    for l in range(HALF):
        a = src_ref[pl.ds(l, modes, stride=NL), :]
        b = src_ref[pl.ds(NL - 1 - l, modes, stride=NL), :]
        plus.append(a + b)
        minus.append(a - b)
    for m in range(NL):
        src = plus if m % 2 == 0 else minus
        acc = src[0] * float(COS[0, m])
        for l in range(1, HALF):
            acc = acc + src[l] * float(COS[l, m])
        rows_ref[pl.ds(m, modes, stride=NL), :] = acc
    rows_ref[...] = jnp.dot(rows_ref[...], sine_ref[...], precision=HIGHEST, preferred_element_type=F32)
    mine = pl.multiple_of(core * HALF, HALF)
    others = pl.multiple_of((1 - core) * HALF, HALF)
    for j in range(modes):
        keep_ref[j] = rows_ref[pl.ds(j * NL + mine, HALF), :]
        send_ref[j] = rows_ref[pl.ds(j * NL + others, HALF), :]


def first_kernel(modes, comp, me_ref, raw_ref, sine_ref, keep_ref, send_ref, b_ref, rows_ref):
    for j in range(modes):
        at = (j * COMPS + comp) * NL
        b_ref[j * NL : (j + 1) * NL, :] = exchange_bits(raw_ref[at : at + NL, :])
    forward(modes, me_ref[0] & 1, b_ref, sine_ref, keep_ref, send_ref, rows_ref)


def next_kernel(modes, me_ref, b_ref, own_ref, recv_ref, sine_ref, keep_ref, send_ref, image_ref, work_ref, rows_ref):
    image = own_ref[...] + recv_ref[...]
    image_ref[...] = image
    work_ref[...] = b_ref[...] - SHIFT * image
    forward(modes, me_ref[0] & 1, work_ref, sine_ref, keep_ref, send_ref, rows_ref)


def four_cells(core, keep, recv):
    first = jnp.where(core == 0, keep, recv)
    second = jnp.where(core == 0, recv, keep)
    return first, swap_halves(first), second, swap_halves(second)


def ends_kernel(modes, me_ref, keep_ref, recv_ref, power_ref, ends_ref):
    core = me_ref[0] & 1
    low = low_lanes(HALF)
    coefs = [
        jnp.where(low, power_ref[core, a], power_ref[core, b]) for a, b in ((0, 2), (1, 3), (2, 0), (3, 1))
    ]
    for j in range(modes):
        acc = None
        for coef, cell in zip(coefs, four_cells(core, keep_ref[j], recv_ref[j])):
            acc = coef * cell if acc is None else acc + coef * cell
        ends_ref[j] = acc


def stage_kernel(modes, n_circ, stage, last, me_ref, *refs):
    own_ref, recv_ref, power_ref = refs[:3]
    sum_ref = None if stage == 0 else refs[3]
    outs = refs[3 if stage == 0 else 4 :]
    core, chip = me_ref[0] & 1, me_ref[0] >> 1
    block = 4 << stage
    bit = (chip >> stage) & 1
    place = 4 * (chip & ((1 << stage) - 1))
    right = jnp.where(bit == 0, block - 3 - place, n_circ - 3 - place - block)
    left = jnp.where(bit == 0, n_circ - 2 * block + place + 1, place + 1)
    low = low_lanes(HALF)

    def pair(a, b):
        return jnp.where(low, power_ref[core, a], power_ref[core, b])

    action = pair(right, left)
    if not last:
        near, far = bit * block, (1 - bit) * block
        own_coef, recv_coef = pair(near, far), pair(far, near)
    for j in range(modes):
        other = recv_ref[j]
        total = action * other
        outs[0][j] = total if sum_ref is None else total + sum_ref[j]
        if not last:
            outs[1][j] = own_coef * own_ref[j] + recv_coef * other


def cells_kernel(modes, me_ref, keep_ref, recv_ref, sum_ref, cell_ref, mine_ref, send_ref):
    core = me_ref[0] & 1
    low = low_lanes(HALF)
    for j in range(modes):
        outside = sum_ref[j]
        terms = four_cells(core, keep_ref[j], recv_ref[j]) + (outside, swap_halves(outside))
        cells = []
        for group in range(3):
            acc = None
            for i, term in enumerate(terms):
                part = cell_ref[core, 6 * group + i] * term
                acc = part if acc is None else acc + part
            cells.append(acc)
        near0 = jnp.where(low, cells[1], cells[2])
        near1 = jnp.where(low, cells[2], cells[0])
        mine_ref[0, j] = jnp.where(core == 0, cells[0], cells[1])
        mine_ref[1, j] = jnp.where(core == 0, near0, near1)
        send_ref[0, j] = jnp.where(core == 0, cells[1], cells[0])
        send_ref[1, j] = jnp.where(core == 0, near1, near0)


def neighbours(mid, ends, low):
    right = swap_halves(jnp.where(low, ends, mid))
    left = swap_halves(jnp.where(low, mid, ends))
    return right, left


def lane_ends(rows):
    lane = lax.broadcasted_iota(jnp.int32, (rows, LANES), 1) % NT
    return lane == 0, lane == NT - 1


def prepare_kernel(
    modes, row_ref, pair_ref, coup_ref, own_ref, left_ref, right_ref, *refs
):
    *face_refs, index_ref, coef_ref, inv_ref = refs
    total_modes = pair_ref.shape[1]
    low = low_lanes(NL)
    first, last = lane_ends(NL)
    row = lax.broadcasted_iota(jnp.int32, (NL, LANES), 0)
    for k in range(KM):
        at = slice(k * NL, (k + 1) * NL)
        a = exchange_bits(own_ref[at, :])
        ends = jnp.where(low, exchange_bits(right_ref[at, :]), exchange_bits(left_ref[at, :]))
        right, left = neighbours(a, ends, low)
        above = jnp.where(last, a, pltpu.roll(a, LANES - 1, 1))
        below = jnp.where(first, a, pltpu.roll(a, 1, 1))
        faces = [
            0.5 * (a + right),
            0.5 * (a + left),
            jnp.where(row == NL - 1, 0.0, 0.5 * (a + pltpu.roll(a, NL - 1, 0))),
            jnp.where(row == 0, 0.0, 0.5 * (a + pltpu.roll(a, 1, 0))),
            0.5 * (a + above),
            0.5 * (a + below),
        ]
        for comp in range(COMPS):
            for nb in range(6):
                w = weight(comp, nb // 2)
                face_refs[comp][k, nb] = faces[nb] * w if w != 1.0 else faces[nb]

    def invert(j, carry):
        for k in range(KM - 1):
            inv_ref[k, pair_ref[k, j]] = j
        return carry

    lax.fori_loop(0, total_modes, invert, 0)

    def entry(i, carry):
        for k in range(KM - 1):
            for way in range(2):
                partner = pair_ref[k, i] if way == 0 else inv_ref[k, i]
                coef = 0.5 * (coup_ref[k, i] if way == 0 else coup_ref[k, partner])
                local = partner - row_ref[0]
                inside = jnp.logical_and(local >= 0, local < modes)
                coef_ref[2 * k + way, i] = jnp.where(inside, coef, 0.0)
                index_ref[2 * k + way, i] = jnp.clip(local, 0, modes - 1)
        return carry

    lax.fori_loop(0, total_modes, entry, 0)


def operator_kernel(
    modes, total_modes, me_ref, row_ref, index_ref, coef_ref, keep_ref, recv_ref, sine_ref, face_ref,
    field_ref, own_ref, cross_ref, spec_ref, ends_ref, term_ref
):
    core = me_ref[0] & 1
    mine = pl.multiple_of(core * HALF, HALF)
    others = pl.multiple_of((1 - core) * HALF, HALF)
    for part in range(2):
        for j in range(modes):
            spec_ref[part, pl.ds(j * NL + mine, HALF), :] = keep_ref[part, j]
            spec_ref[part, pl.ds(j * NL + others, HALF), :] = recv_ref[part, j]
    for part in range(2):
        spec_ref[part] = jnp.dot(spec_ref[part], sine_ref[...], precision=HIGHEST, preferred_element_type=F32)
    for part in range(2):
        dst = field_ref if part == 0 else ends_ref
        y = [spec_ref[part, pl.ds(m, modes, stride=NL), :] for m in range(NL)]
        for l in range(HALF):
            even = y[0] * float(COS[l, 0])
            odd = y[1] * float(COS[l, 1])
            for m in range(2, NL, 2):
                even = even + y[m] * float(COS[l, m])
                odd = odd + y[m + 1] * float(COS[l, m + 1])
            dst[pl.ds(l, modes, stride=NL), :] = even + odd
            dst[pl.ds(NL - 1 - l, modes, stride=NL), :] = even - odd
    low = low_lanes(NL)
    first, last = lane_ends(NL)
    for j in range(modes):
        at = slice(j * NL, (j + 1) * NL)
        mid = field_ref[at, :]
        right, left = neighbours(mid, ends_ref[at, :], low)
        diffs = [
            mid - right,
            mid - left,
            mid - pltpu.roll(mid, NL - 1, 0),
            mid - pltpu.roll(mid, 1, 0),
            mid - jnp.where(last, 0.0, pltpu.roll(mid, LANES - 1, 1)),
            mid - jnp.where(first, 0.0, pltpu.roll(mid, 1, 1)),
        ]
        for k in range(KM):
            acc = face_ref[k, 0] * diffs[0]
            for nb in range(1, 6):
                acc = acc + face_ref[k, nb] * diffs[nb]
            term_ref[k, j] = acc
    row_start = row_ref[0]
    other_start = total_modes - modes - row_start

    def mixed(i, acc):
        for e in range(WAYS):
            part = coef_ref[e, i] * term_ref[1 + e // 2, index_ref[e, i]]
            acc = part if acc is None else acc + part
        return acc

    for i in range(modes):
        cross_ref[i * NL : (i + 1) * NL, :] = mixed(other_start + i, None)
    for i in range(modes):
        own_ref[i * NL : (i + 1) * NL, :] = mixed(row_start + i, term_ref[0, i])


def sums_kernel(rows, b_ref, u_ref, v_ref, z_ref, own_ref, recv_ref, *refs):
    *before, image_ref, part_ref = refs
    q = own_ref[...] + recv_ref[...]
    image_ref[...] = q
    b, u, v, z = b_ref[...], u_ref[...], v_ref[...], z_ref[...]

    def fold(x):
        x = jnp.sum(x.reshape(rows // 8, 8, LANES), axis=0)
        return jnp.sum(x, axis=0, keepdims=True)

    sums = [fold(b * u), fold(u * v), fold(v * z), fold(b * z), fold(z * q), jnp.zeros((3, LANES), F32)]
    part = jnp.concatenate(sums, axis=0)
    part_ref[...] = part + before[0][...] if before else part


def add_kernel(a_ref, b_ref, out_ref):
    out_ref[...] = a_ref[...] + b_ref[...]


def final_kernel(modes, a_ref, b_ref, *refs):
    *fields, x_ref, r_ref = refs
    total = jnp.sum(a_ref[...] + b_ref[...], axis=1, keepdims=True)
    bu, uv, vz, bz, zq = (total[i : i + 1, :] for i in range(5))
    a0 = bu / uv
    t = vz / uv
    c1 = (bz - a0 * vz) / (zq - t * vz)
    c0 = a0 - c1 * t
    for comp in range(COMPS):
        rhs_ref, u_ref, v_ref, z_ref, q_ref = fields[5 * comp : 5 * comp + 5]
        for j in range(modes):
            at = slice(j * NL, (j + 1) * NL)
            to = (j * COMPS + comp) * NL
            x_ref[to : to + NL, :] = exchange_bits(c0 * u_ref[at, :] + c1 * z_ref[at, :])
            r_ref[to : to + NL, :] = exchange_bits(rhs_ref[at, :] - c0 * v_ref[at, :] - c1 * q_ref[at, :])


def struct(*shape, dtype=F32):
    return jax.ShapeDtypeStruct(shape, dtype)


def call(kernel, out_shape, *args, scalars=0, scalar_outs=0, scratch_shapes=()):
    vmem, smem = pl.BlockSpec(memory_space=pltpu.VMEM), pl.BlockSpec(memory_space=pltpu.SMEM)
    size = 4 * sum(math.prod(a.shape) for a in list(args) + list(out_shape))
    return pl.pallas_call(
        kernel,
        out_shape=out_shape,
        in_specs=[smem] * scalars + [vmem] * (len(args) - scalars),
        out_specs=[vmem] * (len(out_shape) - scalar_outs) + [smem] * scalar_outs,
        scratch_shapes=scratch_shapes,
        compiler_params=pltpu.CompilerParams(vmem_limit_bytes=32 * 1024 * 1024),
        cost_estimate=pl.CostEstimate(flops=4 * size, bytes_accessed=size, transcendentals=0),
    )(*args)


def on_device(right_side, stiffness, pairing, coupling):
    modes, comps, local_circ, num_cells = right_side.shape
    circ = lax.axis_size("circ")
    total_modes = pairing.shape[1]
    n_circ = local_circ * circ
    rows = modes * NL
    stages = (circ // 2).bit_length() - 1

    def raw(values, count):
        values = values.reshape(count, local_circ, num_cells // LANES, LANES)
        return jnp.swapaxes(values, 1, 2).reshape(count * NL, LANES)

    def partner(values, d):
        return lax.ppermute(values, "circ", [(i, i ^ d) for i in range(circ)])

    def other_block(values):
        return lax.ppermute(values, "mode", [(0, 1), (1, 0)])

    sine = jnp.asarray(sine_pair())
    power = [jnp.asarray(power_table(c, n_circ)) for c in range(COMPS)]
    cell = [jnp.asarray(cell_table(c, n_circ)) for c in range(COMPS)]
    row_start = (lax.axis_index("mode") * modes).astype(jnp.int32).reshape(1)
    me = lax.axis_index("circ").astype(jnp.int32).reshape(1)
    half = struct(modes, HALF, LANES)
    pairs = struct(2, modes, HALF, LANES)
    column = struct(rows, LANES)
    each = range(COMPS)

    stiff = raw(stiffness, KM)
    stiff_l = lax.ppermute(stiff, "circ", [(i, (i + 1) % circ) for i in range(circ)])
    stiff_r = lax.ppermute(stiff, "circ", [((i + 1) % circ, i) for i in range(circ)])
    *faces, index, coef = call(
        functools.partial(prepare_kernel, modes),
        [struct(KM, 6, NL, LANES)] * COMPS + [struct(WAYS, total_modes, dtype=jnp.int32), struct(WAYS, total_modes)],
        row_start, pairing, coupling, stiff, stiff_l, stiff_r,
        scalars=3, scalar_outs=2,
        scratch_shapes=[pltpu.SMEM((KM - 1, total_modes), jnp.int32)],
    )

    def round_trip(keep, send):
        recv = [partner(send[c], 1) for c in each]
        ends = [call(functools.partial(ends_kernel, modes), [half], me, keep[c], recv[c], power[c], scalars=1)[0] for c in each]
        total = [()] * COMPS
        for stage in range(stages):
            last = stage == stages - 1
            kernel = functools.partial(stage_kernel, modes, n_circ, stage, last)
            other = [partner(ends[c], 2 << stage) for c in each]
            done = [
                call(kernel, [half] if last else [half, half], me, ends[c], other[c], power[c], *total[c], scalars=1)
                for c in each
            ]
            total = [done[c][:1] for c in each]
            ends = [done[c][-1] for c in each]
        done = [
            call(functools.partial(cells_kernel, modes), [pairs, pairs], me, keep[c], recv[c], *total[c], cell[c], scalars=1)
            for c in each
        ]
        return [(done[c][0], partner(done[c][1], 1)) for c in each]

    def operate(spec):
        done = [
            call(
                functools.partial(operator_kernel, modes, total_modes),
                [column] * 3,
                me, row_start, index, coef, *spec[c], sine, faces[c],
                scalars=4,
                scratch_shapes=[
                    pltpu.VMEM((2, rows, LANES), F32),
                    pltpu.VMEM((rows, LANES), F32),
                    pltpu.VMEM((KM, modes, NL, LANES), F32),
                ],
            )
            for c in each
        ]
        field, own, cross = zip(*done)
        return field, own, [other_block(cross[c]) for c in each]

    source = raw(right_side, modes * comps)
    keep, send, b = zip(*[
        call(
            functools.partial(first_kernel, modes, c),
            [half, half, column],
            me, source, sine,
            scalars=1, scratch_shapes=[pltpu.VMEM((rows, LANES), F32)],
        )
        for c in each
    ])
    u, own, recv = operate(round_trip(keep, send))
    keep, send, v = zip(*[
        call(
            functools.partial(next_kernel, modes),
            [half, half, column],
            me, b[c], own[c], recv[c], sine,
            scalars=1, scratch_shapes=[pltpu.VMEM((rows, LANES), F32)] * 2,
        )
        for c in each
    ])
    z, own, recv = operate(round_trip(keep, send))
    q, before = [], ()
    for c in each:
        image, part = call(
            functools.partial(sums_kernel, rows), [column, struct(8, LANES)], b[c], u[c], v[c], z[c], own[c], recv[c], *before
        )
        q.append(image)
        before = (part,)
    for d in range(circ.bit_length() - 1):
        part = call(add_kernel, [struct(8, LANES)], part, partner(part, 1 << d))[0]
    other = other_block(part)
    x, r = call(
        functools.partial(final_kernel, modes),
        [struct(modes * comps * NL, LANES)] * 2,
        part, other, *[values for c in each for values in (b[c], u[c], v[c], z[c], q[c])],
    )

    def give(values):
        values = values.reshape(modes * comps, num_cells // LANES, local_circ, LANES)
        return jnp.swapaxes(values, 1, 2).reshape(right_side.shape)

    return give(x), give(r)


def solution(mesh):
    placed = (P("mode", None, "circ", None), P(None, "circ", None), P(), P())
    return jax.shard_map(
        on_device,
        mesh=mesh,
        in_specs=placed,
        out_specs=(P("mode", None, "circ", None), P("mode", None, "circ", None)),
        check_vma=False,
    )
```

time: 336 us -> 93.2 us (0.28); the launches traced: 330 us -> 92.9 us
  blocking collectives: 168 us -> 0 us
  local copies, waits for them, and re-layouts: 72.1 us -> 5.04 us
  other arithmetic: 28.6 us -> 0 us
  Pallas kernels: 0 us -> 17.2 us
  starting transfers between devices: 24.8 us -> 40.4 us
  matrix products: 14.5 us -> 0 us
  waiting for transfers between devices: 15.2 us -> 29.2 us
  between operations: 6 us -> 1.08 us
    psum x3 -> x0, blocking collectives: 118 us -> none  [the longest x2 78.6 us: precond_sum(): return lax.psum(jnp.sum(residual * smoothed), ('circ', 'mode'))]
    ppermute x6 -> x43, starting transfers between devices: 11.6 us -> 40.4 us  [the longest x34 27.1 us: partner(): return lax.ppermute(values, 'circ', [(i, i ^ d) for i in range(circ)])]
    reshape x21 -> x0, local copies, waits for them, and re-layouts: 27.9 us -> none  [the longest x8 14.4 us: stencil(): inner.reshape(num_modes, num_comps, span, num_cells)]
    all_to_all x2 -> x0, blocking collectives: 27.8 us -> none  [the longest x1 15.3 us: precondition(): lax.all_to_all(spec, 'circ', split_axis=3, concat_axis=2, tiled=True)]
    unnamed x122 -> x24, local copies, waits for them, and re-layouts: 29.3 us -> 5.04 us
    all_gather x2 -> x0, blocking collectives: 22.1 us -> none  [on_device(): fold_piece = lax.all_gather(padded, 'mode', axis=0, tiled=True)]
    ppermute x6 -> x43, waiting for transfers between devices: 7.52 us -> 29.2 us  [the longest x34 20.5 us: partner(): return lax.ppermute(values, 'circ', [(i, i ^ d) for i in range(circ)])]
    pallas_call x0 -> x51, Pallas kernels: none -> 17.2 us  [call(): pl.pallas_call(kernel, out_shape=out_shape, in_specs=[smem] * scalars + [...]
  transfers between devices with their start and end apart: 8 -> 43, of which waited for: 4 -> 20; matrix products, arithmetic and copies ran while one was open for 8% -> 0% of each run, Pallas kernels for 0% -> 17%
where the time goes in v4:
time: 93.2 us; the launch traced here: 92.9 us
  starting transfers between devices  40.4 us (43%)
  waiting for transfers between devices  29.2 us (31%)
  Pallas kernels  17.2 us (18%)
  local copies, waits for them, and re-layouts  5.04 us (5%)
  between operations  1.08 us (1%)
    ppermute x34, starting transfers between devices, partner(): return lax.ppermute(values, 'circ', [(i, i ^ d) for i in range(circ)])  27.1 us
    ppermute x34, waiting for transfers between devices, partner(): return lax.ppermute(values, 'circ', [(i, i ^ d) for i in range(circ)])  20.5 us
    pallas_call x51, Pallas kernels, call(): pl.pallas_call(kernel, out_shape=out_shape, in_specs=[smem] * scalars + [...  17.2 us
    ppermute x7, starting transfers between devices, other_block(): return lax.ppermute(values, 'mode', [(0, 1), (1, 0)])  8.89 us
    ppermute x7, waiting for transfers between devices, other_block(): return lax.ppermute(values, 'mode', [(0, 1), (1, 0)])  7.04 us
    unnamed x24, local copies, waits for them, and re-layouts  5.04 us
    ppermute x1, starting transfers between devices, on_device(): lax.ppermute(stiff, 'circ', [((i + 1) % circ, i) for i in range(circ)])  4.44 us
  transfers between devices with their start and end apart: 43, of which 20 were waited for; matrix products, arithmetic and copies ran while one was open for 0% of the time, Pallas kernels for 17%

profile of v4, /device:TPU:0, one launch (start us, length us, event | category | flops | bytes accessed | tf_op | source)
XLA Modules:
  0.0 92.9 jit_solution(9817085885146526745)
XLA Ops:
  5.0 2.6 %collective-permute-start.27 = (f32[10,8,128]{2,1,0:T(8,128)S(1)}, f32[10,8,128]{2,1,0:T(8,128)S(1)}, u32[]{:S(2)}, u32[]{:S(2)}) collective-permute-start(f32[10,8,128]{2,1,0:T(8,128)S(1)} %shard_map.152.refs_0_), channel_id=1, source_target_pairs={{0,4},{2,6},{4,0},{6,2},{8,12},{10,14},{12,8},{14,10},{16,20},{18,... | collective-permute-start | bytes 122888 | tf_op jit(solution)/shard_map/ppermute | solution.py:385
  8.5 1.4 %collective-permute-start.3 = (f32[10,8,128]{2,1,0:T(8,128)S(1)}, f32[10,8,128]{2,1,0:T(8,128)S(1)}, u32[]{:S(2)}, u32[]{:S(2)}) collective-permute-start(f32[10,8,128]{2,1,0:T(8,128)S(1)} %shard_map.124.refs_0_), channel_id=1, source_target_pairs={{0,4},{2,6},{4,0},{6,2},{8,12},{10,14},{12,8},{14,10},{16,20},{18,... | collective-permute-start | bytes 122888 | tf_op jit(solution)/shard_map/ppermute | solution.py:385
  10.0 1.8 %collective-permute-start.28 = (f32[10,8,128]{2,1,0:T(8,128)S(1)}, f32[10,8,128]{2,1,0:T(8,128)S(1)}, u32[]{:S(2)}, u32[]{:S(2)}) collective-permute-start(f32[10,8,128]{2,1,0:T(8,128)S(1)} %get-tuple-element.142.refs_0_), channel_id=1, source_target_pairs={{0,8},{2,10},{4,12},{6,14},{8,0},{10,2},{12,4},{14,6},{16,24},{18,... | collective-permute-start | bytes 122888 | tf_op jit(solution)/shard_map/ppermute | solution.py:385
  11.9 1.6 %collective-permute-start.16 = (f32[10,8,128]{2,1,0:T(8,128)S(1)}, f32[10,8,128]{2,1,0:T(8,128)S(1)}, u32[]{:S(2)}, u32[]{:S(2)}) collective-permute-start(f32[10,8,128]{2,1,0:T(8,128)S(1)} %get-tuple-element.117.refs_0_), channel_id=1, source_target_pairs={{0,8},{2,10},{4,12},{6,14},{8,0},{10,2},{12,4},{14,6},{16,24},{18,... | collective-permute-start | bytes 122888 | tf_op jit(solution)/shard_map/ppermute | solution.py:385
  14.5 2.8 %collective-permute-start.29 = (f32[10,8,128]{2,1,0:T(8,128)S(1)}, f32[10,8,128]{2,1,0:T(8,128)S(1)}, u32[]{:S(2)}, u32[]{:S(2)}) collective-permute-start(f32[10,8,128]{2,1,0:T(8,128)S(1)} %get-tuple-element.144.refs_0_), channel_id=1, source_target_pairs={{0,16},{2,18},{4,20},{6,22},{8,24},{10,26},{12,28},{14,30},{16,0},... | collective-permute-start | bytes 122888 | tf_op jit(solution)/shard_map/ppermute | solution.py:385
  17.3 1.6 %collective-permute-start.17 = (f32[10,8,128]{2,1,0:T(8,128)S(1)}, f32[10,8,128]{2,1,0:T(8,128)S(1)}, u32[]{:S(2)}, u32[]{:S(2)}) collective-permute-start(f32[10,8,128]{2,1,0:T(8,128)S(1)} %get-tuple-element.119.refs_0_), channel_id=1, source_target_pairs={{0,16},{2,18},{4,20},{6,22},{8,24},{10,26},{12,28},{14,30},{16,0},... | collective-permute-start | bytes 122888 | tf_op jit(solution)/shard_map/ppermute | solution.py:385
  25.6 4.4 %collective-permute-start.1 = (f32[64,128]{1,0:T(8,128)S(1)}, f32[64,128]{1,0:T(8,128)S(1)}, u32[]{:S(2)}, u32[]{:S(2)}) collective-permute-start(f32[64,128]{1,0:T(8,128)S(1)} %bitcast.26), channel_id=1, source_target_pairs={{2,0},{4,2},{6,4},{8,6},{10,8},{12,10},{14,12},{16,14},{18,16},{20... | collective-permute-start | bytes 98312 | tf_op jit(solution)/shard_map/ppermute | solution.py:402
  30.0 1.6 %collective-permute-done.left_ref = f32[64,128]{1,0:T(8,128)S(1)} collective-permute-done((f32[64,128]{1,0:T(8,128)S(1)}, f32[64,128]{1,0:T(8,128)S(1)}, u32[]{:S(2)}, u32[]{:S(2)}) %collective-permute-start) | collective-permute-done | bytes 32800 | tf_op jit(solution)/shard_map/ppermute | solution.py:401
  31.6 2.5 %shard_map.123 = (f32[4,6,16,128]{3,2,1,0:T(8,128)S(1)}, f32[4,6,16,128]{3,2,1,0:T(8,128)S(1)}, f32[4,6,16,128]{3,2,1,0:T(8,128)S(1)}, s32[6,20]{1,0:T(8,128)S(1)}, f32[6,20]{1,0:T(8,128)S(1)}) custom-call(s32[1]{0:T(128)} %bitcast.4.row_ref, s32[3,20]{1,0:T(4,128)S(1)} %copy-done.10, f32[3,20]{1,0:T(4,128)S(1)} %copy-done.11, f32[64,128]{1,0:T(8,128)S(1)} %bitcast.27, ...), custom_call_target="tpu_custom_call" | custom-call | flops 2758288 | bytes 689572 | tf_op jit(solution)/shard_map/pallas_call | solution.py:361
  34.1 1.6 %shard_map.157 = (f32[160,128]{1,0:T(8,128)S(1)}, f32[160,128]{1,0:T(8,128)S(1)}, f32[160,128]{1,0:T(8,128)S(1)}) custom-call(s32[1]{0:T(128)} %bitcast.me_ref, s32[1]{0:T(128)} %bitcast.4.row_ref, s32[6,20]{1,0:T(8,128)S(1)} %get-tuple-element.88.index_ref, f32[6,20]{1,0:T(8,128)S(1)} %get-tuple-element.89.coef_ref, ...), custom_call_target="tpu_custom_call" | custom-call | flops 2690848 | bytes 672712 | tf_op jit(solution)/shard_map/pallas_call | solution.py:361
  35.7 1.6 %collective-permute-start.31 = (f32[160,128]{1,0:T(8,128)S(1)}, f32[160,128]{1,0:T(8,128)S(1)}, u32[]{:S(2)}, u32[]{:S(2)}) collective-permute-start(f32[160,128]{1,0:T(8,128)S(1)} %get-tuple-element.151), channel_id=1, source_target_pairs={{0,1},{1,0},{2,3},{3,2},{4,5},{5,4},{6,7},{7,6},{8,9},{9,8},{10,11... | collective-permute-start | bytes 245768 | tf_op jit(solution)/shard_map/ppermute | solution.py:388
  37.3 1.6 %shard_map.143 = (f32[160,128]{1,0:T(8,128)S(1)}, f32[160,128]{1,0:T(8,128)S(1)}, f32[160,128]{1,0:T(8,128)S(1)}) custom-call(s32[1]{0:T(128)} %bitcast.me_ref, s32[1]{0:T(128)} %bitcast.4.row_ref, s32[6,20]{1,0:T(8,128)S(1)} %get-tuple-element.88.index_ref, f32[6,20]{1,0:T(8,128)S(1)} %get-tuple-element.89.coef_ref, ...), custom_call_target="tpu_custom_call" | custom-call | flops 2690848 | bytes 672712 | tf_op jit(solution)/shard_map/pallas_call | solution.py:361
  39.5 1.6 %shard_map.129 = (f32[160,128]{1,0:T(8,128)S(1)}, f32[160,128]{1,0:T(8,128)S(1)}, f32[160,128]{1,0:T(8,128)S(1)}) custom-call(s32[1]{0:T(128)} %bitcast.me_ref, s32[1]{0:T(128)} %bitcast.4.row_ref, s32[6,20]{1,0:T(8,128)S(1)} %get-tuple-element.88.index_ref, f32[6,20]{1,0:T(8,128)S(1)} %get-tuple-element.89.coef_ref, ...), custom_call_target="tpu_custom_call" | custom-call | flops 2690848 | bytes 672712 | tf_op jit(solution)/shard_map/pallas_call | solution.py:361
  41.1 1.5 %collective-permute-start.7 = (f32[160,128]{1,0:T(8,128)S(1)}, f32[160,128]{1,0:T(8,128)S(1)}, u32[]{:S(2)}, u32[]{:S(2)}) collective-permute-start(f32[160,128]{1,0:T(8,128)S(1)} %get-tuple-element.101), channel_id=1, source_target_pairs={{0,1},{1,0},{2,3},{3,2},{4,5},{5,4},{6,7},{7,6},{8,9},{9,8},{10,11... | collective-permute-start | bytes 245768 | tf_op jit(solution)/shard_map/ppermute | solution.py:388
  46.4 2.1 %collective-permute-start.21 = (f32[10,8,128]{2,1,0:T(8,128)S(1)}, f32[10,8,128]{2,1,0:T(8,128)S(1)}, u32[]{:S(2)}, u32[]{:S(2)}) collective-permute-start(f32[10,8,128]{2,1,0:T(8,128)S(1)} %shard_map.145.refs_0_), channel_id=1, source_target_pairs={{0,4},{2,6},{4,0},{6,2},{8,12},{10,14},{12,8},{14,10},{16,20},{18,... | collective-permute-start | bytes 122888 | tf_op jit(solution)/shard_map/ppermute | solution.py:385
  48.7 2.0 %collective-permute-done.33.refs_1_ = f32[10,8,128]{2,1,0:T(8,128)S(1)} collective-permute-done((f32[10,8,128]{2,1,0:T(8,128)S(1)}, f32[10,8,128]{2,1,0:T(8,128)S(1)}, u32[]{:S(2)}, u32[]{:S(2)}) %collective-permute-start.33) | collective-permute-done | bytes 40992 | tf_op jit(solution)/shard_map/ppermute | solution.py:385
  51.1 1.7 %collective-permute-start.22 = (f32[10,8,128]{2,1,0:T(8,128)S(1)}, f32[10,8,128]{2,1,0:T(8,128)S(1)}, u32[]{:S(2)}, u32[]{:S(2)}) collective-permute-start(f32[10,8,128]{2,1,0:T(8,128)S(1)} %get-tuple-element.130.refs_0_), channel_id=1, source_target_pairs={{0,8},{2,10},{4,12},{6,14},{8,0},{10,2},{12,4},{14,6},{16,24},{18,... | collective-permute-start | bytes 122888 | tf_op jit(solution)/shard_map/ppermute | solution.py:385
  53.3 1.7 %collective-permute-done.34.refs_1_ = f32[10,8,128]{2,1,0:T(8,128)S(1)} collective-permute-done((f32[10,8,128]{2,1,0:T(8,128)S(1)}, f32[10,8,128]{2,1,0:T(8,128)S(1)}, u32[]{:S(2)}, u32[]{:S(2)}) %collective-permute-start.34) | collective-permute-done | bytes 40992 | tf_op jit(solution)/shard_map/ppermute | solution.py:385
  55.4 2.7 %collective-permute-start.23 = (f32[10,8,128]{2,1,0:T(8,128)S(1)}, f32[10,8,128]{2,1,0:T(8,128)S(1)}, u32[]{:S(2)}, u32[]{:S(2)}) collective-permute-start(f32[10,8,128]{2,1,0:T(8,128)S(1)} %get-tuple-element.132.refs_0_), channel_id=1, source_target_pairs={{0,16},{2,18},{4,20},{6,22},{8,24},{10,26},{12,28},{14,30},{16,0},... | collective-permute-start | bytes 122888 | tf_op jit(solution)/shard_map/ppermute | solution.py:385
  59.1 1.5 %collective-permute-done.35.refs_1_ = f32[10,8,128]{2,1,0:T(8,128)S(1)} collective-permute-done((f32[10,8,128]{2,1,0:T(8,128)S(1)}, f32[10,8,128]{2,1,0:T(8,128)S(1)}, u32[]{:S(2)}, u32[]{:S(2)}) %collective-permute-start.35) | collective-permute-done | bytes 40992 | tf_op jit(solution)/shard_map/ppermute | solution.py:385
  61.6 1.9 %collective-permute-done.11.refs_1_ = f32[10,8,128]{2,1,0:T(8,128)S(1)} collective-permute-done((f32[10,8,128]{2,1,0:T(8,128)S(1)}, f32[10,8,128]{2,1,0:T(8,128)S(1)}, u32[]{:S(2)}, u32[]{:S(2)}) %collective-permute-start.11) | collective-permute-done | bytes 40992 | tf_op jit(solution)/shard_map/ppermute | solution.py:385
  63.7 1.6 %shard_map.164 = (f32[160,128]{1,0:T(8,128)S(1)}, f32[160,128]{1,0:T(8,128)S(1)}, f32[160,128]{1,0:T(8,128)S(1)}) custom-call(s32[1]{0:T(128)} %bitcast.me_ref, s32[1]{0:T(128)} %bitcast.4.row_ref, s32[6,20]{1,0:T(8,128)S(1)} %get-tuple-element.88.index_ref, f32[6,20]{1,0:T(8,128)S(1)} %get-tuple-element.89.coef_ref, ...), custom_call_target="tpu_custom_call" | custom-call | flops 2690848 | bytes 672712 | tf_op jit(solution)/shard_map/pallas_call | solution.py:361
  65.4 1.5 %collective-permute-start.37 = (f32[160,128]{1,0:T(8,128)S(1)}, f32[160,128]{1,0:T(8,128)S(1)}, u32[]{:S(2)}, u32[]{:S(2)}) collective-permute-start(f32[160,128]{1,0:T(8,128)S(1)} %get-tuple-element.163), channel_id=1, source_target_pairs={{0,1},{1,0},{2,3},{3,2},{4,5},{5,4},{6,7},{7,6},{8,9},{9,8},{10,11... | collective-permute-start | bytes 245768 | tf_op jit(solution)/shard_map/ppermute | solution.py:388
  66.9 1.6 %shard_map.150 = (f32[160,128]{1,0:T(8,128)S(1)}, f32[160,128]{1,0:T(8,128)S(1)}, f32[160,128]{1,0:T(8,128)S(1)}) custom-call(s32[1]{0:T(128)} %bitcast.me_ref, s32[1]{0:T(128)} %bitcast.4.row_ref, s32[6,20]{1,0:T(8,128)S(1)} %get-tuple-element.88.index_ref, f32[6,20]{1,0:T(8,128)S(1)} %get-tuple-element.89.coef_ref, ...), custom_call_target="tpu_custom_call" | custom-call | flops 2690848 | bytes 672712 | tf_op jit(solution)/shard_map/pallas_call | solution.py:361
  69.1 1.6 %shard_map.136 = (f32[160,128]{1,0:T(8,128)S(1)}, f32[160,128]{1,0:T(8,128)S(1)}, f32[160,128]{1,0:T(8,128)S(1)}) custom-call(s32[1]{0:T(128)} %bitcast.me_ref, s32[1]{0:T(128)} %bitcast.4.row_ref, s32[6,20]{1,0:T(8,128)S(1)} %get-tuple-element.88.index_ref, f32[6,20]{1,0:T(8,128)S(1)} %get-tuple-element.89.coef_ref, ...), custom_call_target="tpu_custom_call" | custom-call | flops 2690848 | bytes 672712 | tf_op jit(solution)/shard_map/pallas_call | solution.py:361
  70.7 1.5 %collective-permute-start.13 = (f32[160,128]{1,0:T(8,128)S(1)}, f32[160,128]{1,0:T(8,128)S(1)}, u32[]{:S(2)}, u32[]{:S(2)}) collective-permute-start(f32[160,128]{1,0:T(8,128)S(1)} %get-tuple-element.113), channel_id=1, source_target_pairs={{0,1},{1,0},{2,3},{3,2},{4,5},{5,4},{6,7},{7,6},{8,9},{9,8},{10,11... | collective-permute-start | bytes 245768 | tf_op jit(solution)/shard_map/ppermute | solution.py:388
  73.2 2.1 %collective-permute-done.13.recv_ref = f32[160,128]{1,0:T(8,128)S(1)} collective-permute-done((f32[160,128]{1,0:T(8,128)S(1)}, f32[160,128]{1,0:T(8,128)S(1)}, u32[]{:S(2)}, u32[]{:S(2)}) %collective-permute-start.13) | collective-permute-done | bytes 81952 | tf_op jit(solution)/shard_map/ppermute | solution.py:388
  77.2 3.0 %collective-permute-done.39.b_ref = f32[8,128]{1,0:T(8,128)S(1)} collective-permute-done((f32[8,128]{1,0:T(8,128)S(1)}, f32[8,128]{1,0:T(8,128)S(1)}, u32[]{:S(2)}, u32[]{:S(2)}) %collective-permute-start.39) | collective-permute-done | bytes 4128 | tf_op jit(solution)/shard_map/ppermute | solution.py:385
  80.6 3.2 %collective-permute-done.40.b_ref = f32[8,128]{1,0:T(8,128)S(1)} collective-permute-done((f32[8,128]{1,0:T(8,128)S(1)}, f32[8,128]{1,0:T(8,128)S(1)}, u32[]{:S(2)}, u32[]{:S(2)}) %collective-permute-start.40) | collective-permute-done | bytes 4128 | tf_op jit(solution)/shard_map/ppermute | solution.py:385
  84.4 3.9 %collective-permute-done.41.b_ref = f32[8,128]{1,0:T(8,128)S(1)} collective-permute-done((f32[8,128]{1,0:T(8,128)S(1)}, f32[8,128]{1,0:T(8,128)S(1)}, u32[]{:S(2)}, u32[]{:S(2)}) %collective-permute-start.41) | collective-permute-done | bytes 4128 | tf_op jit(solution)/shard_map/ppermute | solution.py:385
  88.3 1.5 %collective-permute-start.42 = (f32[8,128]{1,0:T(8,128)S(1)}, f32[8,128]{1,0:T(8,128)S(1)}, u32[]{:S(2)}, u32[]{:S(2)}) collective-permute-start(f32[8,128]{1,0:T(8,128)S(1)} %shard_map.171.a_ref), channel_id=1, source_target_pairs={{0,1},{1,0},{2,3},{3,2},{4,5},{5,4},{6,7},{7,6},{8,9},{9,8},{10,11... | collective-permute-start | bytes 12296 | tf_op jit(solution)/shard_map/ppermute | solution.py:388
  89.7 2.1 %collective-permute-done.42.b_ref = f32[8,128]{1,0:T(8,128)S(1)} collective-permute-done((f32[8,128]{1,0:T(8,128)S(1)}, f32[8,128]{1,0:T(8,128)S(1)}, u32[]{:S(2)}, u32[]{:S(2)}) %collective-permute-start.42) | collective-permute-done | bytes 4128 | tf_op jit(solution)/shard_map/ppermute | solution.py:388
  (129 shorter events, 26.4 us)
Async XLA Ops:
  5.0 5.0 %collective-permute-start.27 = (f32[10,8,128]{2,1,0:T(8,128)S(1)}, f32[10,8,128]{2,1,0:T(8,128)S(1)}, u32[]{:S(2)}, u32[]{:S(2)}) collective-permute-start(f32[10,8,128]{2,1,0:T(8,128)S(1)} %shard_map.152.refs_0_), channel_id=1, source_target_pairs={{0,4},{2,6},{4,0},{6,2},{8,12},{10,14},{12,8},{14,10},{16,20},{18,... | collective-permute-start | bytes 122888 | tf_op jit(solution)/shard_map/ppermute | solution.py:385
  7.7 4.2 %collective-permute-start.15 = (f32[10,8,128]{2,1,0:T(8,128)S(1)}, f32[10,8,128]{2,1,0:T(8,128)S(1)}, u32[]{:S(2)}, u32[]{:S(2)}) collective-permute-start(f32[10,8,128]{2,1,0:T(8,128)S(1)} %shard_map.138.refs_0_), channel_id=1, source_target_pairs={{0,4},{2,6},{4,0},{6,2},{8,12},{10,14},{12,8},{14,10},{16,20},{18,... | collective-permute-start | bytes 122888 | tf_op jit(solution)/shard_map/ppermute | solution.py:385
  8.5 5.0 %collective-permute-start.3 = (f32[10,8,128]{2,1,0:T(8,128)S(1)}, f32[10,8,128]{2,1,0:T(8,128)S(1)}, u32[]{:S(2)}, u32[]{:S(2)}) collective-permute-start(f32[10,8,128]{2,1,0:T(8,128)S(1)} %shard_map.124.refs_0_), channel_id=1, source_target_pairs={{0,4},{2,6},{4,0},{6,2},{8,12},{10,14},{12,8},{14,10},{16,20},{18,... | collective-permute-start | bytes 122888 | tf_op jit(solution)/shard_map/ppermute | solution.py:385
  10.0 4.5 %collective-permute-start.28 = (f32[10,8,128]{2,1,0:T(8,128)S(1)}, f32[10,8,128]{2,1,0:T(8,128)S(1)}, u32[]{:S(2)}, u32[]{:S(2)}) collective-permute-start(f32[10,8,128]{2,1,0:T(8,128)S(1)} %get-tuple-element.142.refs_0_), channel_id=1, source_target_pairs={{0,8},{2,10},{4,12},{6,14},{8,0},{10,2},{12,4},{14,6},{16,24},{18,... | collective-permute-start | bytes 122888 | tf_op jit(solution)/shard_map/ppermute | solution.py:385
  11.9 5.3 %collective-permute-start.16 = (f32[10,8,128]{2,1,0:T(8,128)S(1)}, f32[10,8,128]{2,1,0:T(8,128)S(1)}, u32[]{:S(2)}, u32[]{:S(2)}) collective-permute-start(f32[10,8,128]{2,1,0:T(8,128)S(1)} %get-tuple-element.117.refs_0_), channel_id=1, source_target_pairs={{0,8},{2,10},{4,12},{6,14},{8,0},{10,2},{12,4},{14,6},{16,24},{18,... | collective-permute-start | bytes 122888 | tf_op jit(solution)/shard_map/ppermute | solution.py:385
  13.6 5.3 %collective-permute-start.4 = (f32[10,8,128]{2,1,0:T(8,128)S(1)}, f32[10,8,128]{2,1,0:T(8,128)S(1)}, u32[]{:S(2)}, u32[]{:S(2)}) collective-permute-start(f32[10,8,128]{2,1,0:T(8,128)S(1)} %get-tuple-element.92.refs_0_), channel_id=1, source_target_pairs={{0,8},{2,10},{4,12},{6,14},{8,0},{10,2},{12,4},{14,6},{16,24},{18,... | collective-permute-start | bytes 122888 | tf_op jit(solution)/shard_map/ppermute | solution.py:385
  14.5 5.9 %collective-permute-start.29 = (f32[10,8,128]{2,1,0:T(8,128)S(1)}, f32[10,8,128]{2,1,0:T(8,128)S(1)}, u32[]{:S(2)}, u32[]{:S(2)}) collective-permute-start(f32[10,8,128]{2,1,0:T(8,128)S(1)} %get-tuple-element.144.refs_0_), channel_id=1, source_target_pairs={{0,16},{2,18},{4,20},{6,22},{8,24},{10,26},{12,28},{14,30},{16,0},... | collective-permute-start | bytes 122888 | tf_op jit(solution)/shard_map/ppermute | solution.py:385
  17.3 5.0 %collective-permute-start.17 = (f32[10,8,128]{2,1,0:T(8,128)S(1)}, f32[10,8,128]{2,1,0:T(8,128)S(1)}, u32[]{:S(2)}, u32[]{:S(2)}) collective-permute-start(f32[10,8,128]{2,1,0:T(8,128)S(1)} %get-tuple-element.119.refs_0_), channel_id=1, source_target_pairs={{0,16},{2,18},{4,20},{6,22},{8,24},{10,26},{12,28},{14,30},{16,0},... | collective-permute-start | bytes 122888 | tf_op jit(solution)/shard_map/ppermute | solution.py:385
  18.9 5.0 %collective-permute-start.5 = (f32[10,8,128]{2,1,0:T(8,128)S(1)}, f32[10,8,128]{2,1,0:T(8,128)S(1)}, u32[]{:S(2)}, u32[]{:S(2)}) collective-permute-start(f32[10,8,128]{2,1,0:T(8,128)S(1)} %get-tuple-element.94.refs_0_), channel_id=1, source_target_pairs={{0,16},{2,18},{4,20},{6,22},{8,24},{10,26},{12,28},{14,30},{16,0},... | collective-permute-start | bytes 122888 | tf_op jit(solution)/shard_map/ppermute | solution.py:385
  21.4 12.7 %collective-permute-start.30 = (f32[2,10,8,128]{3,2,1,0:T(8,128)S(1)}, f32[2,10,8,128]{3,2,1,0:T(8,128)S(1)}, u32[]{:S(2)}, u32[]{:S(2)}) collective-permute-start(f32[2,10,8,128]{3,2,1,0:T(8,128)S(1)} %get-tuple-element.147), channel_id=1, source_target_pairs={{0,2},{2,0},{4,6},{6,4},{8,10},{10,8},{12,14},{14,12},{16,18},{18,... | collective-permute-start | bytes 245768 | tf_op jit(solution)/shard_map/ppermute | solution.py:385
  23.3 14.0 %collective-permute-start.18 = (f32[2,10,8,128]{3,2,1,0:T(8,128)S(1)}, f32[2,10,8,128]{3,2,1,0:T(8,128)S(1)}, u32[]{:S(2)}, u32[]{:S(2)}) collective-permute-start(f32[2,10,8,128]{3,2,1,0:T(8,128)S(1)} %get-tuple-element.122), channel_id=1, source_target_pairs={{0,2},{2,0},{4,6},{6,4},{8,10},{10,8},{12,14},{14,12},{16,18},{18,... | collective-permute-start | bytes 245768 | tf_op jit(solution)/shard_map/ppermute | solution.py:385
  24.9 14.6 %collective-permute-start.6 = (f32[2,10,8,128]{3,2,1,0:T(8,128)S(1)}, f32[2,10,8,128]{3,2,1,0:T(8,128)S(1)}, u32[]{:S(2)}, u32[]{:S(2)}) collective-permute-start(f32[2,10,8,128]{3,2,1,0:T(8,128)S(1)} %get-tuple-element.97), channel_id=1, source_target_pairs={{0,2},{2,0},{4,6},{6,4},{8,10},{10,8},{12,14},{14,12},{16,18},{18,... | collective-permute-start | bytes 245768 | tf_op jit(solution)/shard_map/ppermute | solution.py:385
  25.6 6.0 %collective-permute-start = (f32[64,128]{1,0:T(8,128)S(1)}, f32[64,128]{1,0:T(8,128)S(1)}, u32[]{:S(2)}, u32[]{:S(2)}) collective-permute-start(f32[64,128]{1,0:T(8,128)S(1)} %bitcast.25), channel_id=1, source_target_pairs={{0,2},{2,4},{4,6},{6,8},{8,10},{10,12},{12,14},{14,16},{16,18},{18... | collective-permute-start | bytes 98312 | tf_op jit(solution)/shard_map/ppermute | solution.py:401
  25.6 6.0 %collective-permute-start.1 = (f32[64,128]{1,0:T(8,128)S(1)}, f32[64,128]{1,0:T(8,128)S(1)}, u32[]{:S(2)}, u32[]{:S(2)}) collective-permute-start(f32[64,128]{1,0:T(8,128)S(1)} %bitcast.26), channel_id=1, source_target_pairs={{2,0},{4,2},{6,4},{8,6},{10,8},{12,10},{14,12},{16,14},{18,16},{20... | collective-permute-start | bytes 98312 | tf_op jit(solution)/shard_map/ppermute | solution.py:402
  35.7 6.9 %collective-permute-start.31 = (f32[160,128]{1,0:T(8,128)S(1)}, f32[160,128]{1,0:T(8,128)S(1)}, u32[]{:S(2)}, u32[]{:S(2)}) collective-permute-start(f32[160,128]{1,0:T(8,128)S(1)} %get-tuple-element.151), channel_id=1, source_target_pairs={{0,1},{1,0},{2,3},{3,2},{4,5},{5,4},{6,7},{7,6},{8,9},{9,8},{10,11... | collective-permute-start | bytes 245768 | tf_op jit(solution)/shard_map/ppermute | solution.py:388
  38.9 5.1 %collective-permute-start.19 = (f32[160,128]{1,0:T(8,128)S(1)}, f32[160,128]{1,0:T(8,128)S(1)}, u32[]{:S(2)}, u32[]{:S(2)}) collective-permute-start(f32[160,128]{1,0:T(8,128)S(1)} %get-tuple-element.126), channel_id=1, source_target_pairs={{0,1},{1,0},{2,3},{3,2},{4,5},{5,4},{6,7},{7,6},{8,9},{9,8},{10,11... | collective-permute-start | bytes 245768 | tf_op jit(solution)/shard_map/ppermute | solution.py:388
  41.1 4.5 %collective-permute-start.7 = (f32[160,128]{1,0:T(8,128)S(1)}, f32[160,128]{1,0:T(8,128)S(1)}, u32[]{:S(2)}, u32[]{:S(2)}) collective-permute-start(f32[160,128]{1,0:T(8,128)S(1)} %get-tuple-element.101), channel_id=1, source_target_pairs={{0,1},{1,0},{2,3},{3,2},{4,5},{5,4},{6,7},{7,6},{8,9},{9,8},{10,11... | collective-permute-start | bytes 245768 | tf_op jit(solution)/shard_map/ppermute | solution.py:388
  46.2 4.4 %collective-permute-start.33 = (f32[10,8,128]{2,1,0:T(8,128)S(1)}, f32[10,8,128]{2,1,0:T(8,128)S(1)}, u32[]{:S(2)}, u32[]{:S(2)}) collective-permute-start(f32[10,8,128]{2,1,0:T(8,128)S(1)} %shard_map.159.refs_0_), channel_id=1, source_target_pairs={{0,4},{2,6},{4,0},{6,2},{8,12},{10,14},{12,8},{14,10},{16,20},{18,... | collective-permute-start | bytes 122888 | tf_op jit(solution)/shard_map/ppermute | solution.py:385
  46.4 4.7 %collective-permute-start.21 = (f32[10,8,128]{2,1,0:T(8,128)S(1)}, f32[10,8,128]{2,1,0:T(8,128)S(1)}, u32[]{:S(2)}, u32[]{:S(2)}) collective-permute-start(f32[10,8,128]{2,1,0:T(8,128)S(1)} %shard_map.145.refs_0_), channel_id=1, source_target_pairs={{0,4},{2,6},{4,0},{6,2},{8,12},{10,14},{12,8},{14,10},{16,20},{18,... | collective-permute-start | bytes 122888 | tf_op jit(solution)/shard_map/ppermute | solution.py:385
  48.6 4.2 %collective-permute-start.9 = (f32[10,8,128]{2,1,0:T(8,128)S(1)}, f32[10,8,128]{2,1,0:T(8,128)S(1)}, u32[]{:S(2)}, u32[]{:S(2)}) collective-permute-start(f32[10,8,128]{2,1,0:T(8,128)S(1)} %shard_map.131.refs_0_), channel_id=1, source_target_pairs={{0,4},{2,6},{4,0},{6,2},{8,12},{10,14},{12,8},{14,10},{16,20},{18,... | collective-permute-start | bytes 122888 | tf_op jit(solution)/shard_map/ppermute | solution.py:385
  50.6 4.3 %collective-permute-start.34 = (f32[10,8,128]{2,1,0:T(8,128)S(1)}, f32[10,8,128]{2,1,0:T(8,128)S(1)}, u32[]{:S(2)}, u32[]{:S(2)}) collective-permute-start(f32[10,8,128]{2,1,0:T(8,128)S(1)} %get-tuple-element.155.refs_0_), channel_id=1, source_target_pairs={{0,8},{2,10},{4,12},{6,14},{8,0},{10,2},{12,4},{14,6},{16,24},{18,... | collective-permute-start | bytes 122888 | tf_op jit(solution)/shard_map/ppermute | solution.py:385
  51.1 4.3 %collective-permute-start.22 = (f32[10,8,128]{2,1,0:T(8,128)S(1)}, f32[10,8,128]{2,1,0:T(8,128)S(1)}, u32[]{:S(2)}, u32[]{:S(2)}) collective-permute-start(f32[10,8,128]{2,1,0:T(8,128)S(1)} %get-tuple-element.130.refs_0_), channel_id=1, source_target_pairs={{0,8},{2,10},{4,12},{6,14},{8,0},{10,2},{12,4},{14,6},{16,24},{18,... | collective-permute-start | bytes 122888 | tf_op jit(solution)/shard_map/ppermute | solution.py:385
  52.8 5.2 %collective-permute-start.10 = (f32[10,8,128]{2,1,0:T(8,128)S(1)}, f32[10,8,128]{2,1,0:T(8,128)S(1)}, u32[]{:S(2)}, u32[]{:S(2)}) collective-permute-start(f32[10,8,128]{2,1,0:T(8,128)S(1)} %get-tuple-element.105.refs_0_), channel_id=1, source_target_pairs={{0,8},{2,10},{4,12},{6,14},{8,0},{10,2},{12,4},{14,6},{16,24},{18,... | collective-permute-start | bytes 122888 | tf_op jit(solution)/shard_map/ppermute | solution.py:385
  55.0 5.7 %collective-permute-start.35 = (f32[10,8,128]{2,1,0:T(8,128)S(1)}, f32[10,8,128]{2,1,0:T(8,128)S(1)}, u32[]{:S(2)}, u32[]{:S(2)}) collective-permute-start(f32[10,8,128]{2,1,0:T(8,128)S(1)} %get-tuple-element.157.refs_0_), channel_id=1, source_target_pairs={{0,16},{2,18},{4,20},{6,22},{8,24},{10,26},{12,28},{14,30},{16,0},... | collective-permute-start | bytes 122888 | tf_op jit(solution)/shard_map/ppermute | solution.py:385
  55.4 5.7 %collective-permute-start.23 = (f32[10,8,128]{2,1,0:T(8,128)S(1)}, f32[10,8,128]{2,1,0:T(8,128)S(1)}, u32[]{:S(2)}, u32[]{:S(2)}) collective-permute-start(f32[10,8,128]{2,1,0:T(8,128)S(1)} %get-tuple-element.132.refs_0_), channel_id=1, source_target_pairs={{0,16},{2,18},{4,20},{6,22},{8,24},{10,26},{12,28},{14,30},{16,0},... | collective-permute-start | bytes 122888 | tf_op jit(solution)/shard_map/ppermute | solution.py:385
  58.1 5.4 %collective-permute-start.11 = (f32[10,8,128]{2,1,0:T(8,128)S(1)}, f32[10,8,128]{2,1,0:T(8,128)S(1)}, u32[]{:S(2)}, u32[]{:S(2)}) collective-permute-start(f32[10,8,128]{2,1,0:T(8,128)S(1)} %get-tuple-element.107.refs_0_), channel_id=1, source_target_pairs={{0,16},{2,18},{4,20},{6,22},{8,24},{10,26},{12,28},{14,30},{16,0},... | collective-permute-start | bytes 122888 | tf_op jit(solution)/shard_map/ppermute | solution.py:385
  61.2 5.7 %collective-permute-start.24 = (f32[2,10,8,128]{3,2,1,0:T(8,128)S(1)}, f32[2,10,8,128]{3,2,1,0:T(8,128)S(1)}, u32[]{:S(2)}, u32[]{:S(2)}) collective-permute-start(f32[2,10,8,128]{3,2,1,0:T(8,128)S(1)} %get-tuple-element.135), channel_id=1, source_target_pairs={{0,2},{2,0},{4,6},{6,4},{8,10},{10,8},{12,14},{14,12},{16,18},{18,... | collective-permute-start | bytes 245768 | tf_op jit(solution)/shard_map/ppermute | solution.py:385
  63.6 5.5 %collective-permute-start.12 = (f32[2,10,8,128]{3,2,1,0:T(8,128)S(1)}, f32[2,10,8,128]{3,2,1,0:T(8,128)S(1)}, u32[]{:S(2)}, u32[]{:S(2)}) collective-permute-start(f32[2,10,8,128]{3,2,1,0:T(8,128)S(1)} %get-tuple-element.110), channel_id=1, source_target_pairs={{0,2},{2,0},{4,6},{6,4},{8,10},{10,8},{12,14},{14,12},{16,18},{18,... | collective-permute-start | bytes 245768 | tf_op jit(solution)/shard_map/ppermute | solution.py:385
  65.4 6.9 %collective-permute-start.37 = (f32[160,128]{1,0:T(8,128)S(1)}, f32[160,128]{1,0:T(8,128)S(1)}, u32[]{:S(2)}, u32[]{:S(2)}) collective-permute-start(f32[160,128]{1,0:T(8,128)S(1)} %get-tuple-element.163), channel_id=1, source_target_pairs={{0,1},{1,0},{2,3},{3,2},{4,5},{5,4},{6,7},{7,6},{8,9},{9,8},{10,11... | collective-permute-start | bytes 245768 | tf_op jit(solution)/shard_map/ppermute | solution.py:388
  68.5 4.6 %collective-permute-start.25 = (f32[160,128]{1,0:T(8,128)S(1)}, f32[160,128]{1,0:T(8,128)S(1)}, u32[]{:S(2)}, u32[]{:S(2)}) collective-permute-start(f32[160,128]{1,0:T(8,128)S(1)} %get-tuple-element.138), channel_id=1, source_target_pairs={{0,1},{1,0},{2,3},{3,2},{4,5},{5,4},{6,7},{7,6},{8,9},{9,8},{10,11... | collective-permute-start | bytes 245768 | tf_op jit(solution)/shard_map/ppermute | solution.py:388
  70.7 4.5 %collective-permute-start.13 = (f32[160,128]{1,0:T(8,128)S(1)}, f32[160,128]{1,0:T(8,128)S(1)}, u32[]{:S(2)}, u32[]{:S(2)}) collective-permute-start(f32[160,128]{1,0:T(8,128)S(1)} %get-tuple-element.113), channel_id=1, source_target_pairs={{0,1},{1,0},{2,3},{3,2},{4,5},{5,4},{6,7},{7,6},{8,9},{9,8},{10,11... | collective-permute-start | bytes 245768 | tf_op jit(solution)/shard_map/ppermute | solution.py:388
  83.8 4.5 %collective-permute-start.41 = (f32[8,128]{1,0:T(8,128)S(1)}, f32[8,128]{1,0:T(8,128)S(1)}, u32[]{:S(2)}, u32[]{:S(2)}) collective-permute-start(f32[8,128]{1,0:T(8,128)S(1)} %shard_map.170.a_ref), channel_id=1, source_target_pairs={{0,16},{2,18},{4,20},{6,22},{8,24},{10,26},{12,28},{14,30},{16,0},... | collective-permute-start | bytes 12296 | tf_op jit(solution)/shard_map/ppermute | solution.py:385
  (23 other events, 68.2 us)

commit v5 on v4

v5 whole, which is shorter than its diff:
```python
import functools
import math

import jax
import jax.numpy as jnp
import numpy as np
from jax import lax
from jax.experimental import pallas as pl
from jax.experimental.pallas import tpu as pltpu
from jax.sharding import PartitionSpec as P

KM = 4
NL = 16
NT = 64
COMPS = 3
LANES = 2 * NT
HALF = NL // 2
WAYS = 2 * (KM - 1)
HIGHEST = lax.Precision.HIGHEST
F32 = jnp.float32

SHIFT = 2.0 / 3.0

CHAINS = ((0,), (1, 2))


def weight(comp, direction):
    return 2.0 if comp == direction else 1.0


def cosine_np():
    l = np.arange(NL)
    return np.cos(math.pi * l[None, :] * (2 * l[:, None] + 1) / (2 * NL))


COS = cosine_np()


def sine_pair():
    t = np.arange(NT) + 1
    both = np.zeros((LANES, LANES))
    both[:NT, :NT] = both[NT:, NT:] = np.sin(math.pi * t[:, None] * t[None, :] / (NT + 1))
    return both.astype(np.float32)


def root_np(comp):
    lam_l = 2.0 - 2.0 * np.cos(math.pi / NL * np.arange(NL))[:, None]
    lam_t = 2.0 - 2.0 * np.cos(math.pi / (NT + 1) * (np.arange(NT) + 1))[None, :]
    norm = np.where(np.arange(NL) == 0, 1.0 * NL, 0.5 * NL)[:, None] * (0.5 * (NT + 1))
    w = weight(comp, 0)
    half = 1.0 + (weight(comp, 1) * lam_l + weight(comp, 2) * lam_t) / (2.0 * w)
    big = half + np.sqrt(half * half - 1.0)
    return 1.0 / big, 1.0 / (w * (big - 1.0 / big) * norm)


def by_core(table):
    table = table.reshape(table.shape[0], 2, HALF, LANES)
    return np.moveaxis(table, 1, 0).reshape(-1, LANES)


def power_table(comp, n_circ):
    root, _ = root_np(comp)
    powers = root[None] ** np.arange(n_circ - 6)[:, None, None]
    return by_core(np.concatenate([powers, powers], -1))


def cell_table(comp, n_circ):
    root, scale = root_np(comp)
    scale = scale / (1.0 - root**n_circ)

    def kernel(d):
        return scale * (root ** abs(d) + root ** (n_circ - abs(d)))

    out = []
    for low, high in ((0, 1), (2, 3), (4, -1)):
        for first, second in ((0, 1), (1, 0), (2, 3), (3, 2)):
            out.append(np.concatenate([kernel(low - first), kernel(high - second)], -1))
        out.append(np.concatenate([scale * root ** (3.0 - low), scale * root ** float(high)], -1))
        out.append(np.concatenate([scale * root ** float(low), scale * root ** (3.0 - high)], -1))
    return by_core(np.stack(out))


CELL_TERMS = 18


def all_tables(n_circ):
    parts = [sine_pair()]
    for comp in range(COMPS):
        parts += [power_table(comp, n_circ), cell_table(comp, n_circ)]
    return np.concatenate(parts).astype(np.float32)


class Tables:
    def __init__(self, ref, core, n_circ):
        self.ref, self.core, self.count = ref, core, n_circ - 6

    def sine(self):
        return self.ref[:LANES, :]

    def _tile(self, comp, offset, entry):
        base = LANES + comp * 2 * HALF * (self.count + CELL_TERMS) + offset
        return self.ref[pl.ds(pl.multiple_of(base + entry * HALF, HALF), HALF), :]

    def power(self, comp, a):
        return self._tile(comp, 0, self.core * self.count + a)

    def powers(self, comp, a, b):
        return jnp.where(low_lanes(HALF), self.power(comp, a), self.power(comp, b))

    def cell(self, comp, i):
        return self._tile(comp, 2 * HALF * self.count, self.core * CELL_TERMS + i)


def low_lanes(rows):
    return lax.broadcasted_iota(jnp.int32, (rows, LANES), 1) < NT


def swap_halves(x):
    return pltpu.roll(x, NT, x.ndim - 1)


def exchange_bits(x):
    rows = x.shape[0]
    even = lax.broadcasted_iota(jnp.int32, x.shape, 0) % 2 == 0
    low = low_lanes(rows)
    other = swap_halves(x)
    moved = jnp.where(even, pltpu.roll(other, rows - 1, 0), pltpu.roll(other, 1, 0))
    return jnp.where(low == even, x, moved)


def forward(fields, core, src_ref, sine, keep_ref, send_ref, rows_ref):
    plus, minus = [], []
    for l in range(HALF):
        a = src_ref[pl.ds(l, fields, stride=NL), :]
        b = src_ref[pl.ds(NL - 1 - l, fields, stride=NL), :]
        plus.append(a + b)
        minus.append(a - b)
    for m in range(NL):
        src = plus if m % 2 == 0 else minus
        acc = src[0] * float(COS[0, m])
        for l in range(1, HALF):
            acc = acc + src[l] * float(COS[l, m])
        rows_ref[pl.ds(m, fields, stride=NL), :] = acc
    rows_ref[...] = jnp.dot(rows_ref[...], sine, precision=HIGHEST, preferred_element_type=F32)
    mine = pl.multiple_of(core * HALF, HALF)
    others = pl.multiple_of((1 - core) * HALF, HALF)
    for j in range(fields):
        keep_ref[j] = rows_ref[pl.ds(j * NL + mine, HALF), :]
        send_ref[j] = rows_ref[pl.ds(j * NL + others, HALF), :]


def first_kernel(modes, comps, n_circ, me_ref, raw_ref, table_ref, keep_ref, send_ref, b_ref, rows_ref):
    core = me_ref[0] & 1
    for i, comp in enumerate(comps):
        for j in range(modes):
            at = (j * COMPS + comp) * NL
            to = (i * modes + j) * NL
            b_ref[to : to + NL, :] = exchange_bits(raw_ref[at : at + NL, :])
    sine = Tables(table_ref, core, n_circ).sine()
    forward(modes * len(comps), core, b_ref, sine, keep_ref, send_ref, rows_ref)


def next_kernel(
    fields, n_circ, me_ref, b_ref, own_ref, recv_ref, table_ref, keep_ref, send_ref, image_ref, work_ref, rows_ref
):
    core = me_ref[0] & 1
    image = own_ref[...] + recv_ref[...]
    image_ref[...] = image
    work_ref[...] = b_ref[...] - SHIFT * image
    forward(fields, core, work_ref, Tables(table_ref, core, n_circ).sine(), keep_ref, send_ref, rows_ref)


def four_cells(core, keep, recv):
    first = jnp.where(core == 0, keep, recv)
    second = jnp.where(core == 0, recv, keep)
    return first, swap_halves(first), second, swap_halves(second)


def ends_kernel(modes, comps, n_circ, me_ref, keep_ref, recv_ref, table_ref, ends_ref):
    core = me_ref[0] & 1
    tables = Tables(table_ref, core, n_circ)
    for i, comp in enumerate(comps):
        coefs = [tables.powers(comp, a, b) for a, b in ((0, 2), (1, 3), (2, 0), (3, 1))]
        for j in range(i * modes, (i + 1) * modes):
            acc = None
            for coef, cell in zip(coefs, four_cells(core, keep_ref[j], recv_ref[j])):
                acc = coef * cell if acc is None else acc + coef * cell
            ends_ref[j] = acc


def stage_kernel(modes, comps, n_circ, stage, last, me_ref, *refs):
    own_ref, recv_ref, table_ref = refs[:3]
    sum_ref = None if stage == 0 else refs[3]
    outs = refs[3 if stage == 0 else 4 :]
    core, chip = me_ref[0] & 1, me_ref[0] >> 1
    tables = Tables(table_ref, core, n_circ)
    block = 4 << stage
    bit = (chip >> stage) & 1
    place = 4 * (chip & ((1 << stage) - 1))
    right = jnp.where(bit == 0, block - 3 - place, n_circ - 3 - place - block)
    left = jnp.where(bit == 0, n_circ - 2 * block + place + 1, place + 1)
    near, far = bit * block, (1 - bit) * block
    for i, comp in enumerate(comps):
        action = tables.powers(comp, right, left)
        if not last:
            own_coef, recv_coef = tables.powers(comp, near, far), tables.powers(comp, far, near)
        for j in range(i * modes, (i + 1) * modes):
            other = recv_ref[j]
            total = action * other
            outs[0][j] = total if sum_ref is None else total + sum_ref[j]
            if not last:
                outs[1][j] = own_coef * own_ref[j] + recv_coef * other


def cells_kernel(modes, comps, n_circ, me_ref, keep_ref, recv_ref, sum_ref, table_ref, mine_ref, send_ref):
    core = me_ref[0] & 1
    tables = Tables(table_ref, core, n_circ)
    low = low_lanes(HALF)
    for i, comp in enumerate(comps):
        for j in range(i * modes, (i + 1) * modes):
            outside = sum_ref[j]
            terms = four_cells(core, keep_ref[j], recv_ref[j]) + (outside, swap_halves(outside))
            cells = []
            for group in range(3):
                acc = None
                for e, term in enumerate(terms):
                    part = tables.cell(comp, 6 * group + e) * term
                    acc = part if acc is None else acc + part
                cells.append(acc)
            near0 = jnp.where(low, cells[1], cells[2])
            near1 = jnp.where(low, cells[2], cells[0])
            mine_ref[0, j] = jnp.where(core == 0, cells[0], cells[1])
            mine_ref[1, j] = jnp.where(core == 0, near0, near1)
            send_ref[0, j] = jnp.where(core == 0, cells[1], cells[0])
            send_ref[1, j] = jnp.where(core == 0, near1, near0)


def neighbours(mid, ends, low):
    right = swap_halves(jnp.where(low, ends, mid))
    left = swap_halves(jnp.where(low, mid, ends))
    return right, left


def lane_ends(rows):
    lane = lax.broadcasted_iota(jnp.int32, (rows, LANES), 1) % NT
    return lane == 0, lane == NT - 1


def prepare_kernel(
    modes, row_ref, pair_ref, coup_ref, own_ref, left_ref, right_ref, *refs
):
    *face_refs, index_ref, coef_ref, inv_ref = refs
    total_modes = pair_ref.shape[1]
    low = low_lanes(NL)
    first, last = lane_ends(NL)
    row = lax.broadcasted_iota(jnp.int32, (NL, LANES), 0)
    for k in range(KM):
        at = slice(k * NL, (k + 1) * NL)
        a = exchange_bits(own_ref[at, :])
        ends = jnp.where(low, exchange_bits(right_ref[at, :]), exchange_bits(left_ref[at, :]))
        right, left = neighbours(a, ends, low)
        above = jnp.where(last, a, pltpu.roll(a, LANES - 1, 1))
        below = jnp.where(first, a, pltpu.roll(a, 1, 1))
        faces = [
            0.5 * (a + right),
            0.5 * (a + left),
            jnp.where(row == NL - 1, 0.0, 0.5 * (a + pltpu.roll(a, NL - 1, 0))),
            jnp.where(row == 0, 0.0, 0.5 * (a + pltpu.roll(a, 1, 0))),
            0.5 * (a + above),
            0.5 * (a + below),
        ]
        for comp in range(COMPS):
            for nb in range(6):
                w = weight(comp, nb // 2)
                face_refs[comp][k, nb] = faces[nb] * w if w != 1.0 else faces[nb]

    for k in range(KM - 1):
        for j in range(total_modes):
            inv_ref[k, pair_ref[k, j]] = j
    for k in range(KM - 1):
        for i in range(total_modes):
            for way in range(2):
                partner = pair_ref[k, i] if way == 0 else inv_ref[k, i]
                coef = 0.5 * (coup_ref[k, i] if way == 0 else coup_ref[k, partner])
                local = partner - row_ref[0]
                inside = jnp.logical_and(local >= 0, local < modes)
                coef_ref[2 * k + way, i] = jnp.where(inside, coef, 0.0)
                index_ref[2 * k + way, i] = jnp.clip(local, 0, modes - 1)


def operator_kernel(modes, total_modes, comps, n_circ, me_ref, row_ref, index_ref, coef_ref, keep_ref, recv_ref, table_ref, *refs):
    face_refs = refs[: len(comps)]
    field_ref, own_ref, cross_ref, spec_ref, ends_ref, term_ref = refs[len(comps) :]
    fields = modes * len(comps)
    core = me_ref[0] & 1
    sine = Tables(table_ref, core, n_circ).sine()
    mine = pl.multiple_of(core * HALF, HALF)
    others = pl.multiple_of((1 - core) * HALF, HALF)
    for part in range(2):
        for j in range(fields):
            spec_ref[part, pl.ds(j * NL + mine, HALF), :] = keep_ref[part, j]
            spec_ref[part, pl.ds(j * NL + others, HALF), :] = recv_ref[part, j]
    for part in range(2):
        spec_ref[part] = jnp.dot(spec_ref[part], sine, precision=HIGHEST, preferred_element_type=F32)
    for part in range(2):
        dst = field_ref if part == 0 else ends_ref
        y = [spec_ref[part, pl.ds(m, fields, stride=NL), :] for m in range(NL)]
        for l in range(HALF):
            even = y[0] * float(COS[l, 0])
            odd = y[1] * float(COS[l, 1])
            for m in range(2, NL, 2):
                even = even + y[m] * float(COS[l, m])
                odd = odd + y[m + 1] * float(COS[l, m + 1])
            dst[pl.ds(l, fields, stride=NL), :] = even + odd
            dst[pl.ds(NL - 1 - l, fields, stride=NL), :] = even - odd
    low = low_lanes(NL)
    first, last = lane_ends(NL)
    for j in range(fields):
        face_ref = face_refs[j // modes]
        at = slice(j * NL, (j + 1) * NL)
        mid = field_ref[at, :]
        right, left = neighbours(mid, ends_ref[at, :], low)
        diffs = [
            mid - right,
            mid - left,
            mid - pltpu.roll(mid, NL - 1, 0),
            mid - pltpu.roll(mid, 1, 0),
            mid - jnp.where(last, 0.0, pltpu.roll(mid, LANES - 1, 1)),
            mid - jnp.where(first, 0.0, pltpu.roll(mid, 1, 1)),
        ]
        for k in range(KM):
            acc = face_ref[k, 0] * diffs[0]
            for nb in range(1, 6):
                acc = acc + face_ref[k, nb] * diffs[nb]
            term_ref[k, j % modes, (j // modes) * NL : (j // modes + 1) * NL, :] = acc
    row_start = row_ref[0]
    other_start = total_modes - modes - row_start

    def mixed(i, acc):
        for e in range(WAYS):
            part = coef_ref[e, i] * term_ref[1 + e // 2, index_ref[e, i]]
            acc = part if acc is None else acc + part
        return acc

    def put(dst, i, value):
        for c in range(len(comps)):
            dst[(c * modes + i) * NL : (c * modes + i + 1) * NL, :] = value[c * NL : (c + 1) * NL, :]

    for i in range(modes):
        put(cross_ref, i, mixed(other_start + i, None))
    for i in range(modes):
        put(own_ref, i, mixed(row_start + i, term_ref[0, i]))


def sums_kernel(rows, b_ref, u_ref, v_ref, z_ref, own_ref, recv_ref, *refs):
    *before, image_ref, part_ref = refs
    q = own_ref[...] + recv_ref[...]
    image_ref[...] = q
    b, u, v, z = b_ref[...], u_ref[...], v_ref[...], z_ref[...]

    def fold(x):
        x = jnp.sum(x.reshape(rows // 8, 8, LANES), axis=0)
        return jnp.sum(x, axis=0, keepdims=True)

    sums = [fold(b * u), fold(u * v), fold(v * z), fold(b * z), fold(z * q), jnp.zeros((3, LANES), F32)]
    part = jnp.concatenate(sums, axis=0)
    if before:
        part = part + before[0][...]
    if part_ref.shape == part.shape:
        part_ref[...] = part
    else:
        for i in range(part_ref.shape[0]):
            part_ref[i] = part


def final_kernel(modes, chains, parts_ref, *refs):
    *fields, x_ref, r_ref = refs
    total = jnp.sum(jnp.sum(parts_ref[...], axis=0), axis=1, keepdims=True)
    bu, uv, vz, bz, zq = (total[i : i + 1, :] for i in range(5))
    a0 = bu / uv
    t = vz / uv
    c1 = (bz - a0 * vz) / (zq - t * vz)
    c0 = a0 - c1 * t
    for n, comps in enumerate(chains):
        rhs_ref, u_ref, v_ref, z_ref, q_ref = fields[5 * n : 5 * n + 5]
        for i, comp in enumerate(comps):
            for j in range(modes):
                at = slice((i * modes + j) * NL, (i * modes + j + 1) * NL)
                to = (j * COMPS + comp) * NL
                x_ref[to : to + NL, :] = exchange_bits(c0 * u_ref[at, :] + c1 * z_ref[at, :])
                r_ref[to : to + NL, :] = exchange_bits(rhs_ref[at, :] - c0 * v_ref[at, :] - c1 * q_ref[at, :])


def struct(*shape, dtype=F32):
    return jax.ShapeDtypeStruct(shape, dtype)


def call(kernel, out_shape, *args, scalars=0, scalar_outs=0, scratch_shapes=()):
    vmem, smem = pl.BlockSpec(memory_space=pltpu.VMEM), pl.BlockSpec(memory_space=pltpu.SMEM)
    size = 4 * sum(math.prod(a.shape) for a in list(args) + list(out_shape))
    return pl.pallas_call(
        kernel,
        out_shape=out_shape,
        in_specs=[smem] * scalars + [vmem] * (len(args) - scalars),
        out_specs=[vmem] * (len(out_shape) - scalar_outs) + [smem] * scalar_outs,
        scratch_shapes=scratch_shapes,
        compiler_params=pltpu.CompilerParams(vmem_limit_bytes=32 * 1024 * 1024),
        cost_estimate=pl.CostEstimate(flops=4 * size, bytes_accessed=size, transcendentals=0),
    )(*args)


def on_device(right_side, stiffness, pairing, coupling):
    modes, comps, local_circ, num_cells = right_side.shape
    circ = lax.axis_size("circ")
    total_modes = pairing.shape[1]
    n_circ = local_circ * circ
    stages = (circ // 2).bit_length() - 1

    def raw(values, count):
        values = values.reshape(count, local_circ, num_cells // LANES, LANES)
        return jnp.swapaxes(values, 1, 2).reshape(count * NL, LANES)

    def partner(values, d):
        return lax.ppermute(values, "circ", [(i, i ^ d) for i in range(circ)])

    def other_block(values):
        return lax.ppermute(values, "mode", [(0, 1), (1, 0)])

    table = jnp.asarray(all_tables(n_circ))
    row_start = (lax.axis_index("mode") * modes).astype(jnp.int32).reshape(1)
    me = lax.axis_index("circ").astype(jnp.int32).reshape(1)
    sizes = [modes * len(comps) for comps in CHAINS]
    half = [struct(size, HALF, LANES) for size in sizes]
    pairs = [struct(2, size, HALF, LANES) for size in sizes]
    column = [struct(size * NL, LANES) for size in sizes]
    each = range(len(CHAINS))

    stiff = raw(stiffness, KM)
    stiff_l = lax.ppermute(stiff, "circ", [(i, (i + 1) % circ) for i in range(circ)])
    stiff_r = lax.ppermute(stiff, "circ", [((i + 1) % circ, i) for i in range(circ)])
    *faces, index, coef = call(
        functools.partial(prepare_kernel, modes),
        [struct(KM, 6, NL, LANES)] * COMPS + [struct(WAYS, total_modes, dtype=jnp.int32), struct(WAYS, total_modes)],
        row_start, pairing, coupling, stiff, stiff_l, stiff_r,
        scalars=3, scalar_outs=2,
        scratch_shapes=[pltpu.SMEM((KM - 1, total_modes), jnp.int32)],
    )

    def round_trip(keep, send, hold=None):
        recv = [partner(send[c], 1) for c in each]
        ends = [
            call(
                functools.partial(ends_kernel, modes, CHAINS[c], n_circ), [half[c]], me, keep[c], recv[c], table, scalars=1
            )[0]
            for c in each
        ]
        total = [()] * len(CHAINS)
        for stage in range(stages):
            last = stage == stages - 1
            other = [partner(ends[c], 2 << stage) for c in each]
            if hold is not None and stage == 1:
                other[-1], hold = lax.optimization_barrier((other[-1], hold))
            done = [
                call(
                    functools.partial(stage_kernel, modes, CHAINS[c], n_circ, stage, last),
                    [half[c]] if last else [half[c]] * 2,
                    me, ends[c], other[c], table, *total[c],
                    scalars=1,
                )
                for c in each
            ]
            total = [done[c][:1] for c in each]
            ends = [done[c][-1] for c in each]
        done = [
            call(
                functools.partial(cells_kernel, modes, CHAINS[c], n_circ),
                [pairs[c]] * 2,
                me, keep[c], recv[c], *total[c], table,
                scalars=1,
            )
            for c in each
        ]
        return [(done[c][0], partner(done[c][1], 1)) for c in each], hold

    def operate(spec, index, coef, faces):
        done = [
            call(
                functools.partial(operator_kernel, modes, total_modes, CHAINS[c], n_circ),
                [column[c]] * 3,
                me, row_start, index, coef, *spec[c], table, *[faces[i] for i in CHAINS[c]],
                scalars=4,
                scratch_shapes=[
                    pltpu.VMEM((2, sizes[c] * NL, LANES), F32),
                    pltpu.VMEM((sizes[c] * NL, LANES), F32),
                    pltpu.VMEM((KM, modes, len(CHAINS[c]) * NL, LANES), F32),
                ],
            )
            for c in each
        ]
        field, own, cross = zip(*done)
        return field, own, [other_block(cross[c]) for c in each]

    source = raw(right_side, modes * comps)
    keep, send, b = zip(*[
        call(
            functools.partial(first_kernel, modes, CHAINS[c], n_circ),
            [half[c], half[c], column[c]],
            me, source, table,
            scalars=1, scratch_shapes=[pltpu.VMEM((sizes[c] * NL, LANES), F32)],
        )
        for c in each
    ])
    spec, hold = round_trip(keep, send, (index, coef, faces))
    u, own, recv = operate(spec, *hold)
    keep, send, v = zip(*[
        call(
            functools.partial(next_kernel, sizes[c], n_circ),
            [half[c], half[c], column[c]],
            me, b[c], own[c], recv[c], table,
            scalars=1, scratch_shapes=[pltpu.VMEM((sizes[c] * NL, LANES), F32)] * 2,
        )
        for c in each
    ])
    spec, _ = round_trip(keep, send)
    z, own, recv = operate(spec, *hold)
    devices = circ * lax.axis_size("mode")
    q, before = [], ()
    for c in each:
        shape = struct(devices, 8, LANES) if c == each[-1] else struct(8, LANES)
        image, part = call(
            functools.partial(sums_kernel, sizes[c] * NL), [column[c], shape], b[c], u[c], v[c], z[c], own[c], recv[c], *before
        )
        q.append(image)
        before = (part,)
    parts = lax.all_to_all(part, ("circ", "mode"), split_axis=0, concat_axis=0)
    x, r = call(
        functools.partial(final_kernel, modes, CHAINS),
        [struct(modes * comps * NL, LANES)] * 2,
        parts, *[values for c in each for values in (b[c], u[c], v[c], z[c], q[c])],
    )

    def give(values):
        values = values.reshape(modes * comps, num_cells // LANES, local_circ, LANES)
        return jnp.swapaxes(values, 1, 2).reshape(right_side.shape)

    return give(x), give(r)


def solution(mesh):
    placed = (P("mode", None, "circ", None), P(None, "circ", None), P(), P())
    return jax.shard_map(
        on_device,
        mesh=mesh,
        in_specs=placed,
        out_specs=(P("mode", None, "circ", None), P("mode", None, "circ", None)),
        check_vma=False,
    )
```

time: 93.2 us -> 101 us (1.084)
  waiting for transfers between devices: 29.2 us -> 48.9 us
  starting transfers between devices: 40.4 us -> 22.2 us
  blocking collectives: 0 us -> 12.6 us
  Pallas kernels: 17.2 us -> 13.7 us
  local copies, waits for them, and re-layouts: 5.04 us -> 2.22 us
    ppermute x34 -> x20, waiting for transfers between devices: 20.5 us -> 37.3 us  [partner(): return lax.ppermute(values, 'circ', [(i, i ^ d) for i in range(circ)])]
    ppermute x34 -> x20, starting transfers between devices: 27.1 us -> 12.5 us  [partner(): return lax.ppermute(values, 'circ', [(i, i ^ d) for i in range(circ)])]
    all_to_all x0 -> x1, blocking collectives: none -> 12.6 us  [on_device(): parts = lax.all_to_all(part, ('circ', 'mode'), split_axis=0, concat_axis=0)]
    ppermute x7 -> x4, starting transfers between devices: 8.89 us -> 5.27 us  [other_block(): return lax.ppermute(values, 'mode', [(0, 1), (1, 0)])]
    pallas_call x51 -> x32, Pallas kernels: 17.2 us -> 13.7 us  [call(): pl.pallas_call(kernel, out_shape=out_shape, in_specs=[smem] * scalars + [...]
    ppermute x7 -> x4, waiting for transfers between devices: 7.04 us -> 9.9 us  [other_block(): return lax.ppermute(values, 'mode', [(0, 1), (1, 0)])]
    unnamed x24 -> x14, local copies, waits for them, and re-layouts: 5.04 us -> 2.22 us
  transfers between devices with their start and end apart: 43 -> 26, of which waited for: 20 -> 17; matrix products, arithmetic and copies ran while one was open for 0% -> 0% of each run, Pallas kernels for 17% -> 9%
where the time goes in v5:
time: 101 us
  waiting for transfers between devices  48.9 us (48%)
  starting transfers between devices  22.2 us (22%)
  Pallas kernels  13.7 us (14%)
  blocking collectives  12.6 us (12%)
  local copies, waits for them, and re-layouts  2.22 us (2%)
    ppermute x20, waiting for transfers between devices, partner(): return lax.ppermute(values, 'circ', [(i, i ^ d) for i in range(circ)])  37.3 us
    pallas_call x32, Pallas kernels, call(): pl.pallas_call(kernel, out_shape=out_shape, in_specs=[smem] * scalars + [...  13.7 us
    all_to_all x1, blocking collectives, on_device(): parts = lax.all_to_all(part, ('circ', 'mode'), split_axis=0, concat_axis=0)  12.6 us
    ppermute x20, starting transfers between devices, partner(): return lax.ppermute(values, 'circ', [(i, i ^ d) for i in range(circ)])  12.5 us
    ppermute x4, waiting for transfers between devices, other_block(): return lax.ppermute(values, 'mode', [(0, 1), (1, 0)])  9.9 us
    ppermute x4, starting transfers between devices, other_block(): return lax.ppermute(values, 'mode', [(0, 1), (1, 0)])  5.27 us
    ppermute x1, starting transfers between devices, on_device(): lax.ppermute(stiff, 'circ', [((i + 1) % circ, i) for i in range(circ)])  4.44 us
    unnamed x14, local copies, waits for them, and re-layouts  2.22 us
  transfers between devices with their start and end apart: 26, of which 17 were waited for; matrix products, arithmetic and copies ran while one was open for 0% of the time, Pallas kernels for 9%

profile of v5, /device:TPU:0, one launch (start us, length us, event | category | flops | bytes accessed | tf_op | source)
XLA Modules:
  0.0 100.7 jit_solution(18230205958217831768)
XLA Ops:
  0.6 1.2 %copy-done = f32[2240,128]{1,0:T(8,128)S(1)} copy-done((f32[2240,128]{1,0:T(8,128)S(1)}, f32[2240,128]{1,0:T(8,128)}, u32[]{:S(2)}) %copy-start) | copy-done | bytes 1146904
  5.0 2.9 %collective-permute-start.1 = (f32[20,8,128]{2,1,0:T(8,128)S(1)}, f32[20,8,128]{2,1,0:T(8,128)S(1)}, u32[]{:S(2)}, u32[]{:S(2)}) collective-permute-start(f32[20,8,128]{2,1,0:T(8,128)S(1)} %shard_map.69.refs_0_), channel_id=1, source_target_pairs={{0,4},{2,6},{4,0},{6,2},{8,12},{10,14},{12,8},{14,10},{16,20},{18,... | collective-permute-start | bytes 245768 | tf_op jit(solution)/shard_map/ppermute | solution.py:424
  8.0 2.8 %collective-permute-done.1.refs_1_ = f32[20,8,128]{2,1,0:T(8,128)S(1)} collective-permute-done((f32[20,8,128]{2,1,0:T(8,128)S(1)}, f32[20,8,128]{2,1,0:T(8,128)S(1)}, u32[]{:S(2)}, u32[]{:S(2)}) %collective-permute-start.1) | collective-permute-done | bytes 81952 | tf_op jit(solution)/shard_map/ppermute | solution.py:424
  10.8 1.9 %collective-permute-start.2 = (f32[20,8,128]{2,1,0:T(8,128)S(1)}, f32[20,8,128]{2,1,0:T(8,128)S(1)}, u32[]{:S(2)}, u32[]{:S(2)}) collective-permute-start(f32[20,8,128]{2,1,0:T(8,128)S(1)} %get-tuple-element.70.refs_0_), channel_id=1, source_target_pairs={{0,8},{2,10},{4,12},{6,14},{8,0},{10,2},{12,4},{14,6},{16,24},{18,... | collective-permute-start | bytes 245768 | tf_op jit(solution)/shard_map/ppermute | solution.py:424
  12.6 4.4 %collective-permute-start.4 = (f32[64,128]{1,0:T(8,128)S(1)}, f32[64,128]{1,0:T(8,128)S(1)}, u32[]{:S(2)}, u32[]{:S(2)}) collective-permute-start(f32[64,128]{1,0:T(8,128)S(1)} %bitcast.25), channel_id=1, source_target_pairs={{2,0},{4,2},{6,4},{8,6},{10,8},{12,10},{14,12},{16,14},{18,16},{20... | collective-permute-start | bytes 98312 | tf_op jit(solution)/shard_map/ppermute | solution.py:440
  17.1 1.8 %collective-permute-done.3.left_ref = f32[64,128]{1,0:T(8,128)S(1)} collective-permute-done((f32[64,128]{1,0:T(8,128)S(1)}, f32[64,128]{1,0:T(8,128)S(1)}, u32[]{:S(2)}, u32[]{:S(2)}) %collective-permute-start.3) | collective-permute-done | bytes 32800 | tf_op jit(solution)/shard_map/ppermute | solution.py:439
  18.8 2.0 %shard_map.71 = (f32[4,6,16,128]{3,2,1,0:T(8,128)S(1)}, f32[4,6,16,128]{3,2,1,0:T(8,128)S(1)}, f32[4,6,16,128]{3,2,1,0:T(8,128)S(1)}, s32[6,20]{1,0:T(8,128)S(1)}, f32[6,20]{1,0:T(8,128)S(1)}) custom-call(s32[1]{0:T(128)} %bitcast.4.row_ref, s32[3,20]{1,0:T(4,128)S(1)} %copy-done.5, f32[3,20]{1,0:T(4,128)S(1)} %copy-done.6, f32[64,128]{1,0:T(8,128)S(1)} %bitcast.26, ...), custom_call_target="tpu_custom_call" | custom-call | flops 2758288 | bytes 689572 | tf_op jit(solution)/shard_map/pallas_call | solution.py:401
  21.6 5.0 %collective-permute-done.5.refs_1_ = f32[20,8,128]{2,1,0:T(8,128)S(1)} collective-permute-done((f32[20,8,128]{2,1,0:T(8,128)S(1)}, f32[20,8,128]{2,1,0:T(8,128)S(1)}, u32[]{:S(2)}, u32[]{:S(2)}) %collective-permute-start.5) | collective-permute-done | bytes 81952 | tf_op jit(solution)/shard_map/ppermute | solution.py:424
  26.9 1.4 %collective-permute-done.6.recv_ref = f32[2,20,8,128]{3,2,1,0:T(8,128)S(1)} collective-permute-done((f32[2,20,8,128]{3,2,1,0:T(8,128)S(1)}, f32[2,20,8,128]{3,2,1,0:T(8,128)S(1)}, u32[]{:S(2)}, u32[]{:S(2)}) %collective-permute-start.6) | collective-permute-done | bytes 163872 | tf_op jit(solution)/shard_map/ppermute | solution.py:424
  28.3 2.1 %shard_map.75 = (f32[320,128]{1,0:T(8,128)S(1)}, f32[320,128]{1,0:T(8,128)S(1)}, f32[320,128]{1,0:T(8,128)S(1)}) custom-call(s32[1]{0:T(128)} %bitcast.me_ref, s32[1]{0:T(128)} %bitcast.4.row_ref, s32[6,20]{1,0:T(8,128)S(1)} %get-tuple-element.76.index_ref, f32[6,20]{1,0:T(8,128)S(1)} %get-tuple-element.77.coef_ref, ...), custom_call_target="tpu_custom_call" | custom-call | flops 9441056 | bytes 2360264 | tf_op jit(solution)/shard_map/pallas_call | solution.py:401
  30.4 1.6 %collective-permute-start.7 = (f32[320,128]{1,0:T(8,128)S(1)}, f32[320,128]{1,0:T(8,128)S(1)}, u32[]{:S(2)}, u32[]{:S(2)}) collective-permute-start(f32[320,128]{1,0:T(8,128)S(1)} %get-tuple-element.88), channel_id=1, source_target_pairs={{0,1},{1,0},{2,3},{3,2},{4,5},{5,4},{6,7},{7,6},{8,9},{9,8},{10,11... | collective-permute-start | bytes 491528 | tf_op jit(solution)/shard_map/ppermute | solution.py:427
  32.4 4.2 %collective-permute-done.7.recv_ref = f32[320,128]{1,0:T(8,128)S(1)} collective-permute-done((f32[320,128]{1,0:T(8,128)S(1)}, f32[320,128]{1,0:T(8,128)S(1)}, u32[]{:S(2)}, u32[]{:S(2)}) %collective-permute-start.7) | collective-permute-done | bytes 163872 | tf_op jit(solution)/shard_map/ppermute | solution.py:427
  37.5 3.9 %collective-permute-done.15.refs_1_ = f32[10,8,128]{2,1,0:T(8,128)S(1)} collective-permute-done((f32[10,8,128]{2,1,0:T(8,128)S(1)}, f32[10,8,128]{2,1,0:T(8,128)S(1)}, u32[]{:S(2)}, u32[]{:S(2)}) %collective-permute-start.15) | collective-permute-done | bytes 40992 | tf_op jit(solution)/shard_map/ppermute | solution.py:424
  41.7 1.6 %collective-permute-start.9 = (f32[20,8,128]{2,1,0:T(8,128)S(1)}, f32[20,8,128]{2,1,0:T(8,128)S(1)}, u32[]{:S(2)}, u32[]{:S(2)}) collective-permute-start(f32[20,8,128]{2,1,0:T(8,128)S(1)} %shard_map.77.refs_0_), channel_id=1, source_target_pairs={{0,4},{2,6},{4,0},{6,2},{8,12},{10,14},{12,8},{14,10},{16,20},{18,... | collective-permute-start | bytes 245768 | tf_op jit(solution)/shard_map/ppermute | solution.py:424
  43.3 2.3 %collective-permute-done.16.refs_1_ = f32[10,8,128]{2,1,0:T(8,128)S(1)} collective-permute-done((f32[10,8,128]{2,1,0:T(8,128)S(1)}, f32[10,8,128]{2,1,0:T(8,128)S(1)}, u32[]{:S(2)}, u32[]{:S(2)}) %collective-permute-start.16) | collective-permute-done | bytes 40992 | tf_op jit(solution)/shard_map/ppermute | solution.py:424
  45.6 1.2 %collective-permute-start.17 = (f32[10,8,128]{2,1,0:T(8,128)S(1)}, f32[10,8,128]{2,1,0:T(8,128)S(1)}, u32[]{:S(2)}, u32[]{:S(2)}) collective-permute-start(f32[10,8,128]{2,1,0:T(8,128)S(1)} %get-tuple-element.106.refs_0_), channel_id=1, source_target_pairs={{0,16},{2,18},{4,20},{6,22},{8,24},{10,26},{12,28},{14,30},{16,0},... | collective-permute-start | bytes 122888 | tf_op jit(solution)/shard_map/ppermute | solution.py:424
  46.8 3.9 %collective-permute-done.17.refs_1_ = f32[10,8,128]{2,1,0:T(8,128)S(1)} collective-permute-done((f32[10,8,128]{2,1,0:T(8,128)S(1)}, f32[10,8,128]{2,1,0:T(8,128)S(1)}, u32[]{:S(2)}, u32[]{:S(2)}) %collective-permute-start.17) | collective-permute-done | bytes 40992 | tf_op jit(solution)/shard_map/ppermute | solution.py:424
  52.1 1.6 %shard_map.89 = (f32[160,128]{1,0:T(8,128)S(1)}, f32[160,128]{1,0:T(8,128)S(1)}, f32[160,128]{1,0:T(8,128)S(1)}) custom-call(s32[1]{0:T(128)} %bitcast.me_ref, s32[1]{0:T(128)} %bitcast.4.row_ref, s32[6,20]{1,0:T(8,128)S(1)} %get-tuple-element.76.index_ref, f32[6,20]{1,0:T(8,128)S(1)} %get-tuple-element.77.coef_ref, ...), custom_call_target="tpu_custom_call" | custom-call | flops 7016224 | bytes 1754056 | tf_op jit(solution)/shard_map/pallas_call | solution.py:401
  53.7 1.6 %collective-permute-start.19 = (f32[160,128]{1,0:T(8,128)S(1)}, f32[160,128]{1,0:T(8,128)S(1)}, u32[]{:S(2)}, u32[]{:S(2)}) collective-permute-start(f32[160,128]{1,0:T(8,128)S(1)} %get-tuple-element.113), channel_id=1, source_target_pairs={{0,1},{1,0},{2,3},{3,2},{4,5},{5,4},{6,7},{7,6},{8,9},{9,8},{10,11... | collective-permute-start | bytes 245768 | tf_op jit(solution)/shard_map/ppermute | solution.py:427
  55.8 1.5 %collective-permute-start.11 = (f32[20,8,128]{2,1,0:T(8,128)S(1)}, f32[20,8,128]{2,1,0:T(8,128)S(1)}, u32[]{:S(2)}, u32[]{:S(2)}) collective-permute-start(f32[20,8,128]{2,1,0:T(8,128)S(1)} %get-tuple-element.94.refs_0_), channel_id=1, source_target_pairs={{0,16},{2,18},{4,20},{6,22},{8,24},{10,26},{12,28},{14,30},{16,0},... | collective-permute-start | bytes 245768 | tf_op jit(solution)/shard_map/ppermute | solution.py:424
  57.3 1.0 %collective-permute-done.19.recv_ref = f32[160,128]{1,0:T(8,128)S(1)} collective-permute-done((f32[160,128]{1,0:T(8,128)S(1)}, f32[160,128]{1,0:T(8,128)S(1)}, u32[]{:S(2)}, u32[]{:S(2)}) %collective-permute-start.19) | collective-permute-done | bytes 81952 | tf_op jit(solution)/shard_map/ppermute | solution.py:427
  58.8 3.8 %collective-permute-done.11.refs_1_ = f32[20,8,128]{2,1,0:T(8,128)S(1)} collective-permute-done((f32[20,8,128]{2,1,0:T(8,128)S(1)}, f32[20,8,128]{2,1,0:T(8,128)S(1)}, u32[]{:S(2)}, u32[]{:S(2)}) %collective-permute-start.11) | collective-permute-done | bytes 81952 | tf_op jit(solution)/shard_map/ppermute | solution.py:424
  63.2 3.9 %collective-permute-done.21.refs_1_ = f32[10,8,128]{2,1,0:T(8,128)S(1)} collective-permute-done((f32[10,8,128]{2,1,0:T(8,128)S(1)}, f32[10,8,128]{2,1,0:T(8,128)S(1)}, u32[]{:S(2)}, u32[]{:S(2)}) %collective-permute-start.21) | collective-permute-done | bytes 40992 | tf_op jit(solution)/shard_map/ppermute | solution.py:424
  67.1 4.0 %collective-permute-done.22.refs_1_ = f32[10,8,128]{2,1,0:T(8,128)S(1)} collective-permute-done((f32[10,8,128]{2,1,0:T(8,128)S(1)}, f32[10,8,128]{2,1,0:T(8,128)S(1)}, u32[]{:S(2)}, u32[]{:S(2)}) %collective-permute-start.22) | collective-permute-done | bytes 40992 | tf_op jit(solution)/shard_map/ppermute | solution.py:424
  71.1 1.1 %collective-permute-start.23 = (f32[10,8,128]{2,1,0:T(8,128)S(1)}, f32[10,8,128]{2,1,0:T(8,128)S(1)}, u32[]{:S(2)}, u32[]{:S(2)}) collective-permute-start(f32[10,8,128]{2,1,0:T(8,128)S(1)} %get-tuple-element.119.refs_0_), channel_id=1, source_target_pairs={{0,16},{2,18},{4,20},{6,22},{8,24},{10,26},{12,28},{14,30},{16,0},... | collective-permute-start | bytes 122888 | tf_op jit(solution)/shard_map/ppermute | solution.py:424
  72.2 3.9 %collective-permute-done.23.refs_1_ = f32[10,8,128]{2,1,0:T(8,128)S(1)} collective-permute-done((f32[10,8,128]{2,1,0:T(8,128)S(1)}, f32[10,8,128]{2,1,0:T(8,128)S(1)}, u32[]{:S(2)}, u32[]{:S(2)}) %collective-permute-start.23) | collective-permute-done | bytes 40992 | tf_op jit(solution)/shard_map/ppermute | solution.py:424
  76.3 2.1 %shard_map.82 = (f32[320,128]{1,0:T(8,128)S(1)}, f32[320,128]{1,0:T(8,128)S(1)}, f32[320,128]{1,0:T(8,128)S(1)}) custom-call(s32[1]{0:T(128)} %bitcast.me_ref, s32[1]{0:T(128)} %bitcast.4.row_ref, s32[6,20]{1,0:T(8,128)S(1)} %get-tuple-element.76.index_ref, f32[6,20]{1,0:T(8,128)S(1)} %get-tuple-element.77.coef_ref, ...), custom_call_target="tpu_custom_call" | custom-call | flops 9441056 | bytes 2360264 | tf_op jit(solution)/shard_map/pallas_call | solution.py:401
  78.4 1.5 %collective-permute-start.13 = (f32[320,128]{1,0:T(8,128)S(1)}, f32[320,128]{1,0:T(8,128)S(1)}, u32[]{:S(2)}, u32[]{:S(2)}) collective-permute-start(f32[320,128]{1,0:T(8,128)S(1)} %get-tuple-element.100), channel_id=1, source_target_pairs={{0,1},{1,0},{2,3},{3,2},{4,5},{5,4},{6,7},{7,6},{8,9},{9,8},{10,11... | collective-permute-start | bytes 491528 | tf_op jit(solution)/shard_map/ppermute | solution.py:427
  79.9 1.6 %shard_map.96 = (f32[160,128]{1,0:T(8,128)S(1)}, f32[160,128]{1,0:T(8,128)S(1)}, f32[160,128]{1,0:T(8,128)S(1)}) custom-call(s32[1]{0:T(128)} %bitcast.me_ref, s32[1]{0:T(128)} %bitcast.4.row_ref, s32[6,20]{1,0:T(8,128)S(1)} %get-tuple-element.76.index_ref, f32[6,20]{1,0:T(8,128)S(1)} %get-tuple-element.77.coef_ref, ...), custom_call_target="tpu_custom_call" | custom-call | flops 7016224 | bytes 1754056 | tf_op jit(solution)/shard_map/pallas_call | solution.py:401
  82.2 4.6 %collective-permute-done.25.recv_ref = f32[160,128]{1,0:T(8,128)S(1)} collective-permute-done((f32[160,128]{1,0:T(8,128)S(1)}, f32[160,128]{1,0:T(8,128)S(1)}, u32[]{:S(2)}, u32[]{:S(2)}) %collective-permute-start.25) | collective-permute-done | bytes 81952 | tf_op jit(solution)/shard_map/ppermute | solution.py:427
  87.0 12.6 %all_to_all.5.parts_ref = f32[32,8,128]{2,1,0:T(8,128)S(1)} all-to-all(f32[32,8,128]{2,1,0:T(8,128)S(1)} %get-tuple-element.127), channel_id=1, replica_groups=mesh['circ'=16,'mode'=2] {'circ','mode'}, dimensions={0} | all-to-all | bytes 262144 | tf_op jit(solution)/shard_map/all_to_all | solution.py:535
  99.6 1.1 %shard_map.99 = (f32[480,128]{1,0:T(8,128)}, f32[480,128]{1,0:T(8,128)}) custom-call(f32[32,8,128]{2,1,0:T(8,128)S(1)} %all_to_all.5.parts_ref, f32[160,128]{1,0:T(8,128)S(1)} %get-tuple-element.101.b_ref.refs_0_, f32[160,128]{1,0:T(8,128)S(1)} %get-tuple-element.111.u_ref.refs_1_, f32[160,128]{1,0:T(8,128)S(1)} %get-tuple-element.114.v_ref.refs_2_, ...), custom_call_target="tpu_custom_call" | custom-call | flops 7405568 | bytes 1851392 | tf_op jit(solution)/shard_map/pallas_call | solution.py:401
  (67 shorter events, 9.8 us)
Async XLA Ops:
  0.6 1.3 %copy-start = (f32[2240,128]{1,0:T(8,128)S(1)}, f32[2240,128]{1,0:T(8,128)}, u32[]{:S(2)}) copy-start(f32[2240,128]{1,0:T(8,128)} %constant.12.clone.table_ref.refs_2_) | copy-start | bytes 3440644
  2.8 2.0 %copy-start.1 = (f32[2240,128]{1,0:T(8,128)S(1)}, f32[2240,128]{1,0:T(8,128)}, u32[]{:S(2)}) copy-start(f32[2240,128]{1,0:T(8,128)} %constant.12.clone.table_ref.refs_2_) | copy-start | bytes 3440644
  3.4 1.4 %collective-permute-start = (f32[20,8,128]{2,1,0:T(8,128)S(1)}, f32[20,8,128]{2,1,0:T(8,128)S(1)}, u32[]{:S(2)}, u32[]{:S(2)}) collective-permute-start(f32[20,8,128]{2,1,0:T(8,128)S(1)} %get-tuple-element.69), channel_id=1, source_target_pairs={{0,2},{2,0},{4,6},{6,4},{8,10},{10,8},{12,14},{14,12},{16,18},{18,... | collective-permute-start | bytes 245768 | tf_op jit(solution)/shard_map/ppermute | solution.py:424
  4.9 7.7 %copy-start.4 = (f32[4,2,1024]{2,1,0:T(2,128)S(1)}, f32[4,2,1024]{2,1,0:T(2,128)}, u32[]{:S(2)}) copy-start(f32[4,2,1024]{2,1,0:T(2,128)} %param.6) | copy-start | bytes 98308
  4.9 13.9 %copy-start.5 = (s32[3,20]{1,0:T(4,128)S(1)}, s32[3,20]{1,0:T(4,128)}, u32[]{:S(2)}) copy-start(s32[3,20]{1,0:T(4,128)} %pair_ref.1) | copy-start | bytes 724
  4.9 13.9 %copy-start.6 = (f32[3,20]{1,0:T(4,128)S(1)}, f32[3,20]{1,0:T(4,128)}, u32[]{:S(2)}) copy-start(f32[3,20]{1,0:T(4,128)} %coup_ref.1) | copy-start | bytes 724
  5.0 5.7 %collective-permute-start.1 = (f32[20,8,128]{2,1,0:T(8,128)S(1)}, f32[20,8,128]{2,1,0:T(8,128)S(1)}, u32[]{:S(2)}, u32[]{:S(2)}) collective-permute-start(f32[20,8,128]{2,1,0:T(8,128)S(1)} %shard_map.69.refs_0_), channel_id=1, source_target_pairs={{0,4},{2,6},{4,0},{6,2},{8,12},{10,14},{12,8},{14,10},{16,20},{18,... | collective-permute-start | bytes 245768 | tf_op jit(solution)/shard_map/ppermute | solution.py:424
  10.8 10.1 %collective-permute-start.2 = (f32[20,8,128]{2,1,0:T(8,128)S(1)}, f32[20,8,128]{2,1,0:T(8,128)S(1)}, u32[]{:S(2)}, u32[]{:S(2)}) collective-permute-start(f32[20,8,128]{2,1,0:T(8,128)S(1)} %get-tuple-element.70.refs_0_), channel_id=1, source_target_pairs={{0,8},{2,10},{4,12},{6,14},{8,0},{10,2},{12,4},{14,6},{16,24},{18,... | collective-permute-start | bytes 245768 | tf_op jit(solution)/shard_map/ppermute | solution.py:424
  12.6 6.2 %collective-permute-start.3 = (f32[64,128]{1,0:T(8,128)S(1)}, f32[64,128]{1,0:T(8,128)S(1)}, u32[]{:S(2)}, u32[]{:S(2)}) collective-permute-start(f32[64,128]{1,0:T(8,128)S(1)} %bitcast.24), channel_id=1, source_target_pairs={{0,2},{2,4},{4,6},{6,8},{8,10},{10,12},{12,14},{14,16},{16,18},{18... | collective-permute-start | bytes 98312 | tf_op jit(solution)/shard_map/ppermute | solution.py:439
  12.6 6.2 %collective-permute-start.4 = (f32[64,128]{1,0:T(8,128)S(1)}, f32[64,128]{1,0:T(8,128)S(1)}, u32[]{:S(2)}, u32[]{:S(2)}) collective-permute-start(f32[64,128]{1,0:T(8,128)S(1)} %bitcast.25), channel_id=1, source_target_pairs={{2,0},{4,2},{6,4},{8,6},{10,8},{12,10},{14,12},{16,14},{18,16},{20... | collective-permute-start | bytes 98312 | tf_op jit(solution)/shard_map/ppermute | solution.py:440
  20.9 5.7 %collective-permute-start.5 = (f32[20,8,128]{2,1,0:T(8,128)S(1)}, f32[20,8,128]{2,1,0:T(8,128)S(1)}, u32[]{:S(2)}, u32[]{:S(2)}) collective-permute-start(f32[20,8,128]{2,1,0:T(8,128)S(1)} %get-tuple-element.80.refs_0_), channel_id=1, source_target_pairs={{0,16},{2,18},{4,20},{6,22},{8,24},{10,26},{12,28},{14,30},{16,0},... | collective-permute-start | bytes 245768 | tf_op jit(solution)/shard_map/ppermute | solution.py:424
  26.8 5.1 %copy-start.3 = (f32[10,3,2,1024]{3,2,1,0:T(2,128)S(1)}, f32[10,3,2,1024]{3,2,1,0:T(2,128)}, u32[]{:S(2)}) copy-start(f32[10,3,2,1024]{3,2,1,0:T(2,128)} %param.5) | copy-start | bytes 737284
  26.8 1.5 %collective-permute-start.6 = (f32[2,20,8,128]{3,2,1,0:T(8,128)S(1)}, f32[2,20,8,128]{3,2,1,0:T(8,128)S(1)}, u32[]{:S(2)}, u32[]{:S(2)}) collective-permute-start(f32[2,20,8,128]{3,2,1,0:T(8,128)S(1)} %get-tuple-element.83), channel_id=1, source_target_pairs={{0,2},{2,0},{4,6},{6,4},{8,10},{10,8},{12,14},{14,12},{16,18},{18,... | collective-permute-start | bytes 491528 | tf_op jit(solution)/shard_map/ppermute | solution.py:424
  30.4 6.3 %collective-permute-start.7 = (f32[320,128]{1,0:T(8,128)S(1)}, f32[320,128]{1,0:T(8,128)S(1)}, u32[]{:S(2)}, u32[]{:S(2)}) collective-permute-start(f32[320,128]{1,0:T(8,128)S(1)} %get-tuple-element.88), channel_id=1, source_target_pairs={{0,1},{1,0},{2,3},{3,2},{4,5},{5,4},{6,7},{7,6},{8,9},{9,8},{10,11... | collective-permute-start | bytes 491528 | tf_op jit(solution)/shard_map/ppermute | solution.py:427
  32.3 4.9 %collective-permute-start.14 = (f32[10,8,128]{2,1,0:T(8,128)S(1)}, f32[10,8,128]{2,1,0:T(8,128)S(1)}, u32[]{:S(2)}, u32[]{:S(2)}) collective-permute-start(f32[10,8,128]{2,1,0:T(8,128)S(1)} %get-tuple-element.103), channel_id=1, source_target_pairs={{0,2},{2,0},{4,6},{6,4},{8,10},{10,8},{12,14},{14,12},{16,18},{18,... | collective-permute-start | bytes 122888 | tf_op jit(solution)/shard_map/ppermute | solution.py:424
  37.2 4.4 %collective-permute-start.8 = (f32[20,8,128]{2,1,0:T(8,128)S(1)}, f32[20,8,128]{2,1,0:T(8,128)S(1)}, u32[]{:S(2)}, u32[]{:S(2)}) collective-permute-start(f32[20,8,128]{2,1,0:T(8,128)S(1)} %get-tuple-element.91), channel_id=1, source_target_pairs={{0,2},{2,0},{4,6},{6,4},{8,10},{10,8},{12,14},{14,12},{16,18},{18,... | collective-permute-start | bytes 245768 | tf_op jit(solution)/shard_map/ppermute | solution.py:424
  37.4 4.1 %collective-permute-start.15 = (f32[10,8,128]{2,1,0:T(8,128)S(1)}, f32[10,8,128]{2,1,0:T(8,128)S(1)}, u32[]{:S(2)}, u32[]{:S(2)}) collective-permute-start(f32[10,8,128]{2,1,0:T(8,128)S(1)} %shard_map.84.refs_0_), channel_id=1, source_target_pairs={{0,4},{2,6},{4,0},{6,2},{8,12},{10,14},{12,8},{14,10},{16,20},{18,... | collective-permute-start | bytes 122888 | tf_op jit(solution)/shard_map/ppermute | solution.py:424
  41.5 4.1 %collective-permute-start.16 = (f32[10,8,128]{2,1,0:T(8,128)S(1)}, f32[10,8,128]{2,1,0:T(8,128)S(1)}, u32[]{:S(2)}, u32[]{:S(2)}) collective-permute-start(f32[10,8,128]{2,1,0:T(8,128)S(1)} %get-tuple-element.104.refs_0_), channel_id=1, source_target_pairs={{0,8},{2,10},{4,12},{6,14},{8,0},{10,2},{12,4},{14,6},{16,24},{18,... | collective-permute-start | bytes 122888 | tf_op jit(solution)/shard_map/ppermute | solution.py:424
  41.7 9.2 %collective-permute-start.9 = (f32[20,8,128]{2,1,0:T(8,128)S(1)}, f32[20,8,128]{2,1,0:T(8,128)S(1)}, u32[]{:S(2)}, u32[]{:S(2)}) collective-permute-start(f32[20,8,128]{2,1,0:T(8,128)S(1)} %shard_map.77.refs_0_), channel_id=1, source_target_pairs={{0,4},{2,6},{4,0},{6,2},{8,12},{10,14},{12,8},{14,10},{16,20},{18,... | collective-permute-start | bytes 245768 | tf_op jit(solution)/shard_map/ppermute | solution.py:424
  45.6 5.1 %collective-permute-start.17 = (f32[10,8,128]{2,1,0:T(8,128)S(1)}, f32[10,8,128]{2,1,0:T(8,128)S(1)}, u32[]{:S(2)}, u32[]{:S(2)}) collective-permute-start(f32[10,8,128]{2,1,0:T(8,128)S(1)} %get-tuple-element.106.refs_0_), channel_id=1, source_target_pairs={{0,16},{2,18},{4,20},{6,22},{8,24},{10,26},{12,28},{14,30},{16,0},... | collective-permute-start | bytes 122888 | tf_op jit(solution)/shard_map/ppermute | solution.py:424
  50.8 1.3 %collective-permute-start.18 = (f32[2,10,8,128]{3,2,1,0:T(8,128)S(1)}, f32[2,10,8,128]{3,2,1,0:T(8,128)S(1)}, u32[]{:S(2)}, u32[]{:S(2)}) collective-permute-start(f32[2,10,8,128]{3,2,1,0:T(8,128)S(1)} %get-tuple-element.109), channel_id=1, source_target_pairs={{0,2},{2,0},{4,6},{6,4},{8,10},{10,8},{12,14},{14,12},{16,18},{18,... | collective-permute-start | bytes 245768 | tf_op jit(solution)/shard_map/ppermute | solution.py:424
  50.9 4.9 %collective-permute-start.10 = (f32[20,8,128]{2,1,0:T(8,128)S(1)}, f32[20,8,128]{2,1,0:T(8,128)S(1)}, u32[]{:S(2)}, u32[]{:S(2)}) collective-permute-start(f32[20,8,128]{2,1,0:T(8,128)S(1)} %get-tuple-element.92.refs_0_), channel_id=1, source_target_pairs={{0,8},{2,10},{4,12},{6,14},{8,0},{10,2},{12,4},{14,6},{16,24},{18,... | collective-permute-start | bytes 245768 | tf_op jit(solution)/shard_map/ppermute | solution.py:424
  53.7 4.6 %collective-permute-start.19 = (f32[160,128]{1,0:T(8,128)S(1)}, f32[160,128]{1,0:T(8,128)S(1)}, u32[]{:S(2)}, u32[]{:S(2)}) collective-permute-start(f32[160,128]{1,0:T(8,128)S(1)} %get-tuple-element.113), channel_id=1, source_target_pairs={{0,1},{1,0},{2,3},{3,2},{4,5},{5,4},{6,7},{7,6},{8,9},{9,8},{10,11... | collective-permute-start | bytes 245768 | tf_op jit(solution)/shard_map/ppermute | solution.py:427
  55.8 6.8 %collective-permute-start.11 = (f32[20,8,128]{2,1,0:T(8,128)S(1)}, f32[20,8,128]{2,1,0:T(8,128)S(1)}, u32[]{:S(2)}, u32[]{:S(2)}) collective-permute-start(f32[20,8,128]{2,1,0:T(8,128)S(1)} %get-tuple-element.94.refs_0_), channel_id=1, source_target_pairs={{0,16},{2,18},{4,20},{6,22},{8,24},{10,26},{12,28},{14,30},{16,0},... | collective-permute-start | bytes 245768 | tf_op jit(solution)/shard_map/ppermute | solution.py:424
  58.7 4.2 %collective-permute-start.20 = (f32[10,8,128]{2,1,0:T(8,128)S(1)}, f32[10,8,128]{2,1,0:T(8,128)S(1)}, u32[]{:S(2)}, u32[]{:S(2)}) collective-permute-start(f32[10,8,128]{2,1,0:T(8,128)S(1)} %get-tuple-element.116), channel_id=1, source_target_pairs={{0,2},{2,0},{4,6},{6,4},{8,10},{10,8},{12,14},{14,12},{16,18},{18,... | collective-permute-start | bytes 122888 | tf_op jit(solution)/shard_map/ppermute | solution.py:424
  62.8 13.6 %collective-permute-start.12 = (f32[2,20,8,128]{3,2,1,0:T(8,128)S(1)}, f32[2,20,8,128]{3,2,1,0:T(8,128)S(1)}, u32[]{:S(2)}, u32[]{:S(2)}) collective-permute-start(f32[2,20,8,128]{3,2,1,0:T(8,128)S(1)} %get-tuple-element.97), channel_id=1, source_target_pairs={{0,2},{2,0},{4,6},{6,4},{8,10},{10,8},{12,14},{14,12},{16,18},{18,... | collective-permute-start | bytes 491528 | tf_op jit(solution)/shard_map/ppermute | solution.py:424
  63.0 4.1 %collective-permute-start.21 = (f32[10,8,128]{2,1,0:T(8,128)S(1)}, f32[10,8,128]{2,1,0:T(8,128)S(1)}, u32[]{:S(2)}, u32[]{:S(2)}) collective-permute-start(f32[10,8,128]{2,1,0:T(8,128)S(1)} %shard_map.91.refs_0_), channel_id=1, source_target_pairs={{0,4},{2,6},{4,0},{6,2},{8,12},{10,14},{12,8},{14,10},{16,20},{18,... | collective-permute-start | bytes 122888 | tf_op jit(solution)/shard_map/ppermute | solution.py:424
  67.1 4.1 %collective-permute-start.22 = (f32[10,8,128]{2,1,0:T(8,128)S(1)}, f32[10,8,128]{2,1,0:T(8,128)S(1)}, u32[]{:S(2)}, u32[]{:S(2)}) collective-permute-start(f32[10,8,128]{2,1,0:T(8,128)S(1)} %get-tuple-element.117.refs_0_), channel_id=1, source_target_pairs={{0,8},{2,10},{4,12},{6,14},{8,0},{10,2},{12,4},{14,6},{16,24},{18,... | collective-permute-start | bytes 122888 | tf_op jit(solution)/shard_map/ppermute | solution.py:424
  71.1 5.0 %collective-permute-start.23 = (f32[10,8,128]{2,1,0:T(8,128)S(1)}, f32[10,8,128]{2,1,0:T(8,128)S(1)}, u32[]{:S(2)}, u32[]{:S(2)}) collective-permute-start(f32[10,8,128]{2,1,0:T(8,128)S(1)} %get-tuple-element.119.refs_0_), channel_id=1, source_target_pairs={{0,16},{2,18},{4,20},{6,22},{8,24},{10,26},{12,28},{14,30},{16,0},... | collective-permute-start | bytes 122888 | tf_op jit(solution)/shard_map/ppermute | solution.py:424
  76.3 3.7 %collective-permute-start.24 = (f32[2,10,8,128]{3,2,1,0:T(8,128)S(1)}, f32[2,10,8,128]{3,2,1,0:T(8,128)S(1)}, u32[]{:S(2)}, u32[]{:S(2)}) collective-permute-start(f32[2,10,8,128]{3,2,1,0:T(8,128)S(1)} %get-tuple-element.122), channel_id=1, source_target_pairs={{0,2},{2,0},{4,6},{6,4},{8,10},{10,8},{12,14},{14,12},{16,18},{18,... | collective-permute-start | bytes 245768 | tf_op jit(solution)/shard_map/ppermute | solution.py:424
  78.4 8.5 %collective-permute-start.13 = (f32[320,128]{1,0:T(8,128)S(1)}, f32[320,128]{1,0:T(8,128)S(1)}, u32[]{:S(2)}, u32[]{:S(2)}) collective-permute-start(f32[320,128]{1,0:T(8,128)S(1)} %get-tuple-element.100), channel_id=1, source_target_pairs={{0,1},{1,0},{2,3},{3,2},{4,5},{5,4},{6,7},{7,6},{8,9},{9,8},{10,11... | collective-permute-start | bytes 491528 | tf_op jit(solution)/shard_map/ppermute | solution.py:427
  81.5 5.3 %collective-permute-start.25 = (f32[160,128]{1,0:T(8,128)S(1)}, f32[160,128]{1,0:T(8,128)S(1)}, u32[]{:S(2)}, u32[]{:S(2)}) collective-permute-start(f32[160,128]{1,0:T(8,128)S(1)} %get-tuple-element.125), channel_id=1, source_target_pairs={{0,1},{1,0},{2,3},{3,2},{4,5},{5,4},{6,7},{7,6},{8,9},{9,8},{10,11... | collective-permute-start | bytes 245768 | tf_op jit(solution)/shard_map/ppermute | solution.py:427
  (1 other events, 0.9 us)

commit v6 on v5

--- a/solution.py
+++ b/solution.py
@@ -21,7 +21,7 @@
 
 SHIFT = 2.0 / 3.0
 
-CHAINS = ((0,), (1, 2))
+CHAINS = ((1, 2), (0,))
 
 
 def weight(comp, direction):
@@ -395,18 +395,25 @@
     return jax.ShapeDtypeStruct(shape, dtype)
 
 
-def call(kernel, out_shape, *args, scalars=0, scalar_outs=0, scratch_shapes=()):
-    vmem, smem = pl.BlockSpec(memory_space=pltpu.VMEM), pl.BlockSpec(memory_space=pltpu.SMEM)
-    size = 4 * sum(math.prod(a.shape) for a in list(args) + list(out_shape))
-    return pl.pallas_call(
-        kernel,
-        out_shape=out_shape,
-        in_specs=[smem] * scalars + [vmem] * (len(args) - scalars),
-        out_specs=[vmem] * (len(out_shape) - scalar_outs) + [smem] * scalar_outs,
-        scratch_shapes=scratch_shapes,
-        compiler_params=pltpu.CompilerParams(vmem_limit_bytes=32 * 1024 * 1024),
-        cost_estimate=pl.CostEstimate(flops=4 * size, bytes_accessed=size, transcendentals=0),
-    )(*args)
+class Sequence:
+    def __init__(self):
+        self.last = ()
+
+    def __call__(self, kernel, out_shape, *args, scalars=0, scalar_outs=0, scratch_shapes=(), after=()):
+        vmem, smem = pl.BlockSpec(memory_space=pltpu.VMEM), pl.BlockSpec(memory_space=pltpu.SMEM)
+        size = 4 * sum(math.prod(a.shape) for a in list(args) + list(out_shape))
+        count, unread = len(args), self.last + tuple(after)
+        done = pl.pallas_call(
+            lambda *refs: kernel(*refs[:count], *refs[count + len(unread) :]),
+            out_shape=out_shape,
+            in_specs=[smem] * scalars + [vmem] * (count - scalars) + [pl.BlockSpec(memory_space=pl.ANY)] * len(unread),
+            out_specs=[vmem] * (len(out_shape) - scalar_outs) + [smem] * scalar_outs,
+            scratch_shapes=scratch_shapes,
+            compiler_params=pltpu.CompilerParams(vmem_limit_bytes=32 * 1024 * 1024),
+            cost_estimate=pl.CostEstimate(flops=4 * size, bytes_accessed=size, transcendentals=0),
+        )(*args, *unread)
+        self.last = (done[0],)
+        return done
 
 
 def on_device(right_side, stiffness, pairing, coupling):
@@ -426,6 +433,7 @@
     def other_block(values):
         return lax.ppermute(values, "mode", [(0, 1), (1, 0)])
 
+    call = Sequence()
     table = jnp.asarray(all_tables(n_circ))
     row_start = (lax.axis_index("mode") * modes).astype(jnp.int32).reshape(1)
     me = lax.axis_index("circ").astype(jnp.int32).reshape(1)
@@ -438,15 +446,16 @@
     stiff = raw(stiffness, KM)
     stiff_l = lax.ppermute(stiff, "circ", [(i, (i + 1) % circ) for i in range(circ)])
     stiff_r = lax.ppermute(stiff, "circ", [((i + 1) % circ, i) for i in range(circ)])
-    *faces, index, coef = call(
-        functools.partial(prepare_kernel, modes),
-        [struct(KM, 6, NL, LANES)] * COMPS + [struct(WAYS, total_modes, dtype=jnp.int32), struct(WAYS, total_modes)],
-        row_start, pairing, coupling, stiff, stiff_l, stiff_r,
-        scalars=3, scalar_outs=2,
-        scratch_shapes=[pltpu.SMEM((KM - 1, total_modes), jnp.int32)],
-    )
-
-    def round_trip(keep, send, hold=None):
+    def prepare():
+        return call(
+            functools.partial(prepare_kernel, modes),
+            [struct(KM, 6, NL, LANES)] * COMPS + [struct(WAYS, total_modes, dtype=jnp.int32), struct(WAYS, total_modes)],
+            row_start, pairing, coupling, stiff, stiff_l, stiff_r,
+            scalars=3, scalar_outs=2,
+            scratch_shapes=[pltpu.SMEM((KM - 1, total_modes), jnp.int32)],
+        )
+
+    def round_trip(keep, send, between=lambda: None):
         recv = [partner(send[c], 1) for c in each]
         ends = [
             call(
@@ -458,8 +467,8 @@
         for stage in range(stages):
             last = stage == stages - 1
             other = [partner(ends[c], 2 << stage) for c in each]
-            if hold is not None and stage == 1:
-                other[-1], hold = lax.optimization_barrier((other[-1], hold))
+            if stage == 0:
+                extra = between()
             done = [
                 call(
                     functools.partial(stage_kernel, modes, CHAINS[c], n_circ, stage, last),
@@ -480,7 +489,7 @@
             )
             for c in each
         ]
-        return [(done[c][0], partner(done[c][1], 1)) for c in each], hold
+        return [(done[c][0], partner(done[c][1], 1)) for c in each], extra
 
     def operate(spec, index, coef, faces):
         done = [
@@ -507,11 +516,12 @@
             [half[c], half[c], column[c]],
             me, source, table,
             scalars=1, scratch_shapes=[pltpu.VMEM((sizes[c] * NL, LANES), F32)],
+            after=(stiff_l, stiff_r) if c == 1 else (),
         )
         for c in each
     ])
-    spec, hold = round_trip(keep, send, (index, coef, faces))
-    u, own, recv = operate(spec, *hold)
+    spec, (*faces, index, coef) = round_trip(keep, send, prepare)
+    u, own, recv = operate(spec, index, coef, faces)
     keep, send, v = zip(*[
         call(
             functools.partial(next_kernel, sizes[c], n_circ),
@@ -522,7 +532,7 @@
         for c in each
     ])
     spec, _ = round_trip(keep, send)
-    z, own, recv = operate(spec, *hold)
+    z, own, recv = operate(spec, index, coef, faces)
     devices = circ * lax.axis_size("mode")
     q, before = [], ()
     for c in each:

time: 101 us -> 91 us (0.901)
  waiting for transfers between devices: 48.9 us -> 42.8 us
  blocking collectives: 12.6 us -> 10.3 us
  starting transfers between devices: 22.2 us -> 20.8 us
    ppermute x20, waiting for transfers between devices: 37.3 us -> 29.1 us  [partner(): return lax.ppermute(values, 'circ', [(i, i ^ d) for i in range(circ)])]
    ppermute x1, waiting for transfers between devices: 1.75 us -> 4.44 us  [on_device(): lax.ppermute(stiff, 'circ', [(i, (i + 1) % circ) for i in range(circ)])]
    ppermute x4, waiting for transfers between devices: 9.9 us -> 7.58 us  [other_block(): return lax.ppermute(values, 'mode', [(0, 1), (1, 0)])]
    all_to_all x1, blocking collectives: 12.6 us -> 10.3 us  [on_device(): parts = lax.all_to_all(part, ('circ', 'mode'), split_axis=0, concat_axis=0)]
    ppermute x20, starting transfers between devices: 12.5 us -> 10.9 us  [partner(): return lax.ppermute(values, 'circ', [(i, i ^ d) for i in range(circ)])]
    ppermute x1, waiting for transfers between devices: 0.01 us -> 1.59 us  [on_device(): lax.ppermute(stiff, 'circ', [((i + 1) % circ, i) for i in range(circ)])]
    ppermute x1, starting transfers between devices: 4.44 us -> 5.67 us  [on_device(): lax.ppermute(stiff, 'circ', [((i + 1) % circ, i) for i in range(circ)])]
    unnamed x14 -> x12, local copies, waits for them, and re-layouts: 2.22 us -> 2.22 us
  transfers between devices with their start and end apart: 26 -> 26, of which waited for: 17 -> 21; matrix products, arithmetic and copies ran while one was open for 0% -> 0% of each run, Pallas kernels for 9% -> 10%
where the time goes in v6:
time: 91 us; the launch traced here: 90.8 us
  waiting for transfers between devices  42.8 us (47%)
  starting transfers between devices  20.8 us (23%)
  Pallas kernels  13.7 us (15%)
  blocking collectives  10.3 us (11%)
  local copies, waits for them, and re-layouts  2.22 us (2%)
  between operations  0.94 us (1%)
    ppermute x20, waiting for transfers between devices, partner(): return lax.ppermute(values, 'circ', [(i, i ^ d) for i in range(circ)])  29.1 us
    pallas_call x32, Pallas kernels, __call__(): pl.pallas_call(lambda *refs: kernel(*refs[:count], *refs[count + len(unre...  13.7 us
    ppermute x20, starting transfers between devices, partner(): return lax.ppermute(values, 'circ', [(i, i ^ d) for i in range(circ)])  10.9 us
    all_to_all x1, blocking collectives, on_device(): parts = lax.all_to_all(part, ('circ', 'mode'), split_axis=0, concat_axis=0)  10.3 us
    ppermute x4, waiting for transfers between devices, other_block(): return lax.ppermute(values, 'mode', [(0, 1), (1, 0)])  7.58 us
    ppermute x1, starting transfers between devices, on_device(): lax.ppermute(stiff, 'circ', [((i + 1) % circ, i) for i in range(circ)])  5.67 us
    ppermute x1, waiting for transfers between devices, on_device(): lax.ppermute(stiff, 'circ', [(i, (i + 1) % circ) for i in range(circ)])  4.44 us
    ppermute x4, starting transfers between devices, other_block(): return lax.ppermute(values, 'mode', [(0, 1), (1, 0)])  4.31 us
  transfers between devices with their start and end apart: 26, of which 21 were waited for; matrix products, arithmetic and copies ran while one was open for 0% of the time, Pallas kernels for 10%

profile of v6, /device:TPU:0, one launch (start us, length us, event | category | flops | bytes accessed | tf_op | source)
XLA Modules:
  0.0 90.8 jit_solution(1165878282646602056)
XLA Ops:
  0.6 1.2 %copy-done = f32[2240,128]{1,0:T(8,128)S(1)} copy-done((f32[2240,128]{1,0:T(8,128)S(1)}, f32[2240,128]{1,0:T(8,128)}, u32[]{:S(2)}) %copy-start) | copy-done | bytes 1146904
  4.0 5.7 %collective-permute-start.1 = (f32[64,128]{1,0:T(8,128)S(1)}, f32[64,128]{1,0:T(8,128)S(1)}, u32[]{:S(2)}, u32[]{:S(2)}) collective-permute-start(f32[64,128]{1,0:T(8,128)S(1)} %bitcast.24), channel_id=1, source_target_pairs={{2,0},{4,2},{6,4},{8,6},{10,8},{12,10},{14,12},{16,14},{18,16},{20... | collective-permute-start | bytes 98312 | tf_op jit(solution)/shard_map/ppermute | solution.py:448
  9.6 1.6 %collective-permute-done.1.refs_5_ = f32[64,128]{1,0:T(8,128)S(1)} collective-permute-done((f32[64,128]{1,0:T(8,128)S(1)}, f32[64,128]{1,0:T(8,128)S(1)}, u32[]{:S(2)}, u32[]{:S(2)}) %collective-permute-start.1) | collective-permute-done | bytes 32800 | tf_op jit(solution)/shard_map/ppermute | solution.py:448
  11.2 4.4 %collective-permute-done.refs_4_ = f32[64,128]{1,0:T(8,128)S(1)} collective-permute-done((f32[64,128]{1,0:T(8,128)S(1)}, f32[64,128]{1,0:T(8,128)S(1)}, u32[]{:S(2)}, u32[]{:S(2)}) %collective-permute-start) | collective-permute-done | bytes 32800 | tf_op jit(solution)/shard_map/ppermute | solution.py:447
  16.4 1.2 %collective-permute-done.2.refs_2_ = f32[10,8,128]{2,1,0:T(8,128)S(1)} collective-permute-done((f32[10,8,128]{2,1,0:T(8,128)S(1)}, f32[10,8,128]{2,1,0:T(8,128)S(1)}, u32[]{:S(2)}, u32[]{:S(2)}) %collective-permute-start.2) | collective-permute-done | bytes 40992 | tf_op jit(solution)/shard_map/ppermute | solution.py:431
  17.8 2.0 %shard_map.72 = (f32[4,6,16,128]{3,2,1,0:T(8,128)S(1)}, f32[4,6,16,128]{3,2,1,0:T(8,128)S(1)}, f32[4,6,16,128]{3,2,1,0:T(8,128)S(1)}, s32[6,20]{1,0:T(8,128)S(1)}, f32[6,20]{1,0:T(8,128)S(1)}) custom-call(s32[1]{0:T(128)} %bitcast.11.refs_0_.refs_1_, s32[3,20]{1,0:T(4,128)S(1)} %copy-done.4, f32[3,20]{1,0:T(4,128)S(1)} %copy-done.5, f32[64,128]{1,0:T(8,128)S(1)} %bitcast.26, ...), custom_call_target="tpu_custom_call" | custom-call | flops 2758288 | bytes 689572 | tf_op jit(solution)/shard_map/pallas_call | solution.py:406
  19.8 1.0 %collective-permute-done.5.refs_2_ = f32[20,8,128]{2,1,0:T(8,128)S(1)} collective-permute-done((f32[20,8,128]{2,1,0:T(8,128)S(1)}, f32[20,8,128]{2,1,0:T(8,128)S(1)}, u32[]{:S(2)}, u32[]{:S(2)}) %collective-permute-start.5) | collective-permute-done | bytes 81952 | tf_op jit(solution)/shard_map/ppermute | solution.py:431
  20.9 1.0 %collective-permute-start.4 = (f32[10,8,128]{2,1,0:T(8,128)S(1)}, f32[10,8,128]{2,1,0:T(8,128)S(1)}, u32[]{:S(2)}, u32[]{:S(2)}) collective-permute-start(f32[10,8,128]{2,1,0:T(8,128)S(1)} %shard_map.71.refs_6_.refs_1_), channel_id=1, source_target_pairs={{0,4},{2,6},{4,0},{6,2},{8,12},{10,14},{12,8},{14,10},{16,20},{18,... | collective-permute-start | bytes 122888 | tf_op jit(solution)/shard_map/ppermute | solution.py:431
  21.9 3.0 %collective-permute-done.4.refs_2_ = f32[10,8,128]{2,1,0:T(8,128)S(1)} collective-permute-done((f32[10,8,128]{2,1,0:T(8,128)S(1)}, f32[10,8,128]{2,1,0:T(8,128)S(1)}, u32[]{:S(2)}, u32[]{:S(2)}) %collective-permute-start.4) | collective-permute-done | bytes 40992 | tf_op jit(solution)/shard_map/ppermute | solution.py:431
  25.0 2.0 %collective-permute-start.6 = (f32[10,8,128]{2,1,0:T(8,128)S(1)}, f32[10,8,128]{2,1,0:T(8,128)S(1)}, u32[]{:S(2)}, u32[]{:S(2)}) collective-permute-start(f32[10,8,128]{2,1,0:T(8,128)S(1)} %get-tuple-element.70.refs_1_), channel_id=1, source_target_pairs={{0,8},{2,10},{4,12},{6,14},{8,0},{10,2},{12,4},{14,6},{16,24},{18,... | collective-permute-start | bytes 122888 | tf_op jit(solution)/shard_map/ppermute | solution.py:431
  27.1 2.0 %collective-permute-done.6.refs_2_ = f32[10,8,128]{2,1,0:T(8,128)S(1)} collective-permute-done((f32[10,8,128]{2,1,0:T(8,128)S(1)}, f32[10,8,128]{2,1,0:T(8,128)S(1)}, u32[]{:S(2)}, u32[]{:S(2)}) %collective-permute-start.6) | collective-permute-done | bytes 40992 | tf_op jit(solution)/shard_map/ppermute | solution.py:431
  29.1 1.0 %collective-permute-start.8 = (f32[10,8,128]{2,1,0:T(8,128)S(1)}, f32[10,8,128]{2,1,0:T(8,128)S(1)}, u32[]{:S(2)}, u32[]{:S(2)}) collective-permute-start(f32[10,8,128]{2,1,0:T(8,128)S(1)} %get-tuple-element.74.refs_1_), channel_id=1, source_target_pairs={{0,16},{2,18},{4,20},{6,22},{8,24},{10,26},{12,28},{14,30},{16,0},... | collective-permute-start | bytes 122888 | tf_op jit(solution)/shard_map/ppermute | solution.py:431
  30.1 3.2 %collective-permute-done.9.refs_2_ = f32[20,8,128]{2,1,0:T(8,128)S(1)} collective-permute-done((f32[20,8,128]{2,1,0:T(8,128)S(1)}, f32[20,8,128]{2,1,0:T(8,128)S(1)}, u32[]{:S(2)}, u32[]{:S(2)}) %collective-permute-start.9) | collective-permute-done | bytes 81952 | tf_op jit(solution)/shard_map/ppermute | solution.py:431
  34.5 1.3 %collective-permute-done.11.refs_5_ = f32[2,20,8,128]{3,2,1,0:T(8,128)S(1)} collective-permute-done((f32[2,20,8,128]{3,2,1,0:T(8,128)S(1)}, f32[2,20,8,128]{3,2,1,0:T(8,128)S(1)}, u32[]{:S(2)}, u32[]{:S(2)}) %collective-permute-start.11) | collective-permute-done | bytes 163872 | tf_op jit(solution)/shard_map/ppermute | solution.py:431
  35.7 2.1 %shard_map.81 = (f32[320,128]{1,0:T(8,128)S(1)}, f32[320,128]{1,0:T(8,128)S(1)}, f32[320,128]{1,0:T(8,128)S(1)}) custom-call(s32[1]{0:T(128)} %bitcast.refs_0_, s32[1]{0:T(128)} %bitcast.11.refs_0_.refs_1_, s32[6,20]{1,0:T(8,128)S(1)} %get-tuple-element.66.refs_2_, f32[6,20]{1,0:T(8,128)S(1)} %get-tuple-element.67.refs_3_, ...), custom_call_target="tpu_custom_call" | custom-call | flops 9441056 | bytes 2360264 | tf_op jit(solution)/shard_map/pallas_call | solution.py:406
  37.8 1.6 %collective-permute-start.13 = (f32[320,128]{1,0:T(8,128)S(1)}, f32[320,128]{1,0:T(8,128)S(1)}, u32[]{:S(2)}, u32[]{:S(2)}) collective-permute-start(f32[320,128]{1,0:T(8,128)S(1)} %get-tuple-element.89), channel_id=1, source_target_pairs={{0,1},{1,0},{2,3},{3,2},{4,5},{5,4},{6,7},{7,6},{8,9},{9,8},{10,11... | collective-permute-start | bytes 491528 | tf_op jit(solution)/shard_map/ppermute | solution.py:434
  39.4 1.3 %collective-permute-done.10.refs_5_ = f32[2,10,8,128]{3,2,1,0:T(8,128)S(1)} collective-permute-done((f32[2,10,8,128]{3,2,1,0:T(8,128)S(1)}, f32[2,10,8,128]{3,2,1,0:T(8,128)S(1)}, u32[]{:S(2)}, u32[]{:S(2)}) %collective-permute-start.10) | collective-permute-done | bytes 81952 | tf_op jit(solution)/shard_map/ppermute | solution.py:431
  40.7 1.6 %shard_map.82 = (f32[160,128]{1,0:T(8,128)S(1)}, f32[160,128]{1,0:T(8,128)S(1)}, f32[160,128]{1,0:T(8,128)S(1)}) custom-call(s32[1]{0:T(128)} %bitcast.refs_0_, s32[1]{0:T(128)} %bitcast.11.refs_0_.refs_1_, s32[6,20]{1,0:T(8,128)S(1)} %get-tuple-element.66.refs_2_, f32[6,20]{1,0:T(8,128)S(1)} %get-tuple-element.67.refs_3_, ...), custom_call_target="tpu_custom_call" | custom-call | flops 7016224 | bytes 1754056 | tf_op jit(solution)/shard_map/pallas_call | solution.py:406
  42.9 1.3 %collective-permute-done.13.refs_3_ = f32[320,128]{1,0:T(8,128)S(1)} collective-permute-done((f32[320,128]{1,0:T(8,128)S(1)}, f32[320,128]{1,0:T(8,128)S(1)}, u32[]{:S(2)}, u32[]{:S(2)}) %collective-permute-start.13) | collective-permute-done | bytes 163872 | tf_op jit(solution)/shard_map/ppermute | solution.py:434
  44.7 2.1 %collective-permute-done.12.refs_3_ = f32[160,128]{1,0:T(8,128)S(1)} collective-permute-done((f32[160,128]{1,0:T(8,128)S(1)}, f32[160,128]{1,0:T(8,128)S(1)}, u32[]{:S(2)}, u32[]{:S(2)}) %collective-permute-start.12) | collective-permute-done | bytes 81952 | tf_op jit(solution)/shard_map/ppermute | solution.py:434
  48.3 1.2 %collective-permute-done.14.refs_2_ = f32[10,8,128]{2,1,0:T(8,128)S(1)} collective-permute-done((f32[10,8,128]{2,1,0:T(8,128)S(1)}, f32[10,8,128]{2,1,0:T(8,128)S(1)}, u32[]{:S(2)}, u32[]{:S(2)}) %collective-permute-start.14) | collective-permute-done | bytes 40992 | tf_op jit(solution)/shard_map/ppermute | solution.py:431
  49.6 2.2 %collective-permute-done.17.refs_2_ = f32[20,8,128]{2,1,0:T(8,128)S(1)} collective-permute-done((f32[20,8,128]{2,1,0:T(8,128)S(1)}, f32[20,8,128]{2,1,0:T(8,128)S(1)}, u32[]{:S(2)}, u32[]{:S(2)}) %collective-permute-start.17) | collective-permute-done | bytes 81952 | tf_op jit(solution)/shard_map/ppermute | solution.py:431
  51.9 2.2 %collective-permute-start.19 = (f32[20,8,128]{2,1,0:T(8,128)S(1)}, f32[20,8,128]{2,1,0:T(8,128)S(1)}, u32[]{:S(2)}, u32[]{:S(2)}) collective-permute-start(f32[20,8,128]{2,1,0:T(8,128)S(1)} %get-tuple-element.98.refs_1_), channel_id=1, source_target_pairs={{0,8},{2,10},{4,12},{6,14},{8,0},{10,2},{12,4},{14,6},{16,24},{18,... | collective-permute-start | bytes 245768 | tf_op jit(solution)/shard_map/ppermute | solution.py:431
  54.8 3.3 %collective-permute-done.16.refs_2_ = f32[10,8,128]{2,1,0:T(8,128)S(1)} collective-permute-done((f32[10,8,128]{2,1,0:T(8,128)S(1)}, f32[10,8,128]{2,1,0:T(8,128)S(1)}, u32[]{:S(2)}, u32[]{:S(2)}) %collective-permute-start.16) | collective-permute-done | bytes 40992 | tf_op jit(solution)/shard_map/ppermute | solution.py:431
  59.2 3.4 %collective-permute-done.18.refs_2_ = f32[10,8,128]{2,1,0:T(8,128)S(1)} collective-permute-done((f32[10,8,128]{2,1,0:T(8,128)S(1)}, f32[10,8,128]{2,1,0:T(8,128)S(1)}, u32[]{:S(2)}, u32[]{:S(2)}) %collective-permute-start.18) | collective-permute-done | bytes 40992 | tf_op jit(solution)/shard_map/ppermute | solution.py:431
  63.7 3.8 %collective-permute-done.20.refs_2_ = f32[10,8,128]{2,1,0:T(8,128)S(1)} collective-permute-done((f32[10,8,128]{2,1,0:T(8,128)S(1)}, f32[10,8,128]{2,1,0:T(8,128)S(1)}, u32[]{:S(2)}, u32[]{:S(2)}) %collective-permute-start.20) | collective-permute-done | bytes 40992 | tf_op jit(solution)/shard_map/ppermute | solution.py:431
  69.2 2.1 %shard_map.95 = (f32[320,128]{1,0:T(8,128)S(1)}, f32[320,128]{1,0:T(8,128)S(1)}, f32[320,128]{1,0:T(8,128)S(1)}) custom-call(s32[1]{0:T(128)} %bitcast.refs_0_, s32[1]{0:T(128)} %bitcast.11.refs_0_.refs_1_, s32[6,20]{1,0:T(8,128)S(1)} %get-tuple-element.66.refs_2_, f32[6,20]{1,0:T(8,128)S(1)} %get-tuple-element.67.refs_3_, ...), custom_call_target="tpu_custom_call" | custom-call | flops 9441056 | bytes 2360264 | tf_op jit(solution)/shard_map/pallas_call | solution.py:406
  71.7 1.6 %shard_map.96 = (f32[160,128]{1,0:T(8,128)S(1)}, f32[160,128]{1,0:T(8,128)S(1)}, f32[160,128]{1,0:T(8,128)S(1)}) custom-call(s32[1]{0:T(128)} %bitcast.refs_0_, s32[1]{0:T(128)} %bitcast.11.refs_0_.refs_1_, s32[6,20]{1,0:T(8,128)S(1)} %get-tuple-element.66.refs_2_, f32[6,20]{1,0:T(8,128)S(1)} %get-tuple-element.67.refs_3_, ...), custom_call_target="tpu_custom_call" | custom-call | flops 7016224 | bytes 1754056 | tf_op jit(solution)/shard_map/pallas_call | solution.py:406
  73.4 1.7 %collective-permute-start.24 = (f32[160,128]{1,0:T(8,128)S(1)}, f32[160,128]{1,0:T(8,128)S(1)}, u32[]{:S(2)}, u32[]{:S(2)}) collective-permute-start(f32[160,128]{1,0:T(8,128)S(1)} %get-tuple-element.110), channel_id=1, source_target_pairs={{0,1},{1,0},{2,3},{3,2},{4,5},{5,4},{6,7},{7,6},{8,9},{9,8},{10,11... | collective-permute-start | bytes 245768 | tf_op jit(solution)/shard_map/ppermute | solution.py:434
  75.0 3.3 %collective-permute-done.25.refs_5_ = f32[320,128]{1,0:T(8,128)S(1)} collective-permute-done((f32[320,128]{1,0:T(8,128)S(1)}, f32[320,128]{1,0:T(8,128)S(1)}, u32[]{:S(2)}, u32[]{:S(2)}) %collective-permute-start.25) | collective-permute-done | bytes 163872 | tf_op jit(solution)/shard_map/ppermute | solution.py:434
  79.4 10.3 %all_to_all.5.refs_0_ = f32[32,8,128]{2,1,0:T(8,128)S(1)} all-to-all(f32[32,8,128]{2,1,0:T(8,128)S(1)} %get-tuple-element.116), channel_id=1, replica_groups=mesh['circ'=16,'mode'=2] {'circ','mode'}, dimensions={0} | all-to-all | bytes 262144 | tf_op jit(solution)/shard_map/all_to_all | solution.py:545
  89.7 1.1 %shard_map.99 = (f32[480,128]{1,0:T(8,128)}, f32[480,128]{1,0:T(8,128)}) custom-call(f32[32,8,128]{2,1,0:T(8,128)S(1)} %all_to_all.5.refs_0_, f32[320,128]{1,0:T(8,128)S(1)} %get-tuple-element.87.refs_1_.refs_0_, f32[320,128]{1,0:T(8,128)S(1)} %get-tuple-element.83.refs_8_.refs_1_.refs_2_, f32[320,128]{1,0:T(8,128)S(1)} %get-tuple-element.111.refs_2_.refs_3_, ...), custom_call_target="tpu_custom_call" | custom-call | flops 7405568 | bytes 1851392 | tf_op jit(solution)/shard_map/pallas_call | solution.py:406
  (65 shorter events, 13.1 us)
Async XLA Ops:
  0.6 1.3 %copy-start = (f32[2240,128]{1,0:T(8,128)S(1)}, f32[2240,128]{1,0:T(8,128)}, u32[]{:S(2)}) copy-start(f32[2240,128]{1,0:T(8,128)} %constant.12.clone.refs_2_.refs_3_.refs_4_.refs_6_) | copy-start | bytes 3440644
  1.9 0.9 %copy-start.2 = (f32[10,3,2,1024]{3,2,1,0:T(2,128)S(1)}, f32[10,3,2,1024]{3,2,1,0:T(2,128)}, u32[]{:S(2)}) copy-start(f32[10,3,2,1024]{3,2,1,0:T(2,128)} %param.5) | copy-start | bytes 737284
  2.8 1.1 %copy-start.3 = (f32[4,2,1024]{2,1,0:T(2,128)S(1)}, f32[4,2,1024]{2,1,0:T(2,128)}, u32[]{:S(2)}) copy-start(f32[4,2,1024]{2,1,0:T(2,128)} %param.6) | copy-start | bytes 98308
  2.8 13.3 %copy-start.1 = (f32[2240,128]{1,0:T(8,128)S(1)}, f32[2240,128]{1,0:T(8,128)}, u32[]{:S(2)}) copy-start(f32[2240,128]{1,0:T(8,128)} %constant.12.clone.refs_2_.refs_3_.refs_4_.refs_6_) | copy-start | bytes 3440644
  3.5 12.7 %collective-permute-start.3 = (f32[20,8,128]{2,1,0:T(8,128)S(1)}, f32[20,8,128]{2,1,0:T(8,128)S(1)}, u32[]{:S(2)}, u32[]{:S(2)}) collective-permute-start(f32[20,8,128]{2,1,0:T(8,128)S(1)} %get-tuple-element.65), channel_id=1, source_target_pairs={{0,2},{2,0},{4,6},{6,4},{8,10},{10,8},{12,14},{14,12},{16,18},{18,... | collective-permute-start | bytes 245768 | tf_op jit(solution)/shard_map/ppermute | solution.py:431
  4.0 7.3 %collective-permute-start.1 = (f32[64,128]{1,0:T(8,128)S(1)}, f32[64,128]{1,0:T(8,128)S(1)}, u32[]{:S(2)}, u32[]{:S(2)}) collective-permute-start(f32[64,128]{1,0:T(8,128)S(1)} %bitcast.24), channel_id=1, source_target_pairs={{2,0},{4,2},{6,4},{8,6},{10,8},{12,10},{14,12},{16,14},{18,16},{20... | collective-permute-start | bytes 98312 | tf_op jit(solution)/shard_map/ppermute | solution.py:448
  9.6 6.0 %collective-permute-start = (f32[64,128]{1,0:T(8,128)S(1)}, f32[64,128]{1,0:T(8,128)S(1)}, u32[]{:S(2)}, u32[]{:S(2)}) collective-permute-start(f32[64,128]{1,0:T(8,128)S(1)} %bitcast.25), channel_id=1, source_target_pairs={{0,2},{2,4},{4,6},{6,8},{8,10},{10,12},{12,14},{14,16},{16,18},{18... | collective-permute-start | bytes 98312 | tf_op jit(solution)/shard_map/ppermute | solution.py:447
  16.1 1.6 %copy-start.4 = (s32[3,20]{1,0:T(4,128)S(1)}, s32[3,20]{1,0:T(4,128)}, u32[]{:S(2)}) copy-start(s32[3,20]{1,0:T(4,128)} %refs_1_.1) | copy-start | bytes 724
  16.1 1.6 %copy-start.5 = (f32[3,20]{1,0:T(4,128)S(1)}, f32[3,20]{1,0:T(4,128)}, u32[]{:S(2)}) copy-start(f32[3,20]{1,0:T(4,128)} %refs_2_.3) | copy-start | bytes 724
  16.3 4.5 %collective-permute-start.5 = (f32[20,8,128]{2,1,0:T(8,128)S(1)}, f32[20,8,128]{2,1,0:T(8,128)S(1)}, u32[]{:S(2)}, u32[]{:S(2)}) collective-permute-start(f32[20,8,128]{2,1,0:T(8,128)S(1)} %shard_map.70.refs_4_.refs_1_), channel_id=1, source_target_pairs={{0,4},{2,6},{4,0},{6,2},{8,12},{10,14},{12,8},{14,10},{16,20},{18,... | collective-permute-start | bytes 245768 | tf_op jit(solution)/shard_map/ppermute | solution.py:431
  16.4 1.3 %collective-permute-start.2 = (f32[10,8,128]{2,1,0:T(8,128)S(1)}, f32[10,8,128]{2,1,0:T(8,128)S(1)}, u32[]{:S(2)}, u32[]{:S(2)}) collective-permute-start(f32[10,8,128]{2,1,0:T(8,128)S(1)} %get-tuple-element.64), channel_id=1, source_target_pairs={{0,2},{2,0},{4,6},{6,4},{8,10},{10,8},{12,14},{14,12},{16,18},{18,... | collective-permute-start | bytes 122888 | tf_op jit(solution)/shard_map/ppermute | solution.py:431
  20.8 6.2 %collective-permute-start.7 = (f32[20,8,128]{2,1,0:T(8,128)S(1)}, f32[20,8,128]{2,1,0:T(8,128)S(1)}, u32[]{:S(2)}, u32[]{:S(2)}) collective-permute-start(f32[20,8,128]{2,1,0:T(8,128)S(1)} %get-tuple-element.72.refs_1_), channel_id=1, source_target_pairs={{0,8},{2,10},{4,12},{6,14},{8,0},{10,2},{12,4},{14,6},{16,24},{18,... | collective-permute-start | bytes 245768 | tf_op jit(solution)/shard_map/ppermute | solution.py:431
  20.9 4.1 %collective-permute-start.4 = (f32[10,8,128]{2,1,0:T(8,128)S(1)}, f32[10,8,128]{2,1,0:T(8,128)S(1)}, u32[]{:S(2)}, u32[]{:S(2)}) collective-permute-start(f32[10,8,128]{2,1,0:T(8,128)S(1)} %shard_map.71.refs_6_.refs_1_), channel_id=1, source_target_pairs={{0,4},{2,6},{4,0},{6,2},{8,12},{10,14},{12,8},{14,10},{16,20},{18,... | collective-permute-start | bytes 122888 | tf_op jit(solution)/shard_map/ppermute | solution.py:431
  25.0 4.1 %collective-permute-start.6 = (f32[10,8,128]{2,1,0:T(8,128)S(1)}, f32[10,8,128]{2,1,0:T(8,128)S(1)}, u32[]{:S(2)}, u32[]{:S(2)}) collective-permute-start(f32[10,8,128]{2,1,0:T(8,128)S(1)} %get-tuple-element.70.refs_1_), channel_id=1, source_target_pairs={{0,8},{2,10},{4,12},{6,14},{8,0},{10,2},{12,4},{14,6},{16,24},{18,... | collective-permute-start | bytes 122888 | tf_op jit(solution)/shard_map/ppermute | solution.py:431
  27.0 6.2 %collective-permute-start.9 = (f32[20,8,128]{2,1,0:T(8,128)S(1)}, f32[20,8,128]{2,1,0:T(8,128)S(1)}, u32[]{:S(2)}, u32[]{:S(2)}) collective-permute-start(f32[20,8,128]{2,1,0:T(8,128)S(1)} %get-tuple-element.76.refs_1_), channel_id=1, source_target_pairs={{0,16},{2,18},{4,20},{6,22},{8,24},{10,26},{12,28},{14,30},{16,0},... | collective-permute-start | bytes 245768 | tf_op jit(solution)/shard_map/ppermute | solution.py:431
  29.1 5.0 %collective-permute-start.8 = (f32[10,8,128]{2,1,0:T(8,128)S(1)}, f32[10,8,128]{2,1,0:T(8,128)S(1)}, u32[]{:S(2)}, u32[]{:S(2)}) collective-permute-start(f32[10,8,128]{2,1,0:T(8,128)S(1)} %get-tuple-element.74.refs_1_), channel_id=1, source_target_pairs={{0,16},{2,18},{4,20},{6,22},{8,24},{10,26},{12,28},{14,30},{16,0},... | collective-permute-start | bytes 122888 | tf_op jit(solution)/shard_map/ppermute | solution.py:431
  34.3 1.5 %collective-permute-start.11 = (f32[2,20,8,128]{3,2,1,0:T(8,128)S(1)}, f32[2,20,8,128]{3,2,1,0:T(8,128)S(1)}, u32[]{:S(2)}, u32[]{:S(2)}) collective-permute-start(f32[2,20,8,128]{3,2,1,0:T(8,128)S(1)} %get-tuple-element.80), channel_id=1, source_target_pairs={{0,2},{2,0},{4,6},{6,4},{8,10},{10,8},{12,14},{14,12},{16,18},{18,... | collective-permute-start | bytes 491528 | tf_op jit(solution)/shard_map/ppermute | solution.py:431
  37.8 6.3 %collective-permute-start.13 = (f32[320,128]{1,0:T(8,128)S(1)}, f32[320,128]{1,0:T(8,128)S(1)}, u32[]{:S(2)}, u32[]{:S(2)}) collective-permute-start(f32[320,128]{1,0:T(8,128)S(1)} %get-tuple-element.89), channel_id=1, source_target_pairs={{0,1},{1,0},{2,3},{3,2},{4,5},{5,4},{6,7},{7,6},{8,9},{9,8},{10,11... | collective-permute-start | bytes 491528 | tf_op jit(solution)/shard_map/ppermute | solution.py:434
  39.4 1.3 %collective-permute-start.10 = (f32[2,10,8,128]{3,2,1,0:T(8,128)S(1)}, f32[2,10,8,128]{3,2,1,0:T(8,128)S(1)}, u32[]{:S(2)}, u32[]{:S(2)}) collective-permute-start(f32[2,10,8,128]{3,2,1,0:T(8,128)S(1)} %get-tuple-element.79), channel_id=1, source_target_pairs={{0,2},{2,0},{4,6},{6,4},{8,10},{10,8},{12,14},{14,12},{16,18},{18,... | collective-permute-start | bytes 245768 | tf_op jit(solution)/shard_map/ppermute | solution.py:431
  42.3 4.6 %collective-permute-start.12 = (f32[160,128]{1,0:T(8,128)S(1)}, f32[160,128]{1,0:T(8,128)S(1)}, u32[]{:S(2)}, u32[]{:S(2)}) collective-permute-start(f32[160,128]{1,0:T(8,128)S(1)} %get-tuple-element.86), channel_id=1, source_target_pairs={{0,1},{1,0},{2,3},{3,2},{4,5},{5,4},{6,7},{7,6},{8,9},{9,8},{10,11... | collective-permute-start | bytes 245768 | tf_op jit(solution)/shard_map/ppermute | solution.py:434
  44.7 2.5 %collective-permute-start.15 = (f32[20,8,128]{2,1,0:T(8,128)S(1)}, f32[20,8,128]{2,1,0:T(8,128)S(1)}, u32[]{:S(2)}, u32[]{:S(2)}) collective-permute-start(f32[20,8,128]{2,1,0:T(8,128)S(1)} %get-tuple-element.94), channel_id=1, source_target_pairs={{0,2},{2,0},{4,6},{6,4},{8,10},{10,8},{12,14},{14,12},{16,18},{18,... | collective-permute-start | bytes 245768 | tf_op jit(solution)/shard_map/ppermute | solution.py:431
  47.3 4.5 %collective-permute-start.17 = (f32[20,8,128]{2,1,0:T(8,128)S(1)}, f32[20,8,128]{2,1,0:T(8,128)S(1)}, u32[]{:S(2)}, u32[]{:S(2)}) collective-permute-start(f32[20,8,128]{2,1,0:T(8,128)S(1)} %shard_map.85.refs_4_.refs_1_), channel_id=1, source_target_pairs={{0,4},{2,6},{4,0},{6,2},{8,12},{10,14},{12,8},{14,10},{16,20},{18,... | collective-permute-start | bytes 245768 | tf_op jit(solution)/shard_map/ppermute | solution.py:431
  48.3 1.2 %collective-permute-start.14 = (f32[10,8,128]{2,1,0:T(8,128)S(1)}, f32[10,8,128]{2,1,0:T(8,128)S(1)}, u32[]{:S(2)}, u32[]{:S(2)}) collective-permute-start(f32[10,8,128]{2,1,0:T(8,128)S(1)} %get-tuple-element.93), channel_id=1, source_target_pairs={{0,2},{2,0},{4,6},{6,4},{8,10},{10,8},{12,14},{14,12},{16,18},{18,... | collective-permute-start | bytes 122888 | tf_op jit(solution)/shard_map/ppermute | solution.py:431
  51.9 6.4 %collective-permute-start.19 = (f32[20,8,128]{2,1,0:T(8,128)S(1)}, f32[20,8,128]{2,1,0:T(8,128)S(1)}, u32[]{:S(2)}, u32[]{:S(2)}) collective-permute-start(f32[20,8,128]{2,1,0:T(8,128)S(1)} %get-tuple-element.98.refs_1_), channel_id=1, source_target_pairs={{0,8},{2,10},{4,12},{6,14},{8,0},{10,2},{12,4},{14,6},{16,24},{18,... | collective-permute-start | bytes 245768 | tf_op jit(solution)/shard_map/ppermute | solution.py:431
  54.1 4.0 %collective-permute-start.16 = (f32[10,8,128]{2,1,0:T(8,128)S(1)}, f32[10,8,128]{2,1,0:T(8,128)S(1)}, u32[]{:S(2)}, u32[]{:S(2)}) collective-permute-start(f32[10,8,128]{2,1,0:T(8,128)S(1)} %shard_map.86.refs_4_.refs_1_), channel_id=1, source_target_pairs={{0,4},{2,6},{4,0},{6,2},{8,12},{10,14},{12,8},{14,10},{16,20},{18,... | collective-permute-start | bytes 122888 | tf_op jit(solution)/shard_map/ppermute | solution.py:431
  58.1 4.4 %collective-permute-start.18 = (f32[10,8,128]{2,1,0:T(8,128)S(1)}, f32[10,8,128]{2,1,0:T(8,128)S(1)}, u32[]{:S(2)}, u32[]{:S(2)}) collective-permute-start(f32[10,8,128]{2,1,0:T(8,128)S(1)} %get-tuple-element.96.refs_1_), channel_id=1, source_target_pairs={{0,8},{2,10},{4,12},{6,14},{8,0},{10,2},{12,4},{14,6},{16,24},{18,... | collective-permute-start | bytes 122888 | tf_op jit(solution)/shard_map/ppermute | solution.py:431
  58.3 5.4 %collective-permute-start.21 = (f32[20,8,128]{2,1,0:T(8,128)S(1)}, f32[20,8,128]{2,1,0:T(8,128)S(1)}, u32[]{:S(2)}, u32[]{:S(2)}) collective-permute-start(f32[20,8,128]{2,1,0:T(8,128)S(1)} %get-tuple-element.102.refs_1_), channel_id=1, source_target_pairs={{0,16},{2,18},{4,20},{6,22},{8,24},{10,26},{12,28},{14,30},{16,0},... | collective-permute-start | bytes 245768 | tf_op jit(solution)/shard_map/ppermute | solution.py:431
  62.6 5.0 %collective-permute-start.20 = (f32[10,8,128]{2,1,0:T(8,128)S(1)}, f32[10,8,128]{2,1,0:T(8,128)S(1)}, u32[]{:S(2)}, u32[]{:S(2)}) collective-permute-start(f32[10,8,128]{2,1,0:T(8,128)S(1)} %get-tuple-element.100.refs_1_), channel_id=1, source_target_pairs={{0,16},{2,18},{4,20},{6,22},{8,24},{10,26},{12,28},{14,30},{16,0},... | collective-permute-start | bytes 122888 | tf_op jit(solution)/shard_map/ppermute | solution.py:431
  67.7 1.5 %collective-permute-start.23 = (f32[2,20,8,128]{3,2,1,0:T(8,128)S(1)}, f32[2,20,8,128]{3,2,1,0:T(8,128)S(1)}, u32[]{:S(2)}, u32[]{:S(2)}) collective-permute-start(f32[2,20,8,128]{3,2,1,0:T(8,128)S(1)} %get-tuple-element.106), channel_id=1, source_target_pairs={{0,2},{2,0},{4,6},{6,4},{8,10},{10,8},{12,14},{14,12},{16,18},{18,... | collective-permute-start | bytes 491528 | tf_op jit(solution)/shard_map/ppermute | solution.py:431
  67.9 3.8 %collective-permute-start.22 = (f32[2,10,8,128]{3,2,1,0:T(8,128)S(1)}, f32[2,10,8,128]{3,2,1,0:T(8,128)S(1)}, u32[]{:S(2)}, u32[]{:S(2)}) collective-permute-start(f32[2,10,8,128]{3,2,1,0:T(8,128)S(1)} %get-tuple-element.105), channel_id=1, source_target_pairs={{0,2},{2,0},{4,6},{6,4},{8,10},{10,8},{12,14},{14,12},{16,18},{18,... | collective-permute-start | bytes 245768 | tf_op jit(solution)/shard_map/ppermute | solution.py:431
  71.3 7.1 %collective-permute-start.25 = (f32[320,128]{1,0:T(8,128)S(1)}, f32[320,128]{1,0:T(8,128)S(1)}, u32[]{:S(2)}, u32[]{:S(2)}) collective-permute-start(f32[320,128]{1,0:T(8,128)S(1)} %get-tuple-element.113), channel_id=1, source_target_pairs={{0,1},{1,0},{2,3},{3,2},{4,5},{5,4},{6,7},{7,6},{8,9},{9,8},{10,11... | collective-permute-start | bytes 491528 | tf_op jit(solution)/shard_map/ppermute | solution.py:434
  73.4 6.0 %collective-permute-start.24 = (f32[160,128]{1,0:T(8,128)S(1)}, f32[160,128]{1,0:T(8,128)S(1)}, u32[]{:S(2)}, u32[]{:S(2)}) collective-permute-start(f32[160,128]{1,0:T(8,128)S(1)} %get-tuple-element.110), channel_id=1, source_target_pairs={{0,1},{1,0},{2,3},{3,2},{4,5},{5,4},{6,7},{7,6},{8,9},{9,8},{10,11... | collective-permute-start | bytes 245768 | tf_op jit(solution)/shard_map/ppermute | solution.py:434
